TPU v7x, 32 devices: a whole 2x2x4 slice. The times are simulated.
32 devices in a mesh: section: 2 (over core), seq: 4 (over z), dp: 4 (over y, x).
Axes of the slice: x: 2, y: 2, z: 4, core: 2. Of those that a mesh axis runs over, the one named last changes fastest.
Arguments:
- tokens: bfloat16 [8, 2048, 576], P('dp', 'seq'), may hold values from -6 to 6
- cotangent: bfloat16 [8, 2048, 576], P('dp', 'seq'), may hold values from -6 to 6
- doc_lengths: int32 [8, 8], P('dp'), may hold values from 1 to 2048, as said below
- pad_count: int32 [8], P('dp'), may hold values from 0 to 256
- attn_gain: bfloat16 [2, 576], P('section'), may hold values from 0.5 to 1.5
- w_query: bfloat16 [2, 576, 576], P('section'), may hold values from -0.25 to 0.25
- w_key: bfloat16 [2, 576, 192], P('section'), may hold values from -0.25 to 0.25
- w_value: bfloat16 [2, 576, 192], P('section'), may hold values from -0.25 to 0.25
- w_out: bfloat16 [2, 576, 576], P('section'), may hold values from -1 to 1
- ffn_gain: bfloat16 [2, 576], P('section'), may hold values from 0.5 to 1.5
- w_gate: bfloat16 [2, 576, 1536], P('section'), may hold values from -0.25 to 0.25
- w_up: bfloat16 [2, 576, 1536], P('section'), may hold values from -0.25 to 0.25
- w_down: bfloat16 [2, 1536, 576], P('section'), may hold values from -0.15625 to 0.15625
Outputs:
- layer_out: bfloat16 [2, 8, 2048, 576], P('section', 'dp', 'seq')
- input_grad: bfloat16 [2, 8, 2048, 576], P('section', 'dp', 'seq')
- grad_gains: float32 [2, 1152], P('section', ('seq', 'dp'))
- grad_query: float32 [2, 331776], P('section', ('seq', 'dp'))
- grad_key: float32 [2, 110592], P('section', ('seq', 'dp'))
- grad_value: float32 [2, 110592], P('section', ('seq', 'dp'))
- grad_out: float32 [2, 331776], P('section', ('seq', 'dp'))
- grad_gate: float32 [2, 884736], P('section', ('seq', 'dp'))
- grad_up: float32 [2, 884736], P('section', ('seq', 'dp'))
- grad_down: float32 [2, 884736], P('section', ('seq', 'dp'))
Inputs may be any that keep to these rules, and one draw needn't show every extreme that they name: `doc_lengths`: documents lie end to end from position 0; positions at or past the last end form one more document. In each group of 2 sequences of one dp index, one sequence (which one varies) has a first document shorter than 512 and a second of length 2048.
All inputs are finite; a program needn't handle non-finite values.
Results may differ from a plain program's by a relative error of at most 0.025.
Values may be sent and summed in bfloat16 or wider, within the bound.
No kernel may reach another device: no remote copies, remote signals or barrier semaphores. Data moves between devices by JAX's collectives and lax.ppermute only.
A program may use at most 768 MiB of HBM per device.

v0:
```python
import jax
import jax.numpy as jnp
from jax import lax
from jax.sharding import PartitionSpec as P

H = 9
KV = 3
HD = 64


EPS = 1e-05
THETA = 10000.0
NEG = -1e30


def passed_along(value, axis, by):
    peers = lax.axis_size(axis)
    pairs = [(i, i + by) for i in range(peers) if 0 <= i + by < peers]
    return lax.ppermute(value, axis, pairs)


def product(left, right):
    return jnp.dot(left, right, preferred_element_type=jnp.float32)


def times_transposed(left, right):
    return lax.dot_general(
        left, right, (((1,), (1,)), ((), ())), preferred_element_type=jnp.float32
    )


def inner_rows(left, right):
    return lax.dot_general(
        left, right, (((0,), (0,)), ((), ())), preferred_element_type=jnp.float32
    )


def norm_parts(values_in, gain):
    inverse = lax.rsqrt(jnp.mean(values_in * values_in, axis=-1, keepdims=True) + EPS)
    return (values_in * inverse * gain, inverse)


def norm_back(gradient, values_in, inverse, gain):
    scaled = gradient * gain
    gain_grad = jnp.sum(gradient * values_in * inverse, axis=0)
    input_part = inverse * scaled - values_in * inverse**3 * jnp.mean(
        scaled * values_in, axis=-1, keepdims=True
    )
    return (input_part, gain_grad)


def rope_tables(positions):
    half_dim = HD // 2
    frequency = THETA ** (-2.0 * jnp.arange(half_dim, dtype=jnp.float32) / HD)
    angles = positions.astype(jnp.float32)[:, None] * frequency[None, :]
    return (jnp.cos(angles)[:, None, :], jnp.sin(angles)[:, None, :])


def rotate(values_in, tables, turn_sign):
    cosine, sine_tab = tables
    sine_tab = sine_tab * turn_sign
    row_count = values_in.shape[0]
    half_dim = HD // 2
    heads = values_in.reshape(row_count, -1, HD)
    leading = heads[..., :half_dim]
    trailing = heads[..., half_dim:]
    turned = jnp.concatenate(
        [leading * cosine - trailing * sine_tab, trailing * cosine + leading * sine_tab], axis=-1
    )
    return turned.reshape(row_count, -1)


def context(lengths_row, pad_len, shard_len, seq_total, seq_index):
    keys_at = jnp.arange(seq_total, dtype=jnp.int32)
    doc_ends = jnp.cumsum(lengths_row)
    segment = jnp.sum((doc_ends[None, :] <= keys_at[:, None]).astype(jnp.int32), axis=1)
    live_mask = keys_at < seq_total - pad_len
    rows_at = seq_index * shard_len + jnp.arange(shard_len, dtype=jnp.int32)
    row_segment = lax.dynamic_slice_in_dim(segment, seq_index * shard_len, shard_len, 0)
    allowed = (
        (keys_at[None, :] <= rows_at[:, None])
        & (segment[None, :] == row_segment[:, None])
        & live_mask[None, :]
    )
    allowed = allowed | (keys_at[None, :] == rows_at[:, None])
    return (allowed, rope_tables(rows_at))


def attention_scores(queries, keys_all, allowed):
    row_count = queries.shape[0]
    grouped = queries.reshape(row_count, KV, H // KV, HD)
    scores = jnp.einsum(
        "qngd,knd->ngqk",
        grouped,
        keys_all.reshape(keys_all.shape[0], KV, HD),
        preferred_element_type=jnp.float32,
    ) * HD ** (-0.5)
    return jnp.where(allowed[None, None], scores, NEG)


def fetch_first(keys_own, values_own):
    return (
        lax.all_gather(keys_own, "seq", axis=0, tiled=True),
        lax.all_gather(values_own, "seq", axis=0, tiled=True),
    )


def scatter_keys(key_terms, value_terms):
    return (
        lax.psum_scatter(
            key_terms.astype(jnp.bfloat16), "seq", scatter_dimension=0, tiled=True
        ).astype(jnp.float32),
        lax.psum_scatter(
            value_terms.astype(jnp.bfloat16), "seq", scatter_dimension=0, tiled=True
        ).astype(jnp.float32),
    )


def block_forward(resid, weights, allowed, tables, fetch):
    attn_gain, w_query, w_key, w_value, w_out, ffn_gain, w_gate, w_up, w_down = weights
    row_count = resid.shape[0]
    normed, inverse = norm_parts(resid, attn_gain)
    normed = normed.astype(jnp.bfloat16)
    queries = rotate(product(normed, w_query), tables, 1.0).astype(jnp.bfloat16)
    keys_own = rotate(product(normed, w_key), tables, 1.0).astype(jnp.bfloat16)
    values_own = product(normed, w_value).astype(jnp.bfloat16)
    keys_all, values_all = fetch(keys_own, values_own)
    scores = attention_scores(queries, keys_all, allowed)
    row_top = jnp.max(scores, axis=-1, keepdims=True)
    exponent = jnp.exp(scores - row_top)
    row_total = jnp.sum(exponent, axis=-1, keepdims=True)
    probs_low = (exponent / row_total).astype(jnp.bfloat16)
    log_total = row_top + jnp.log(row_total)
    attended = jnp.einsum(
        "ngqk,knd->qngd",
        probs_low,
        values_all.reshape(-1, KV, HD),
        preferred_element_type=jnp.float32,
    )
    attended = attended.reshape(row_count, -1).astype(jnp.bfloat16)
    hidden_in = resid + product(attended, w_out)
    normed_two, inverse_two = norm_parts(hidden_in, ffn_gain)
    normed_two = normed_two.astype(jnp.bfloat16)
    gate_part = product(normed_two, w_gate)
    up_part = product(normed_two, w_up)
    inner_act = (jax.nn.silu(gate_part) * up_part).astype(jnp.bfloat16)
    output = hidden_in + product(inner_act, w_down)
    saved_state = (
        resid,
        inverse,
        normed,
        queries,
        keys_all,
        values_all,
        log_total,
        attended,
        hidden_in,
        inverse_two,
        normed_two,
        gate_part,
        up_part,
        inner_act,
    )
    return (output, saved_state)


def block_backward(grad_out, weights, allowed, tables, saved_state):
    attn_gain, w_query, w_key, w_value, w_out, ffn_gain, w_gate, w_up, w_down = weights
    (
        resid,
        inverse,
        normed,
        queries,
        keys_all,
        values_all,
        log_total,
        attended,
        hidden_in,
        inverse_two,
        normed_two,
        gate_part,
        up_part,
        inner_act,
    ) = saved_state
    row_count = resid.shape[0]
    down_grad = grad_out.astype(jnp.bfloat16)
    inner_grad = times_transposed(down_grad, w_down)
    sigmoid_val = jax.nn.sigmoid(gate_part)
    gate_grad = (
        inner_grad * up_part * sigmoid_val * (1.0 + gate_part * (1.0 - sigmoid_val))
    ).astype(jnp.bfloat16)
    up_grad = (inner_grad * gate_part * sigmoid_val).astype(jnp.bfloat16)
    normed_two_grad = times_transposed(gate_grad, w_gate) + times_transposed(up_grad, w_up)
    hidden_grad, ffn_gain_grad = norm_back(normed_two_grad, hidden_in, inverse_two, ffn_gain)
    hidden_grad = hidden_grad + grad_out
    out_grad = hidden_grad.astype(jnp.bfloat16)
    attended_grad = times_transposed(out_grad, w_out).astype(jnp.bfloat16)
    scores = attention_scores(queries, keys_all, allowed)
    probs = jnp.exp(scores - log_total)
    probs_low = probs.astype(jnp.bfloat16)
    grouped_grad = attended_grad.reshape(row_count, KV, H // KV, HD)
    prob_grad = jnp.einsum(
        "qngd,knd->ngqk",
        grouped_grad,
        values_all.reshape(-1, KV, HD),
        preferred_element_type=jnp.float32,
    )
    score_grad = (probs * (prob_grad - jnp.sum(probs * prob_grad, axis=-1, keepdims=True))).astype(
        jnp.bfloat16
    )
    score_scale = HD ** (-0.5)
    query_grad = (
        jnp.einsum(
            "ngqk,knd->qngd",
            score_grad,
            keys_all.reshape(-1, KV, HD),
            preferred_element_type=jnp.float32,
        )
        * score_scale
    )
    query_grad = rotate(query_grad.reshape(row_count, -1), tables, -1.0).astype(jnp.bfloat16)
    grouped_query = queries.reshape(row_count, KV, H // KV, HD)
    key_total = keys_all.shape[0]
    key_terms = (
        jnp.einsum("ngqk,qngd->knd", score_grad, grouped_query, preferred_element_type=jnp.float32)
        * score_scale
    )
    value_terms = jnp.einsum(
        "ngqk,qngd->knd", probs_low, grouped_grad, preferred_element_type=jnp.float32
    )
    key_grad, value_grad = scatter_keys(
        key_terms.reshape(key_total, -1), value_terms.reshape(key_total, -1)
    )
    key_grad = rotate(key_grad, tables, -1.0).astype(jnp.bfloat16)
    value_grad = value_grad.astype(jnp.bfloat16)
    normed_grad = (
        times_transposed(query_grad, w_query)
        + times_transposed(key_grad, w_key)
        + times_transposed(value_grad, w_value)
    )
    input_part, attn_gain_grad = norm_back(normed_grad, resid, inverse, attn_gain)
    pair_items = (
        normed,
        query_grad,
        key_grad,
        value_grad,
        attended,
        out_grad,
        normed_two,
        gate_grad,
        up_grad,
        inner_act,
        down_grad,
    )
    return (input_part + hidden_grad, attn_gain_grad, ffn_gain_grad, pair_items)


def per_device(
    tokens,
    cotangent,
    doc_lengths,
    pad_count,
    attn_gain,
    w_query,
    w_key,
    w_value,
    w_out,
    ffn_gain,
    w_gate,
    w_up,
    w_down,
):
    weights = (
        attn_gain[0],
        w_query[0],
        w_key[0],
        w_value[0],
        w_out[0],
        ffn_gain[0],
        w_gate[0],
        w_up[0],
        w_down[0],
    )
    micro_count = tokens.shape[0]
    shard_len = tokens.shape[1]
    model_dim = tokens.shape[2]
    seq_total = shard_len * lax.axis_size("seq")
    seq_index = lax.axis_index("seq")
    section_first = lax.axis_index("section") == 0

    def settings(early_micro, late_micro):
        lengths_row = jnp.where(section_first, doc_lengths[early_micro], doc_lengths[late_micro])
        pad_len = jnp.where(section_first, pad_count[early_micro], pad_count[late_micro])
        return context(lengths_row, pad_len, shard_len, seq_total, seq_index)

    received = jnp.zeros((shard_len, model_dim), jnp.bfloat16)
    layer_inputs = []
    layer_outputs = []
    kept_state = []
    for moment in range(micro_count + 1):
        early_micro = min(moment, micro_count - 1)
        late_micro = max(moment - 1, 0)
        layer_in = jnp.where(section_first, tokens[early_micro], received)
        allowed, tables = settings(early_micro, late_micro)
        middle, saved_one = block_forward(
            layer_in.astype(jnp.float32), weights, allowed, tables, fetch_first
        )
        layer_final, saved_two = block_forward(middle, weights, allowed, tables, fetch_first)
        final_low = layer_final.astype(jnp.bfloat16)
        layer_inputs.append(layer_in)
        layer_outputs.append(final_low)
        kept_state.append((saved_one, saved_two))
        if moment < micro_count:
            received = passed_along(final_low, "section", 1)
    sent_grad = jnp.zeros((shard_len, model_dim), jnp.bfloat16)
    zero_grad = jnp.zeros((shard_len, model_dim), jnp.float32)
    attn_gain_sum = jnp.zeros((model_dim,), jnp.float32)
    ffn_gain_sum = jnp.zeros((model_dim,), jnp.float32)
    input_grads = []
    pair_lists = []
    for moment in range(micro_count + 1):
        early_micro = max(moment - 1, 0)
        late_micro = min(moment, micro_count - 1)
        top_grad = cotangent[moment].astype(jnp.float32) if moment < micro_count else zero_grad
        upstream = jnp.where(section_first, sent_grad.astype(jnp.float32), top_grad)
        allowed, tables = settings(early_micro, late_micro)
        early_tick = max(moment - 1, 0)
        late_tick = min(moment + 1, micro_count)
        saved_one, saved_two = jax.tree.map(
            lambda lower, upper: jnp.where(section_first, lower, upper),
            kept_state[early_tick],
            kept_state[late_tick],
        )
        middle_grad, gain_first, gain_second, pairs_two = block_backward(
            upstream, weights, allowed, tables, saved_two
        )
        layer_grad, gain_third, gain_fourth, pairs_one = block_backward(
            middle_grad, weights, allowed, tables, saved_one
        )
        attn_gain_sum = attn_gain_sum + gain_first + gain_third
        ffn_gain_sum = ffn_gain_sum + gain_second + gain_fourth
        pair_lists.append(pairs_one)
        pair_lists.append(pairs_two)
        grad_low = layer_grad.astype(jnp.bfloat16)
        input_grads.append(grad_low)
        if moment < micro_count:
            sent_grad = passed_along(grad_low, "section", -1)
    layer_out = jnp.stack(
        [
            jnp.where(section_first, layer_outputs[micro], layer_outputs[micro + 1])
            for micro in range(micro_count)
        ]
    )[None]
    input_grad = jnp.stack(
        [
            jnp.where(section_first, input_grads[micro + 1], input_grads[micro])
            for micro in range(micro_count)
        ]
    )[None]
    columns = [
        jnp.concatenate([pair_items[index_pos] for pair_items in pair_lists], axis=0)
        for index_pos in range(11)
    ]
    grad_query = inner_rows(columns[0], columns[1]).reshape(-1)
    grad_key = inner_rows(columns[0], columns[2]).reshape(-1)
    grad_value = inner_rows(columns[0], columns[3]).reshape(-1)
    grad_out = inner_rows(columns[4], columns[5]).reshape(-1)
    grad_gate = inner_rows(columns[6], columns[7]).reshape(-1)
    grad_up = inner_rows(columns[6], columns[8]).reshape(-1)
    grad_down = inner_rows(columns[9], columns[10]).reshape(-1)
    grad_gains = jnp.concatenate([attn_gain_sum, ffn_gain_sum])
    summed = (
        lax.psum_scatter(grad_gains, ("seq", "dp"), scatter_dimension=0, tiled=True),
        lax.psum_scatter(grad_query, ("seq", "dp"), scatter_dimension=0, tiled=True),
        lax.psum_scatter(grad_key, ("seq", "dp"), scatter_dimension=0, tiled=True),
        lax.psum_scatter(grad_value, ("seq", "dp"), scatter_dimension=0, tiled=True),
        lax.psum_scatter(grad_out, ("seq", "dp"), scatter_dimension=0, tiled=True),
        lax.psum_scatter(grad_gate, ("seq", "dp"), scatter_dimension=0, tiled=True),
        lax.psum_scatter(grad_up, ("seq", "dp"), scatter_dimension=0, tiled=True),
        lax.psum_scatter(grad_down, ("seq", "dp"), scatter_dimension=0, tiled=True),
    )
    return (layer_out, input_grad) + tuple((piece.reshape(1, -1) for piece in summed))


def solution(mesh):
    placed = (
        P("dp", "seq", None),
        P("dp", "seq", None),
        P("dp", None),
        P("dp"),
        P("section", None),
        P("section", None, None),
        P("section", None, None),
        P("section", None, None),
        P("section", None, None),
        P("section", None),
        P("section", None, None),
        P("section", None, None),
        P("section", None, None),
    )
    return jax.shard_map(
        per_device,
        mesh=mesh,
        in_specs=placed,
        out_specs=(
            P("section", "dp", "seq", None),
            P("section", "dp", "seq", None),
            P("section", ("seq", "dp")),
            P("section", ("seq", "dp")),
            P("section", ("seq", "dp")),
            P("section", ("seq", "dp")),
            P("section", ("seq", "dp")),
            P("section", ("seq", "dp")),
            P("section", ("seq", "dp")),
            P("section", ("seq", "dp")),
        ),
        check_vma=False,
    )
```

profile of v0, /device:TPU:0, one launch (start us, length us, event | category | flops | bytes accessed | tf_op | source)
XLA Modules:
  0.0 2141.8 jit_solution(3883199915125570313)
XLA Ops:
  16.7 21.7 %all_gather.36 = bf16[2048,192]{0,1:T(8,128)(2,1)} all-gather(bf16[512,192]{0,1:T(8,128)(2,1)S(1)} %convolution_convert_fusion.11), channel_id=1, replica_groups=mesh['section'=2,'seq'=4,'dp'=4] {'seq'}, dimensions={0}, use_global_device_ids=true | all-gather | bytes 983040 | tf_op jit(solution)/shard_map/all_gather | solution.py:104
  134.2 18.4 all_gather.38
  235.2 19.2 all_gather.40
  254.5 18.5 all_gather.41
  410.8 18.3 fusion.260
  481.9 32.0 %fusion.19 = (f32[3,3,512]{2,1,0:T(4,128)}, f32[3,2048,512,3]{2,1,3,0:T(8,128)}) fusion(f32[3,2048,512,3]{2,1,3,0:T(8,128)} %fusion.379, f32[3,3,512]{2,1,0:T(4,128)} %broadcast_select_fusion.53, pred[512,2048]{0,1:T(8,128)(4,1)S(1)} %copy-done.4, bf16[2048,3,64,1]{0,2,3,1:T(8,128)(2,1)} %bitcast.1153, bf16[512,3,3,64]{0,3,2,1:T(8,128)(2,1)} %bitcast.1183), kind=kOutput, calls=%fused_computation.33 | convolution fusion | flops 1255140864 | bytes 77959168 | tf_op jit(solution)/shard_map/qngd,knd->ngqk/dot_general | solution.py:202
  513.9 31.6 %fusion.21 = bf16[3,3,512,2048]{2,3,1,0:T(8,128)(2,1)} fusion(f32[3,2048,512,3]{2,1,3,0:T(8,128)} %get-tuple-element.262, f32[3,2048,512,3]{2,1,3,0:T(8,128)} %fusion.379, f32[3,3,512]{2,1,0:T(4,128)} %get-tuple-element.261, f32[3,3,512]{2,1,0:T(4,128)} %broadcast_select_fusion.53, pred[512,2048]{0,1:T(8,128)(4,1)S(1)} %copy-done.4), kind=kLoop, calls=%fused_computation.35 | loop fusion | flops 56623104 | bytes 95457280 | tf_op jit(solution)/shard_map/convert_element_type | solution.py:208
  602.5 20.8 reduce-scatter.15.cloned.1.call-done
  642.0 34.8 %fusion.16 = (f32[3,3,512]{2,1,0:T(4,128)S(1)}, f32[3,2048,512,3]{2,1,3,0:T(8,128)}) fusion(f32[3,2048,512,3]{2,1,3,0:T(8,128)} %fusion.378, f32[3,3,512]{2,1,0:T(4,128)} %broadcast_select_fusion.54, pred[512,2048]{0,1:T(8,128)(4,1)S(1)} %copy-done.4, bf16[2048,3,64,1]{0,2,3,1:T(8,128)(2,1)} %bitcast.1152, bf16[512,3,3,64]{0,3,2,1:T(8,128)(2,1)} %bitcast.1172), kind=kOutput, calls=%fused_computation.28 | convolution fusion | flops 1255140864 | bytes 77959168 | tf_op jit(solution)/shard_map/qngd,knd->ngqk/dot_general | solution.py:202
  676.8 31.5 %fusion.18 = bf16[3,3,512,2048]{2,3,1,0:T(8,128)(2,1)} fusion(f32[3,2048,512,3]{2,1,3,0:T(8,128)} %get-tuple-element.266, f32[3,2048,512,3]{2,1,3,0:T(8,128)} %fusion.378, f32[3,3,512]{2,1,0:T(4,128)S(1)} %get-tuple-element.265, f32[3,3,512]{2,1,0:T(4,128)S(1)} %copy-done.257, pred[512,2048]{0,1:T(8,128)(4,1)S(1)} %copy-done.4), kind=kLoop, calls=%fused_computation.30 | loop fusion | flops 56623104 | bytes 95457280 | tf_op jit(solution)/shard_map/convert_element_type | solution.py:208
  788.6 18.6 all_gather.44
  859.1 18.6 broadcast_select_fusion.19
  970.8 18.3 broadcast_select_fusion.18
  1086.2 32.1 %fusion.13 = (f32[3,3,512]{2,1,0:T(4,128)}, f32[3,2048,512,3]{2,1,3,0:T(8,128)}) fusion(f32[3,2048,512,3]{2,1,3,0:T(8,128)} %fusion.377, f32[3,3,512]{2,1,0:T(4,128)} %get-tuple-element.204, pred[512,2048]{0,1:T(8,128)(4,1)} %get-tuple-element.220, bf16[2048,3,64,1]{0,2,3,1:T(8,128)(2,1)} %bitcast.1157, bf16[512,3,3,64]{0,3,2,1:T(8,128)(2,1)} %bitcast.1178), kind=kOutput, calls=%fused_computation.23 | convolution fusion | flops 1255140864 | bytes 77959168 | tf_op jit(solution)/shard_map/qngd,knd->ngqk/dot_general | solution.py:202
  1118.3 32.4 %fusion.15 = bf16[3,3,512,2048]{2,3,1,0:T(8,128)(2,1)} fusion(f32[3,2048,512,3]{2,1,3,0:T(8,128)} %get-tuple-element.282, f32[3,2048,512,3]{2,1,3,0:T(8,128)} %fusion.377, f32[3,3,512]{2,1,0:T(4,128)} %get-tuple-element.281, f32[3,3,512]{2,1,0:T(4,128)} %get-tuple-element.204, pred[512,2048]{0,1:T(8,128)(4,1)} %get-tuple-element.220), kind=kLoop, calls=%fused_computation.25 | loop fusion | flops 56623104 | bytes 95457280 | tf_op jit(solution)/shard_map/convert_element_type | solution.py:208
  1229.9 32.2 %fusion.10 = (f32[3,3,512]{2,1,0:T(4,128)}, f32[3,2048,512,3]{2,1,3,0:T(8,128)}) fusion(f32[3,2048,512,3]{2,1,3,0:T(8,128)} %fusion.376, f32[3,3,512]{2,1,0:T(4,128)} %get-tuple-element.202, pred[512,2048]{0,1:T(8,128)(4,1)} %get-tuple-element.220, bf16[2048,3,64,1]{0,2,3,1:T(8,128)(2,1)} %bitcast.1156, bf16[512,3,3,64]{0,3,2,1:T(8,128)(2,1)} %bitcast.1174), kind=kOutput, calls=%fused_computation.18 | convolution fusion | flops 1255140864 | bytes 77959168 | tf_op jit(solution)/shard_map/qngd,knd->ngqk/dot_general | solution.py:202
  1262.1 32.6 %fusion.12 = bf16[3,3,512,2048]{2,3,1,0:T(8,128)(2,1)} fusion(f32[3,2048,512,3]{2,1,3,0:T(8,128)} %get-tuple-element.286, f32[3,2048,512,3]{2,1,3,0:T(8,128)} %fusion.376, f32[3,3,512]{2,1,0:T(4,128)} %get-tuple-element.285, f32[3,3,512]{2,1,0:T(4,128)} %get-tuple-element.202, pred[512,2048]{0,1:T(8,128)(4,1)} %get-tuple-element.220), kind=kLoop, calls=%fused_computation.20 | loop fusion | flops 56623104 | bytes 95457280 | tf_op jit(solution)/shard_map/convert_element_type | solution.py:208
  1389.3 31.8 %fusion.3 = (f32[3,3,512]{2,1,0:T(4,128)}, f32[3,2048,512,3]{2,1,3,0:T(8,128)}) fusion(f32[3,2048,512,3]{2,1,3,0:T(8,128)} %fusion.381, f32[3,3,512]{2,1,0:T(4,128)} %get-tuple-element.203, pred[512,2048]{0,1:T(8,128)(4,1)S(1)} %copy-done.2, bf16[2048,3,64,1]{0,2,3,1:T(8,128)(2,1)} %bitcast.1155, bf16[512,3,3,64]{0,3,2,1:T(8,128)(2,1)} %bitcast.1176), kind=kOutput, calls=%fused_computation.7 | convolution fusion | flops 1255140864 | bytes 77959168 | tf_op jit(solution)/shard_map/qngd,knd->ngqk/dot_general | solution.py:202
  1421.1 31.5 %fusion.5 = bf16[3,3,512,2048]{2,3,1,0:T(8,128)(2,1)} fusion(f32[3,2048,512,3]{2,1,3,0:T(8,128)} %get-tuple-element.290, f32[3,2048,512,3]{2,1,3,0:T(8,128)} %fusion.381, f32[3,3,512]{2,1,0:T(4,128)} %get-tuple-element.289, f32[3,3,512]{2,1,0:T(4,128)} %get-tuple-element.203, pred[512,2048]{0,1:T(8,128)(4,1)S(1)} %copy-done.2), kind=kLoop, calls=%fused_computation.9 | loop fusion | flops 56623104 | bytes 95457280 | tf_op jit(solution)/shard_map/convert_element_type | solution.py:208
  1497.3 18.3 reduce-scatter.31.cloned.1.call-done
  1551.3 26.5 %fusion = (f32[3,3,512]{2,1,0:T(4,128)S(1)}, f32[3,2048,512,3]{2,1,3,0:T(8,128)}) fusion(f32[3,2048,512,3]{2,1,3,0:T(8,128)} %fusion.380, f32[3,3,512]{2,1,0:T(4,128)S(1)} %copy-done.256, pred[512,2048]{0,1:T(8,128)(4,1)S(1)} %copy-done.2, bf16[2048,3,64,1]{0,2,3,1:T(8,128)(2,1)} %bitcast.1154, bf16[512,3,3,64]{0,3,2,1:T(8,128)(2,1)S(1)} %bitcast.1181), kind=kOutput, calls=%fused_computation.2 | convolution fusion | flops 1255140864 | bytes 77959168 | tf_op jit(solution)/shard_map/qngd,knd->ngqk/dot_general | solution.py:202
  1577.8 31.4 %fusion.2 = bf16[3,3,512,2048]{2,3,1,0:T(8,128)(2,1)} fusion(f32[3,2048,512,3]{2,1,3,0:T(8,128)} %get-tuple-element.294, f32[3,2048,512,3]{2,1,3,0:T(8,128)} %fusion.380, f32[3,3,512]{2,1,0:T(4,128)S(1)} %get-tuple-element.293, f32[3,3,512]{2,1,0:T(4,128)S(1)} %copy-done.256, pred[512,2048]{0,1:T(8,128)(4,1)S(1)} %copy-done.2), kind=kLoop, calls=%fused_computation.4 | loop fusion | flops 56623104 | bytes 95457280 | tf_op jit(solution)/shard_map/convert_element_type | solution.py:208
  1731.5 43.1 %all-reduce = f32[1152]{0:T(1024)S(1)} all-reduce(f32[1152]{0:T(1024)S(1)} %pad_maximum_fusion.12), channel_id=14, replica_groups=mesh['section'=2,'seq'=4,'dp'=4] {'seq','dp'}, use_global_device_ids=true, to_apply=%region_74.75.clone | all-reduce | flops 1152 | bytes 9216
  1776.3 347.2 %all-reduce.11.cloned.1.call-done = (f32[331776]{0:T(1024)}, f32[110592]{0:T(1024)}, f32[110592]{0:T(1024)}, f32[331776]{0:T(1024)}, f32[884736]{0:T(1024)}, /*index=5*/f32[884736]{0:T(1024)}, f32[884736]{0:T(1024)}) async-done(((f32[331776]{0:T(1024)}, f32[110592]{0:T(1024)}, f32[110592]{0:T(1024)}, f32[331776]{0:T(1024)}, f32[884736]{0:T(1024)}, /*index=5*/f32[884736]{0:T(1024)}, f32[884736]{0:T(1024)}), ...) | async-done | bytes 14155792
  (1190 shorter events, 1154.9 us)
Async XLA Ops:
  7.2 123.3 %copy-start = (bf16[1,1536,576]{1,2,0:T(8,128)(2,1)S(1)}, bf16[1,1536,576]{1,2,0:T(8,128)(2,1)}, u32[]{:S(2)}) copy-start(bf16[1,1536,576]{1,2,0:T(8,128)(2,1)} %param.25) | copy-start | bytes 5308420
  7.2 591.2 %reduce-scatter.13.cloned.1.call-start = ((), (), s32[]{:S(2)}) async-start(), calls=%async_computation.12 | async-start | bytes 983040 | tf_op jit(solution)/shard_map/reduce_scatter | solution.py:110
  13.2 49.6 %copy-start.229 = (f32[576]{0:T(1024)}, f32[576]{0:T(1024)S(1)}, u32[]{:S(2)}) copy-start(f32[576]{0:T(1024)S(1)} %convert_reduce_fusion.5) | copy-start | bytes 6916
  15.1 47.8 %copy-start.317 = (f32[512]{0:T(512)}, f32[512]{0:T(512)S(1)}, u32[]{:S(2)}) copy-start(f32[512]{0:T(512)S(1)} %add_rsqrt_fusion.11) | copy-start | bytes 6148
  72.6 128.2 %copy-start.3 = (pred[512,2048]{0,1:T(8,128)(4,1)}, pred[512,2048]{0,1:T(8,128)(4,1)S(1)}, u32[]{:S(2)}) copy-start(pred[512,2048]{0,1:T(8,128)(4,1)S(1)} %get-tuple-element.222) | copy-start | bytes 3145732
  228.4 3.0 collective-permute-start
  358.7 51.1 %copy-start.152 = (bf16[2048,192]{0,1:T(8,128)(2,1)}, bf16[2048,192]{0,1:T(8,128)(2,1)S(1)}, u32[]{:S(2)}) copy-start(bf16[2048,192]{0,1:T(8,128)(2,1)S(1)} %all_gather.42) | copy-start | bytes 2359300
  573.4 211.7 %collective-permute-start.1 = (bf16[512,576]{0,1:T(8,128)(2,1)}, bf16[512,576]{0,1:T(8,128)(2,1)}, u32[]{:S(2)}, u32[]{:S(2)}) collective-permute-start(bf16[512,576]{0,1:T(8,128)(2,1)} %fusion.252), channel_id=1, source_target_pairs={{0,16},{1,17},{2,18},{3,19},{4,20},{5,21},{6,22},{7,23},{8,24},{9,... | collective-permute-start | bytes 1769480 | tf_op jit(solution)/shard_map/ppermute | solution.py:19
  575.5 47.8 %reduce-scatter.15.cloned.1.call-start = ((), (), s32[]{:S(2)}) async-start(), calls=%async_computation.13 | async-start | bytes 983040 | tf_op jit(solution)/shard_map/reduce_scatter | solution.py:113
  591.7 170.5 %reduce-scatter.17.cloned.1.call-start = ((), (), s32[]{:S(2)}) async-start(), calls=%async_computation.14 | async-start | bytes 983040 | tf_op jit(solution)/shard_map/reduce_scatter | solution.py:110
  732.6 47.5 %reduce-scatter.19.cloned.1.call-start = ((), (), s32[]{:S(2)}) async-start(), calls=%async_computation.15 | async-start | bytes 983040 | tf_op jit(solution)/shard_map/reduce_scatter | solution.py:113
  753.4 438.2 %reduce-scatter.21.cloned.1.call-start = ((), (), s32[]{:S(2)}) async-start(), calls=%async_computation.16 | async-start | bytes 983040 | tf_op jit(solution)/shard_map/reduce_scatter | solution.py:110
  991.4 89.6 %copy-start.45 = (f32[512,576]{0,1:T(8,128)}, f32[512,576]{0,1:T(8,128)S(1)}, u32[]{:S(2)}) copy-start(f32[512,576]{0,1:T(8,128)S(1)} %get-tuple-element.278) | copy-start | bytes 3538948
  996.9 78.7 %collective-permute-start.2 = (bf16[512,576]{0,1:T(8,128)(2,1)S(1)}, bf16[512,576]{0,1:T(8,128)(2,1)S(1)}, u32[]{:S(2)}, u32[]{:S(2)}) collective-permute-start(bf16[512,576]{0,1:T(8,128)(2,1)S(1)} %copy-done.195), channel_id=1, source_target_pairs={{16,0},{17,1},{18,2},{19,3},{20,4},{21,5},{22,6},{23,7},{24,8},{25... | collective-permute-start | bytes 1769480 | tf_op jit(solution)/shard_map/ppermute | solution.py:19
  1163.9 48.4 %reduce-scatter.23.cloned.1.call-start = ((), (), s32[]{:S(2)}) async-start(), calls=%async_computation.17 | async-start | bytes 983040 | tf_op jit(solution)/shard_map/reduce_scatter | solution.py:113
  1181.8 164.8 %reduce-scatter.25.cloned.1.call-start = ((), (), s32[]{:S(2)}) async-start(), calls=%async_computation.18 | async-start | bytes 983040 | tf_op jit(solution)/shard_map/reduce_scatter | solution.py:110
  1318.8 47.6 %reduce-scatter.27.cloned.1.call-start = ((), (), s32[]{:S(2)}) async-start(), calls=%async_computation.19 | async-start | bytes 983040 | tf_op jit(solution)/shard_map/reduce_scatter | solution.py:113
  1340.2 153.1 %reduce-scatter.29.cloned.1.call-start = ((), (), s32[]{:S(2)}) async-start(), calls=%async_computation.20 | async-start | bytes 983040 | tf_op jit(solution)/shard_map/reduce_scatter | solution.py:110
  1373.3 5.4 collective-permute-start.3
  1465.8 49.9 %reduce-scatter.31.cloned.1.call-start = ((), (), s32[]{:S(2)}) async-start(), calls=%async_computation.21 | async-start | bytes 983040 | tf_op jit(solution)/shard_map/reduce_scatter | solution.py:113
  1483.7 208.5 %reduce-scatter.33.cloned.1.call-start = ((), (), s32[]{:S(2)}) async-start(), calls=%async_computation.22 | async-start | bytes 983040 | tf_op jit(solution)/shard_map/reduce_scatter | solution.py:110
  1633.3 62.2 %reduce-scatter.35.cloned.1.call-start = ((), (), s32[]{:S(2)}) async-start(), calls=%async_computation.23 | async-start | bytes 983040 | tf_op jit(solution)/shard_map/reduce_scatter | solution.py:113
  1655.4 468.1 %all-reduce.11.cloned.1.call-start = ((), (), s32[]{:S(2)}) async-start(), calls=%async_computation.24 | async-start | bytes 28311552
  1730.2 45.0 %copy-start.197 = (bf16[1,512,576]{1,2,0:T(8,128)(2,1)S(1)}, bf16[1,512,576]{1,2,0:T(8,128)(2,1)}, u32[]{:S(2)}) copy-start(bf16[1,512,576]{1,2,0:T(8,128)(2,1)} %get-tuple-element.85) | copy-start | bytes 1769476
  (396 other events, 2179.2 us)
Sparse Core Ops, SparseCore 0:
  575.6 22.7 reduce-scatter.12
  600.7 22.5 reduce-scatter.14
  732.7 22.5 reduce-scatter.16
  757.5 22.5 reduce-scatter.18
  1164.0 23.5 reduce-scatter.20
  1189.7 22.4 reduce-scatter.22
  1319.0 22.5 reduce-scatter.24
  1343.9 22.5 reduce-scatter.26
  1465.9 24.9 reduce-scatter.28
  1493.1 22.5 reduce-scatter.30
  1633.4 22.5 reduce-scatter.32
  1658.1 22.6 reduce-scatter.34
  1722.1 401.3 all-reduce.10
where the time goes:
time: 2160 us; the launch traced here: 2140 us
  matrix products  925 us (43%)
  waiting for transfers between devices  438 us (20%)
  other arithmetic  377 us (17%)
  blocking collectives  262 us (12%)
  local copies, waits for them, and re-layouts  106 us (5%)
  between operations  25.2 us (1%)
    unnamed x14, waiting for transfers between devices  347 us
    convert_element_type x6, other arithmetic, block_backward(): (probs * (prob_grad - jnp.sum(probs * prob_grad, axis=-1, keepdims=True))...  191 us
    dot_general x6, matrix products, block_backward(): jnp.einsum('qngd,knd->ngqk', grouped_grad, values_all.reshape(-1, KV, HD)...  189 us
    dot_general x12, matrix products, attention_scores(): jnp.einsum('qngd,knd->ngqk', grouped, keys_all.reshape(keys_all.shape[0],...  181 us
    all_gather x6, blocking collectives, fetch_first(): lax.all_gather(values_own, 'seq', axis=0, tiled=True)  114 us
    dot_general x6, matrix products, block_forward(): jnp.einsum('ngqk,knd->qngd', probs_low, values_all.reshape(-1, KV, HD), p...  109 us
    dot_general x6, matrix products, block_backward(): jnp.einsum('ngqk,qngd->knd', probs_low, grouped_grad, preferred_element_t...  106 us
    all_gather x6, blocking collectives, fetch_first(): lax.all_gather(keys_own, 'seq', axis=0, tiled=True)  105 us
  transfers between devices with their start and end apart: 17, of which 8 were waited for; matrix products, arithmetic and copies ran while one was open for 19% of the time, Pallas kernels for 0%

commit v1 on v0

v1 whole, which is shorter than its diff:
```python
import functools

import jax
import jax.numpy as jnp
import numpy as np
from jax import lax
from jax.experimental import pallas as pl
from jax.experimental.pallas import tpu as pltpu
from jax.sharding import PartitionSpec as P

H = 9
KV = 3
HD = 64
GQ = H // KV
EPS = 1e-05
THETA = 10000.0
NEG = -1e30
LOG2E = 1.4426950408889634
LN2 = 0.6931471805599453
SCALE = HD**-0.5
KB = 256
SLAB = 256
KVD = KV * HD
SEG0 = KVD
LIVE = SEG0 + 9
LSE0 = SEG0 + 10
VOFF = 64
F32 = jnp.float32
BF16 = jnp.bfloat16
ANY = pl.ANY


def dot(a, b):
    return jnp.dot(a, b, preferred_element_type=F32)


def dot_t(a, b):
    return lax.dot_general(a, b, (((1,), (1,)), ((), ())), preferred_element_type=F32)


def masks_host():
    out = np.zeros((16, SLAB), np.float32)
    for n in range(KV):
        out[n, n * HD : (n + 1) * HD] = 1
        out[3 + n, VOFF + n * HD : VOFF + (n + 1) * HD] = 1
        out[6 + n, LSE0 + 3 * n : LSE0 + 3 * n + 3] = 1
        out[9 + n, 3 * n : 3 * n + 3] = 1
    return out


def swapped(t):
    lane = lax.broadcasted_iota(jnp.int32, (t.shape[0], 128), 1)
    first = (lane % HD) < HD // 2
    parts = []
    for at in range(0, t.shape[1], 128):
        u = t[:, at : at + 128]
        parts.append(
            jnp.where(first, pltpu.roll(u, 128 - HD // 2, 1), pltpu.roll(u, HD // 2, 1))
        )
    return jnp.concatenate(parts, axis=1)


def split_three(v):
    hi = v.astype(BF16).astype(F32)
    rest = v - hi
    mid = rest.astype(BF16).astype(F32)
    return hi, mid, rest - mid


class Weights:
    def __init__(self, mine, theirs, scratch, sem, flag):
        self.items = list(zip(mine, theirs, scratch))
        self.sem = sem
        self.flag = flag
        self.scratch = scratch

    def start(self):
        for i, (mine, theirs, into) in enumerate(self.items):

            @pl.when(self.flag == 1)
            def _():
                pltpu.make_async_copy(mine, into, self.sem.at[i]).start()

            @pl.when(self.flag != 1)
            def _():
                pltpu.make_async_copy(theirs, into, self.sem.at[i]).start()

    def wait(self, i):
        mine, _, into = self.items[i]
        pltpu.make_async_copy(mine, into, self.sem.at[i]).wait()
        return into


def copy_pieces(pieces, refs, into, sem, scal, base):
    copies = []
    for i, (part, row, rows) in enumerate(pieces):
        at = pl.multiple_of(scal[base + i] * 32, 32)
        c = pltpu.make_async_copy(
            refs[part].at[pl.ds(row, rows)], into.at[pl.ds(at, rows)], sem.at[i]
        )
        c.start()
        copies.append(c)
    return copies


def qkv_out(y, gain, wqkv, cos, sin, qcode, q_out, kv_out):
    r = lax.rsqrt(jnp.mean(y * y, axis=-1, keepdims=True) + EPS)
    normed = (y * r * gain).astype(BF16)
    for j in range(GQ):
        t = dot(normed, wqkv[:, j * SLAB : (j + 1) * SLAB])
        t = (t * cos + swapped(t) * sin) * (SCALE * LOG2E)
        q_out[j] = t.astype(BF16) + qcode
    t = dot(normed, wqkv[:, GQ * SLAB :])
    u = t[:, :SLAB]
    u = u * cos + swapped(u) * sin
    kv_out[:, :SLAB] = u.astype(BF16)
    kv_out[:, SLAB:] = t[:, SLAB:].astype(BF16)


def first_kernel(scal, x, cos, sin, qcode, wm, wt, gm, gt, q_out, kv_out, wv, gv, sem):
    w = Weights([wm, gm], [wt, gt], [wv, gv], sem, scal[0])
    w.start()
    w.wait(0)
    w.wait(1)
    qkv_out(
        x[...].astype(F32), gv[0:1, :], wv, cos[...], sin[...], qcode[...], q_out, kv_out
    )


def forward_kernel(cfg, *refs):
    (R, G, pieces, n_parts, has_next, rounded) = cfg
    RG = R // G
    M = GQ * RG
    it = iter(refs)
    take = lambda n: [next(it) for _ in range(n)]
    scal, x, q, kcode, bias, masks, cos, sin, qcode = take(9)
    parts = take(n_parts)
    mine, theirs = take(5), take(5)
    if has_next:
        mine_n, theirs_n = take(2), take(2)
    y_out, h_out, att_out, gate_out, up_out, qb_out = take(6)
    if has_next:
        q_out, kv_out = take(2)
    if rounded:
        low_out = next(it)
    kvs, s_scr, m_scr, l_scr, acc, act = take(6)
    wout, wg, wu, wd, gv = take(5)
    if has_next:
        wqkv, gn = take(2)
    sem_kv, sem_w = take(2)
    if has_next:
        sem_n = next(it)
    base = 2 + 2 * G
    copies = copy_pieces(pieces, parts, kvs, sem_kv, scal, base)
    w = Weights(mine, theirs, [wout, wg, wu, wd, gv], sem_w, scal[0])
    w.start()
    if has_next:
        wn = Weights(mine_n, theirs_n, [wqkv, gn], sem_n, scal[1])
        wn.start()
    for c in copies:
        c.wait()

    lane = lax.broadcasted_iota(jnp.int32, (1, SLAB), 1)
    high = lane[:, 128:]
    halves = lambda t: jnp.maximum(t[:, :128], t[:, 128:])
    for g in range(G):
        rows = slice(g * RG, (g + 1) * RG)
        qg = jnp.concatenate([q[j, rows, :] for j in range(GQ)], axis=0)
        db = scal[2 + g]
        lb = scal[2 + G + g]

        def keys_of(b):
            return kvs[pl.ds(pl.multiple_of(b * KB, KB), KB), 0:SLAB]

        def values_of(b):
            return kvs[pl.ds(pl.multiple_of(b * KB, KB), KB), 128 : 128 + SLAB]

        k_d = keys_of(db)
        tile_bias = jnp.concatenate([bias[g]] * GQ, axis=0)
        for n in range(KV):
            s = dot_t(qg, k_d * masks[n : n + 1, :]) + tile_bias
            s_scr[n, db] = s
            m_scr[n] = halves(s)

        def first_pass(b, _):
            k = keys_of(b)
            code = kcode[pl.ds(pl.multiple_of(b * KB, KB), KB), :]
            for n in range(KV):
                s = dot_t(qg, k * masks[n : n + 1, :] + code)
                s_scr[n, b] = s
                m_scr[n] = jnp.maximum(m_scr[n], halves(s))
            return 0

        lax.fori_loop(lb, db, first_pass, 0)
        for n in range(KV):
            m = jnp.max(m_scr[n], axis=1, keepdims=True)
            m_scr[n] = jnp.broadcast_to(m, (M, 128))
        l_scr[...] = jnp.zeros_like(l_scr)
        acc[...] = jnp.zeros_like(acc)

        def second_pass(b, _):
            v = values_of(b)
            for n in range(KV):
                m = m_scr[n]
                s = s_scr[n, b]
                p0 = jnp.exp2(s[:, :128] - m)
                p1 = jnp.exp2(s[:, 128:] - m)
                l_scr[n] += p0 + p1
                p = jnp.concatenate([p0.astype(BF16), p1.astype(BF16)], axis=1)
                acc[n] += dot(p, v * masks[3 + n : 4 + n, :])
            return 0

        lax.fori_loop(lb, db + 1, second_pass, 0)
        out = jnp.zeros((M, SLAB), F32)
        code = jnp.zeros((M, 128), F32)
        for n in range(KV):
            l = jnp.sum(l_scr[n], axis=1, keepdims=True)
            out = out + acc[n] * (1.0 / l)
            lse = m_scr[n][:, :1] + jnp.log2(l)
            for i, part in enumerate(split_three(-lse)):
                code = code + jnp.where(high == LSE0 + 3 * n + i, part, 0.0)
        out = out.astype(BF16)
        qb = jnp.concatenate([qg[:, :128], qg[:, 128:] + code.astype(BF16)], axis=1)
        for j in range(GQ):
            att_out[j, rows, :] = out[j * RG : (j + 1) * RG]
            qb_out[j, rows, :] = qb[j * RG : (j + 1) * RG]

    w.wait(0)
    w.wait(4)
    h = x[...].astype(F32)
    for j in range(GQ):
        h = h + dot(att_out[j], wout[j * SLAB : (j + 1) * SLAB, :])
    h_out[...] = h
    r2 = lax.rsqrt(jnp.mean(h * h, axis=-1, keepdims=True) + EPS)
    n2 = (h * r2 * gv[1:2, :]).astype(BF16)
    w.wait(1)
    w.wait(2)
    w.wait(3)
    FF = wg.shape[1]
    for f in range(0, FF, 512):
        cols = slice(f, f + 512)
        gate = dot(n2, wg[:, cols])
        up = dot(n2, wu[:, cols])
        gate_out[:, cols] = gate.astype(BF16)
        up_out[:, cols] = up.astype(BF16)
        act[:, cols] = (gate * jax.nn.sigmoid(gate) * up).astype(BF16)
    y = h + dot(act[...], wd[...])
    if rounded:
        low = y.astype(BF16)
        low_out[...] = low
        y = low.astype(F32)
    y_out[...] = y
    if has_next:
        wn.wait(0)
        wn.wait(1)
        qkv_out(y, gn[0:1, :], wqkv, cos[...], sin[...], qcode[...], q_out, kv_out)


def backward_kernel(cfg, *refs):
    (R, G, pieces, dests, n_parts, n_sums, part_one, part_two, rounded) = cfg
    n_dests = 1 + max(d for d, _, _ in dests)
    RG = R // G
    M = GQ * RG
    it = iter(refs)
    take = lambda n: [next(it) for _ in range(n)]
    scal, masks, cos, sin = take(4)
    if part_one:
        sums = take(n_sums)
        hg_in, qg_in, x1 = take(3)
        mine_n, theirs_n = take(2), take(2)
    else:
        (g_in,) = take(1)
    if part_two:
        h, gate, up, att, qb, kcode, bias = take(7)
        parts = take(n_parts)
        mine, theirs = take(5), take(5)
    if part_one:
        kvg_out, normed_out, gain1_out = take(3)
        if rounded or not part_two:
            low_out = next(it)
    if part_two:
        hg_out, qg_out = take(2)
        dkv_out = take(n_dests)
        n2_out, gg_out, ug_out, act_out, dg_out, og_out, gain2_out = take(7)
    if part_one:
        wqkv, gn, sem_n = take(3)
    if part_two:
        kvs, dq_scr, dkv_scr, dos = take(4)
        wout, wg, wu, wd, gv = take(5)
        sem_kv, sem_w = take(2)

    if part_one:
        wn = Weights(mine_n, theirs_n, [wqkv, gn], sem_n, scal[1])
        wn.start()
    if part_two:
        w = Weights(mine, theirs, [wout, wg, wu, wd, gv], sem_w, scal[0])
        w.start()
        copies = copy_pieces(pieces, parts, kvs, sem_kv, scal, 2 + 2 * G)
        dkv_scr[...] = jnp.zeros_like(dkv_scr)

    if part_one:
        total = sums[0][...].astype(F32)
        for s in sums[1:]:
            total = total + s[...].astype(F32)
        u = total[:, :SLAB]
        u = u * cos[...] - swapped(u) * sin[...]
        kvg = jnp.concatenate([u.astype(BF16), total[:, SLAB:].astype(BF16)], axis=1)
        kvg_out[...] = kvg
        wn.wait(0)
        wn.wait(1)
        ng = dot_t(kvg, wqkv[:, GQ * SLAB :])
        for j in range(GQ):
            ng = ng + dot_t(qg_in[j], wqkv[:, j * SLAB : (j + 1) * SLAB])
        gain = gn[0:1, :]
        x = x1[...].astype(F32)
        r = lax.rsqrt(jnp.mean(x * x, axis=-1, keepdims=True) + EPS)
        xr = x * r
        normed_out[...] = (xr * gain).astype(BF16)
        gain1_out[...] = jnp.sum(ng * xr, axis=0, keepdims=True)
        scaled = ng * gain
        g = hg_in[...] + r * (scaled - xr * (r * jnp.mean(scaled * x, axis=-1, keepdims=True)))
        if rounded or not part_two:
            low = g.astype(BF16)
            low_out[...] = low
            g = low.astype(F32)
    else:
        g = g_in[...].astype(F32)
    if not part_two:
        return

    dg = g.astype(BF16)
    dg_out[...] = dg
    for i in range(1, 5):
        w.wait(i)
    FF = wg.shape[1]
    ng = jnp.zeros(g.shape, F32)
    for f in range(0, FF, 512):
        cols = slice(f, f + 512)
        ig = dot_t(dg, wd[cols, :])
        gt = gate[:, cols].astype(F32)
        ut = up[:, cols].astype(F32)
        s = jax.nn.sigmoid(gt)
        gs = gt * s
        act_out[:, cols] = (gs * ut).astype(BF16)
        gg = (ig * ut * (s + gs * (1.0 - s))).astype(BF16)
        ug = (ig * gs).astype(BF16)
        gg_out[:, cols] = gg
        ug_out[:, cols] = ug
        ng = ng + dot_t(gg, wg[:, cols]) + dot_t(ug, wu[:, cols])
    gain = gv[1:2, :]
    hh = h[...]
    r = lax.rsqrt(jnp.mean(hh * hh, axis=-1, keepdims=True) + EPS)
    xr = hh * r
    n2_out[...] = (xr * gain).astype(BF16)
    gain2_out[...] = jnp.sum(ng * xr, axis=0, keepdims=True)
    scaled = ng * gain
    hg = g + r * (scaled - xr * (r * jnp.mean(scaled * hh, axis=-1, keepdims=True)))
    hg_out[...] = hg
    og = hg.astype(BF16)
    og_out[...] = og
    w.wait(0)
    lane = lax.broadcasted_iota(jnp.int32, (1, 128), 1)
    for j in range(GQ):
        do = dot_t(og, wout[j * SLAB : (j + 1) * SLAB, :]).astype(BF16)
        prod = do.astype(F32) * att[j].astype(F32)
        code = jnp.zeros((R, 128), F32)
        for n in range(KV):
            delta = jnp.sum(prod * masks[3 + n : 4 + n, :].astype(F32), axis=1, keepdims=True)
            for i, part in enumerate(split_three(-delta)):
                code = code + jnp.where(lane == 3 * n + i, part, 0.0)
        dos[j] = jnp.concatenate([do[:, :128] + code.astype(BF16), do[:, 128:]], axis=1)
    for c in copies:
        c.wait()

    lane_all = lax.broadcasted_iota(jnp.int32, (1, SLAB), 1)
    for gi in range(G):
        rows = slice(gi * RG, (gi + 1) * RG)
        qg = jnp.concatenate([qb[j, rows, :] for j in range(GQ)], axis=0)
        dog = jnp.concatenate([dos[j, rows, :] for j in range(GQ)], axis=0)
        db = scal[2 + gi]
        lb = scal[2 + G + gi]

        def block(b, diagonal):
            at = pl.ds(pl.multiple_of(b * KB, KB), KB)
            k = kvs[at, 0:SLAB]
            v = kvs[at, 128 : 128 + SLAB]
            ds_all, k_all = [], []
            dk = jnp.zeros((KB, SLAB), F32)
            dv = jnp.zeros((KB, SLAB), F32)
            for n in range(KV):
                kn = k * masks[n : n + 1, :] + masks[6 + n : 7 + n, :]
                if not diagonal:
                    kn = kn + kcode[at, :]
                vn = v * masks[3 + n : 4 + n, :] + masks[9 + n : 10 + n, :]
                s = dot_t(qg, kn)
                if diagonal:
                    s = s + jnp.concatenate([bias[gi]] * GQ, axis=0)
                p = jnp.exp2(s)
                dp = dot_t(dog, vn)
                ds = (p * dp).astype(BF16)
                ds_all.append(ds)
                k_all.append(kn)
                dkn = dot(ds.T, qg)
                dvn = dot(p.astype(BF16).T, dog)
                dk = dk + jnp.where((lane_all // HD) == n, dkn, 0.0)
                dv = dv + jnp.where(((lane_all - VOFF) // HD == n) & (lane_all >= VOFF), dvn, 0.0)
            dq = dot(jnp.concatenate(ds_all, axis=1), jnp.concatenate(k_all, axis=0))
            if diagonal:
                dq_scr[...] = dq
            else:
                dq_scr[...] += dq
            dk = dk * LN2
            dkv_scr[at, 0:128] += dk[:, :128]
            dkv_scr[at, 128:256] += dk[:, 128:] + dv[:, :128]
            dkv_scr[at, 256:384] += dv[:, 128:]

        block(db, True)

        def body(b, _):
            block(b, False)
            return 0

        lax.fori_loop(lb, db, body, 0)
        for j in range(GQ):
            t = dq_scr[j * RG : (j + 1) * RG, :]
            t = jnp.where(lane_all < KVD, t, 0.0) * SCALE
            t = t * cos[rows, :] - swapped(t) * sin[rows, :]
            qg_out[j, rows, :] = t.astype(BF16)
    for i, (into, row, n_rows) in enumerate(dests):
        at = pl.multiple_of(scal[2 + 2 * G + i] * 32, 32)
        dkv_out[into][row : row + n_rows] = dkv_scr[pl.ds(at, n_rows), :].astype(BF16)


VM = lambda: pl.BlockSpec(memory_space=pltpu.VMEM)
SM = lambda: pl.BlockSpec(memory_space=pltpu.SMEM)
HB = lambda: pl.BlockSpec(memory_space=pl.ANY)
S = jax.ShapeDtypeStruct


def call(body, args, spaces, outs, scratch, flops, name):
    spec = {"v": VM, "s": SM, "h": HB}
    return pl.pallas_call(
        body,
        out_shape=outs,
        in_specs=[spec[c]() for c in spaces],
        out_specs=[VM() for _ in outs],
        scratch_shapes=scratch,
        compiler_params=pltpu.CompilerParams(vmem_limit_bytes=60 * 1024 * 1024),
        cost_estimate=pl.CostEstimate(flops=flops, bytes_accessed=12_000_000, transcendentals=0),
        name=name,
    )(*args)


def weight_scratch(D, FF):
    return [
        pltpu.VMEM((GQ * SLAB, D), BF16),
        pltpu.VMEM((D, FF), BF16),
        pltpu.VMEM((D, FF), BF16),
        pltpu.VMEM((FF, D), BF16),
        pltpu.VMEM((8, D), F32),
    ]


def qkv_scratch(D):
    return [pltpu.VMEM((D, GQ * SLAB + 2 * KVD), BF16), pltpu.VMEM((8, D), F32)]


def gate_up_kernel(scal, *refs):
    n2, gg, ug = refs[0:4], refs[4:8], refs[8:12]
    keep, give, left = refs[12:15]
    R = n2[0].shape[0]

    @pl.when(pl.program_id(0) == 0)
    def _():
        for i in range(4):
            left[:, i * R : (i + 1) * R] = n2[i][...].T

    a = dot(left[...], jnp.concatenate([t[...] for t in gg], axis=0))
    b = dot(left[...], jnp.concatenate([t[...] for t in ug], axis=0))
    zero = scal[0] == 0
    chunks, rows = keep.shape[0], keep.shape[1]
    k, g = jnp.where(zero, a, b), jnp.where(zero, b, a)
    for c in range(chunks):
        keep[c] = k[c * rows : (c + 1) * rows].astype(BF16)
        give[c] = g[c * rows : (c + 1) * rows].astype(BF16)


def down_kernel(scal, *refs):
    act, dg = refs[0:4], refs[4:8]
    keep, give = refs[8:10]
    left = jnp.concatenate([t[...].T for t in act], axis=1)
    w = dot(left, jnp.concatenate([t[...] for t in dg], axis=0))
    zero = scal[0] == 0
    chunks, rows = keep.shape[0], keep.shape[1]
    for c in range(chunks):
        a = w[2 * c * rows : (2 * c + 1) * rows]
        b = w[(2 * c + 1) * rows : (2 * c + 2) * rows]
        keep[c] = jnp.where(zero, a, b).astype(BF16)
        give[c] = jnp.where(zero, b, a).astype(BF16)


def attention_grads_kernel(scal, *refs):
    normed, qg, kvg, att, og = refs[0:4], refs[4:8], refs[8:12], refs[12:16], refs[16:20]
    keep, give, keep2, give2 = refs[20:24]
    left = jnp.concatenate([t[...].T for t in normed], axis=1)
    slabs = [dot(left, jnp.concatenate([t[j] for t in qg], axis=0)) for j in range(GQ)]
    q = jnp.concatenate(
        [slabs[j][:, n * HD : (n + 1) * HD] for n in range(KV) for j in range(GQ)], axis=1
    )
    kv = dot(left, jnp.concatenate([t[...] for t in kvg], axis=0))
    key, value = kv[:, :KVD], kv[:, KVD:]
    grads = jnp.concatenate([t[...] for t in og], axis=0)
    outs = []
    for j in range(GQ):
        left = jnp.concatenate([t[j].T for t in att], axis=1)
        outs.append(dot(left, grads))
    o = jnp.concatenate(
        [
            outs[j][VOFF + n * HD : VOFF + (n + 1) * HD]
            for n in range(KV)
            for j in range(GQ)
        ],
        axis=0,
    )
    zero = scal[0] == 0
    chunks, rows = keep.shape[0], keep.shape[1]
    for a, b, k_out, g_out in ((q, o, keep, give), (key, value, keep2, give2)):
        k, g = jnp.where(zero, a, b), jnp.where(zero, b, a)
        for c in range(chunks):
            k_out[c] = k[c * rows : (c + 1) * rows].astype(BF16)
            g_out[c] = g[c * rows : (c + 1) * rows].astype(BF16)


def grid_call(body, scal, args, in_specs, outs, out_specs, scratch, grid, flops, name):
    return pl.pallas_call(
        body,
        out_shape=outs,
        grid=grid,
        in_specs=[SM()] + in_specs,
        out_specs=out_specs,
        scratch_shapes=scratch,
        compiler_params=pltpu.CompilerParams(vmem_limit_bytes=60 * 1024 * 1024),
        cost_estimate=pl.CostEstimate(flops=flops, bytes_accessed=16_000_000, transcendentals=0),
        name=name,
    )(scal, *args)


def weight_grads(its, core, R, D, FF, chunks):
    scal = jnp.reshape(core, (1,)).astype(jnp.int32)
    get = lambda key: [t[key] for t in its]
    rows = D // chunks
    tile = 512
    whole = lambda shape: pl.BlockSpec(shape, lambda i: (0,) * len(shape))
    cols = lambda n, shape=None: pl.BlockSpec((R, n), lambda i: (0, i))
    out = pl.BlockSpec((chunks, rows, tile), lambda i: (0, 0, i))
    gu = grid_call(
        gate_up_kernel,
        scal,
        get("n2") + get("gg") + get("ug"),
        [whole((R, D))] * 4 + [cols(tile)] * 8,
        [S((chunks, rows, FF), BF16)] * 2,
        [out] * 2,
        [pltpu.VMEM((D, 4 * R), BF16)],
        (FF // tile,),
        16 * R * D * FF,
        "gate_up_grads",
    )
    down_rows = FF // chunks
    step = 4
    out = pl.BlockSpec((step, down_rows // 2, D), lambda i: (i, 0, 0))
    down = grid_call(
        down_kernel,
        scal,
        get("act") + get("dg"),
        [cols(step * down_rows)] * 4 + [whole((R, D))] * 4,
        [S((chunks, down_rows // 2, D), BF16)] * 2,
        [out] * 2,
        [],
        (chunks // step,),
        8 * R * D * FF,
        "down_grads",
    )
    attn = call(
        attention_grads_kernel,
        [scal, *get("normed"), *get("qg"), *get("kvg"), *get("att"), *get("og")],
        "s" + "v" * 20,
        [S((chunks, rows, D), BF16)] * 2 + [S((chunks, rows, KVD), BF16)] * 2,
        [],
        16 * R * D * D,
        "attention_grads",
    )
    return [tuple(gu), tuple(down), tuple(attn[:2]), tuple(attn[2:])]


class Device:
    def __init__(self, shard_len):
        self.n_seq = lax.axis_size("seq")
        self.n_dp = lax.axis_size("dp")
        self.shard_len = shard_len
        self.seq_total = shard_len * self.n_seq
        self.core = lax.axis_index("section")
        self.z = lax.axis_index("seq")
        self.R = shard_len // 2
        self.G = 1
        self.starts = [self.z * shard_len + self.core * self.R]

    def rows_in(self, tokens):
        return [lax.dynamic_slice_in_dim(t, self.core * self.R, self.R, 0) for t in tokens]

    def rows_out(self, low0, low1):
        give = jnp.where(self.core == 0, low1, low0)
        keep = jnp.where(self.core == 0, low0, low1)
        got = lax.ppermute(give, "section", [(0, 1), (1, 0)])
        first = jnp.where(self.core == 0, keep, got)
        second = jnp.where(self.core == 0, got, keep)
        return jnp.concatenate([first, second], axis=0)

    def documents(self, doc_lengths, pad_count):
        return doc_lengths, pad_count

    def kv_pieces(self):
        whole = ((0, 0, self.seq_total),)
        return whole, whole, [jnp.int32(0)]

    def gather(self, kv):
        return [lax.all_gather(kv, ("seq", "section"), axis=0, tiled=True)]

    def scatter(self, dkv):
        return [lax.psum_scatter(dkv[0], ("seq", "section"), scatter_dimension=0, tiled=True)]


SWAP = [(0, 1), (1, 0)]


class Squares(Device):
    def __init__(self, shard_len):
        super().__init__(shard_len)
        self.d = lax.axis_index("dp")
        self.x = self.d % 2
        self.near = self.z < 2
        self.half = shard_len // 4
        self.G = 2
        self.role = jnp.where(self.near, 2 * self.z + self.x, 2 * (3 - self.z) + 1 - self.x)
        self.starts = list(self.positions(self.role, self.core))
        self.crossing = self.near == (self.x == 1)

    def positions(self, role, core):
        block = 2 * self.half
        return role * block + core * self.half, (7 - role) * block + (1 - core) * self.half

    def along_x(self, t):
        return lax.ppermute(t, "dp", [(i, i ^ 1) for i in range(4)])

    def along_z(self, t):
        return lax.ppermute(t, "seq", [(i, i ^ 1) for i in range(4)])

    def diagonal(self, t):
        pairs = [(z * 4 + d, (z ^ 1) * 4 + (d ^ 1)) for z in range(4) for d in range(4)]
        return lax.ppermute(t, ("seq", "dp"), pairs)

    def mirrored(self, t):
        return lax.ppermute(t, "seq", [(i, 3 - i) for i in range(4)])

    def documents(self, doc_lengths, pad_count):
        both = jnp.concatenate([doc_lengths, pad_count[:, None]], axis=1)
        mine = jnp.where(self.x == self.z // 2, both, self.along_x(both))
        return mine[:, :-1], mine[:, -1]

    def rows_in(self, tokens):
        at = jnp.where(self.near, self.core, 1 - self.core) * self.half
        out = []
        for t in tokens:
            lower = lax.dynamic_slice_in_dim(t, at, self.half, 0)
            upper = lax.dynamic_slice_in_dim(t, at + 2 * self.half, self.half, 0)
            hopped = self.along_x(jnp.where(self.near, upper, lower))
            kept = jnp.where(self.near, lower, upper)
            moved = self.mirrored(jnp.where(self.crossing, kept, hopped))
            stay = jnp.where(self.crossing, hopped, kept)
            early = jnp.where(self.near, stay, moved)
            late = jnp.where(self.near, moved, stay)
            out.append(jnp.concatenate([early, late], axis=0))
        return out

    def rows_out(self, low0, low1):
        n = self.half
        give = jnp.where(self.core == 0, low1, low0)
        keep = jnp.where(self.core == 0, low0, low1)
        got = lax.ppermute(give, "section", SWAP)
        zero = jnp.where(self.core == 0, keep, got)
        one = jnp.where(self.core == 0, got, keep)
        early = jnp.concatenate([zero[:n], one[:n]], axis=0)
        late = jnp.concatenate([one[n:], zero[n:]], axis=0)
        stay = jnp.where(self.near, early, late)
        moved = self.mirrored(jnp.where(self.near, late, early))
        kept = jnp.where(self.crossing, moved, stay)
        hopped = self.along_x(jnp.where(self.crossing, stay, moved))
        lower = jnp.where(self.near, kept, hopped)
        upper = jnp.where(self.near, hopped, kept)
        return jnp.concatenate([lower, upper], axis=0)

    def kv_pieces(self):
        n = self.half
        pieces, dests, at = [], [], []
        for p in range(8):
            low, high = self.positions(self.role ^ (p % 4), self.core if p < 4 else 1 - self.core)
            pieces += [(p, 0, n), (p, n, n)]
            dests += [(p // 4, (p % 4) * 2 * n, n), (p // 4, (p % 4) * 2 * n + n, n)]
            at += [low // 32, high // 32]
        return tuple(pieces), tuple(dests), at

    def gather(self, kv):
        own = [kv, self.along_x(kv), self.along_z(kv), self.diagonal(kv)]
        return own + [lax.ppermute(t, "section", SWAP) for t in own]

    def scatter(self, dkv):
        keep, give = dkv
        n = 2 * self.half
        total = keep.astype(F32) + lax.ppermute(give, "section", SWAP).astype(F32)
        total = total.astype(BF16)
        part = [total[m * n : (m + 1) * n] for m in range(4)]
        return [part[0], self.along_x(part[1]), self.along_z(part[2]), self.diagonal(part[3])]

    def shares(self, keep, give):
        got = lax.ppermute(give, "section", SWAP)
        four = (4, 4) + keep.shape[1:]
        a, b = keep.reshape(four), got.reshape(four)
        pick = lambda t, at: lax.dynamic_index_in_dim(t, at, 1, keepdims=False).astype(F32)
        sums = [(pick(a, self.d ^ m) + pick(b, self.d ^ m)).astype(keep.dtype) for m in range(4)]
        got = [lax.ppermute(sums[m], "dp", [(i, i ^ m) for i in range(4)]) for m in range(1, 4)]
        total = sums[0].astype(F32) + sum(t.astype(F32) for t in got)
        low = total.astype(keep.dtype)
        pick = lambda at: lax.dynamic_index_in_dim(low, at, 0, keepdims=False)
        got = [
            lax.ppermute(pick(self.z ^ m), "seq", [(i, i ^ m) for i in range(4)])
            for m in range(1, 4)
        ]
        return pick(self.z).astype(F32) + sum(t.astype(F32) for t in got)


def make_context(dev, lengths, pad, cos, sin):
    R, G = dev.R, dev.G
    RG = R // G
    total = dev.seq_total
    pos = jnp.arange(total, dtype=jnp.int32)
    ends = jnp.cumsum(lengths)
    segment = jnp.sum((ends[None, :] <= pos[:, None]).astype(jnp.int32), axis=1)
    live = pos < total - pad
    lane = jnp.arange(SLAB, dtype=jnp.int32)[None, :]
    in_seg = (lane >= SEG0) & (lane < LIVE)
    kcode = jnp.where(
        in_seg & (lane - SEG0 != segment[:, None]), NEG, 0.0
    ) + jnp.where((lane == LIVE) & ~live[:, None], NEG, 0.0)
    rows = jnp.concatenate([s + jnp.arange(RG, dtype=jnp.int32) for s in dev.starts])
    row_seg = jnp.sum((ends[None, :] <= rows[:, None]).astype(jnp.int32), axis=1)
    qcode = jnp.where(in_seg & (lane - SEG0 == row_seg[:, None]) | (lane == LIVE), 1.0, 0.0)
    bias, dbs, lbs = [], [], []
    starts_all = jnp.concatenate([jnp.zeros((1,), jnp.int32), ends.astype(jnp.int32)])
    for g in range(G):
        first = dev.starts[g]
        db = first // KB
        ri = rows[g * RG : (g + 1) * RG]
        rs = row_seg[g * RG : (g + 1) * RG]
        kj = db * KB + jnp.arange(KB, dtype=jnp.int32)
        ks = jnp.sum((ends[None, :] <= kj[:, None]).astype(jnp.int32), axis=1)
        kl = kj < total - pad
        allowed = (kj[None, :] <= ri[:, None]) & (ks[None, :] == rs[:, None]) & kl[None, :]
        allowed = allowed | (kj[None, :] == ri[:, None])
        bias.append(jnp.where(allowed, 0.0, NEG))
        doc_start = jnp.max(jnp.where(starts_all <= first, starts_all, 0))
        dbs.append(db)
        lbs.append(doc_start // KB)
    return dict(
        kcode=kcode.astype(BF16),
        qcode=qcode.astype(BF16),
        bias=jnp.stack(bias).astype(F32),
        dbs=dbs,
        lbs=lbs,
    )


def per_device(
    tokens,
    cotangent,
    doc_lengths,
    pad_count,
    attn_gain,
    w_query,
    w_key,
    w_value,
    w_out,
    ffn_gain,
    w_gate,
    w_up,
    w_down,
):
    micro, shard_len, D = tokens.shape
    FF = w_gate.shape[-1]
    fast = (lax.axis_size("seq"), lax.axis_size("dp"), shard_len) == (4, 4, 512)
    dev = Squares(shard_len) if fast else Device(shard_len)
    R, G, total = dev.R, dev.G, dev.seq_total
    RG = R // G
    M = GQ * RG
    NB = total // KB
    core = dev.core

    wq = w_query[0].reshape(D, KV, GQ, HD).transpose(0, 2, 1, 3).reshape(D, GQ, KVD)
    wq = jnp.pad(wq, ((0, 0), (0, 0), (0, SLAB - KVD))).reshape(D, GQ * SLAB)
    wqkv_m = jnp.concatenate([wq, w_key[0], w_value[0]], axis=1)
    wo = w_out[0].reshape(KV, GQ, HD, D).transpose(1, 0, 2, 3).reshape(GQ, KVD, D)
    wout_m = jnp.pad(wo, ((0, 0), (VOFF, SLAB - KVD - VOFF), (0, 0))).reshape(GQ * SLAB, D)
    gains_m = jnp.concatenate([attn_gain, ffn_gain, jnp.ones((6, D), BF16)], axis=0).astype(F32)
    swap = lambda t: lax.ppermute(t, "section", [(0, 1), (1, 0)])
    mine = [wout_m, w_gate[0], w_up[0], w_down[0], gains_m]
    mine_n = [wqkv_m, gains_m]
    wqkv_t = swap(wqkv_m)
    gains_t = swap(gains_m)
    theirs_n = [wqkv_t, gains_t]
    theirs = [swap(wout_m), swap(w_gate[0]), swap(w_up[0]), swap(w_down[0]), gains_t]

    rows = jnp.concatenate([s + jnp.arange(RG, dtype=jnp.int32) for s in dev.starts])
    frequency = THETA ** (-2.0 * jnp.arange(HD // 2, dtype=F32) / HD)
    angles = rows.astype(F32)[:, None] * frequency[None, :]
    c32, s32 = jnp.cos(angles), jnp.sin(angles)
    one = jnp.ones((R, HD), F32)
    cos = jnp.concatenate([c32, c32] * KV + [one], axis=1)
    sin = jnp.concatenate([-s32, s32] * KV + [one * 0], axis=1)
    masks = jnp.asarray(masks_host(), BF16)
    doc_lengths, pad_count = dev.documents(doc_lengths, pad_count)
    contexts = [make_context(dev, doc_lengths[i], pad_count[i], cos, sin) for i in range(micro)]
    pieces, dests, piece_at = dev.kv_pieces()
    dest_rows = [0] * (1 + max(d for d, _, _ in dests))
    for d, row, n_rows in dests:
        dest_rows[d] = max(dest_rows[d], row + n_rows)
    n_pieces = len(pieces)

    def scalars(ctx, layer, layer_n):
        sel = lambda l: (core == l).astype(jnp.int32)
        return jnp.stack([sel(layer), sel(layer_n), *ctx["dbs"], *ctx["lbs"], *piece_at]).astype(
            jnp.int32
        )

    sds = lambda shape, kind: S(shape, kind)
    dense_flops = 2 * R * (D * D * 2 + D * KVD * 2 + 3 * D * FF)

    def first(x, ctx):
        return call(
            first_kernel,
            [scalars(ctx, 0, 0), x, cos, sin, ctx["qcode"], wqkv_m, wqkv_t, gains_m, gains_t],
            "svvvvhhhh",
            [sds((GQ, R, SLAB), BF16), sds((R, 2 * KVD), BF16)],
            qkv_scratch(D) + [pltpu.SemaphoreType.DMA((2,))],
            dense_flops // 5,
            "qkv_first",
        )

    def forward(x, q, kv_parts, ctx, layer, layer_n, rounded):
        has_next = layer_n is not None
        cfg = (R, G, pieces, len(kv_parts), has_next, rounded)
        args = [scalars(ctx, layer, layer_n if has_next else layer), x, q, ctx["kcode"]]
        args += [ctx["bias"], masks, cos, sin, ctx["qcode"], *kv_parts, *mine, *theirs]
        spaces = "s" + "v" * 8 + "h" * (len(kv_parts) + 10)
        outs = [
            sds((R, D), F32),
            sds((R, D), F32),
            sds((GQ, R, SLAB), BF16),
            sds((R, FF), BF16),
            sds((R, FF), BF16),
            sds((GQ, R, SLAB), BF16),
        ]
        scratch = [
            pltpu.VMEM((total, 2 * KVD), BF16),
            pltpu.VMEM((KV, NB, M, KB), F32),
            pltpu.VMEM((KV, M, 128), F32),
            pltpu.VMEM((KV, M, 128), F32),
            pltpu.VMEM((KV, M, SLAB), F32),
            pltpu.VMEM((R, FF), BF16),
        ] + weight_scratch(D, FF)
        sems = [pltpu.SemaphoreType.DMA((n_pieces,)), pltpu.SemaphoreType.DMA((5,))]
        if has_next:
            args += mine_n + theirs_n
            spaces += "hhhh"
            outs += [sds((GQ, R, SLAB), BF16), sds((R, 2 * KVD), BF16)]
            scratch += qkv_scratch(D)
            sems.append(pltpu.SemaphoreType.DMA((2,)))
        if rounded:
            outs.append(sds((R, D), BF16))
        return call(
            functools.partial(forward_kernel, cfg),
            args,
            spaces,
            outs,
            scratch + sems,
            dense_flops * 2,
            "forward",
        )

    def backward(ctx, one, two, layer_n, layer, rounded=False):
        args = [scalars(ctx, layer if two else layer_n, layer_n if "sums" in one else layer), masks, cos, sin]
        spaces = "svvv"
        outs, scratch = [], []
        n_sums = 0
        if "sums" in one:
            n_sums = len(one["sums"])
            args += [*one["sums"], one["hg"], one["qg"], one["x"], *mine_n, *theirs_n]
            spaces += "v" * (n_sums + 3) + "hhhh"
            outs += [sds((R, 2 * KVD), BF16), sds((R, D), BF16), sds((1, D), F32)]
            if rounded or two is None:
                outs.append(sds((R, D), BF16))
            scratch += qkv_scratch(D) + [pltpu.SemaphoreType.DMA((2,))]
        else:
            args += [one["g"]]
            spaces += "v"
        n_parts = 0
        if two is not None:
            n_parts = len(two["parts"])
            args += [two["h"], two["gate"], two["up"], two["att"], two["qb"], ctx["kcode"]]
            args += [ctx["bias"], *two["parts"], *mine, *theirs]
            spaces += "v" * 7 + "h" * (n_parts + 10)
            outs += [
                sds((R, D), F32),
                sds((GQ, R, SLAB), BF16),
                *[sds((n, 2 * KVD), BF16) for n in dest_rows],
                sds((R, D), BF16),
                sds((R, FF), BF16),
                sds((R, FF), BF16),
                sds((R, FF), BF16),
                sds((R, D), BF16),
                sds((R, D), BF16),
                sds((1, D), F32),
            ]
            scratch += [
                pltpu.VMEM((total, 2 * KVD), BF16),
                pltpu.VMEM((M, SLAB), F32),
                pltpu.VMEM((total, 2 * KVD), F32),
                pltpu.VMEM((GQ, R, SLAB), BF16),
            ] + weight_scratch(D, FF)
            scratch += [pltpu.SemaphoreType.DMA((n_pieces,)), pltpu.SemaphoreType.DMA((5,))]
        cfg = (R, G, pieces, dests, n_parts, n_sums, "sums" in one, two is not None, rounded)
        res = call(
            functools.partial(backward_kernel, cfg),
            args,
            spaces,
            outs,
            scratch,
            dense_flops * 4,
            "backward",
        )
        it = iter(res)
        out = {}
        if "sums" in one:
            out["kvg"], out["normed"], out["gain1"] = next(it), next(it), next(it)
            if rounded or two is None:
                out["low"] = next(it)
        if two is not None:
            out["hg"], out["qg"] = next(it), next(it)
            out["dkv"] = [next(it) for _ in dest_rows]
            for key in ("n2", "gg", "ug", "act", "dg", "og", "gain2"):
                out[key] = next(it)
        return out

    xs = dev.rows_in(tokens)
    cots = dev.rows_in(cotangent)
    state = [[None] * 4 for _ in range(micro)]
    lows = [None] * micro
    tops = [None] * micro
    qkv = [first(xs[i], contexts[i]) for i in range(micro)]
    kv_parts = [dev.gather(qkv[i][1]) for i in range(micro)]
    cur = list(xs)
    for app in range(4):
        layer = app // 2
        nxt = None if app == 3 else (app + 1) // 2
        rounded = app in (1, 3)
        for i in range(micro):
            res = forward(cur[i], qkv[i][0], kv_parts[i], contexts[i], layer, nxt, rounded)
            y, h, att, gate, up, qb = res[:6]
            state[i][app] = dict(
                x=cur[i], h=h, att=att, gate=gate, up=up, qb=qb, parts=kv_parts[i]
            )
            if rounded:
                (lows if app == 1 else tops)[i] = res[-1]
            cur[i] = y
            if nxt is not None:
                qkv[i] = (res[6], res[7])
                kv_parts[i] = dev.gather(res[7])
    layer_out = jnp.stack([dev.rows_out(lows[i], tops[i]) for i in range(micro)])[None]

    items = [[{} for _ in range(4)] for _ in range(micro)]
    bound = [None] * micro
    last = [None] * micro
    pend = [dict(g=cots[i]) for i in range(micro)]
    for app in (3, 2, 1, 0, -1):
        for i in range(micro):
            two = state[i][app] if app >= 0 else None
            layer_n = (app + 1) // 2 if app < 3 else None
            rounded = app == 1
            res = backward(contexts[i], pend[i], two, layer_n, app // 2 if app >= 0 else None, rounded)
            if app < 3:
                items[i][app + 1].update({k: res[k] for k in ("kvg", "normed", "gain1")})
                if rounded:
                    bound[i] = res["low"]
                if app < 0:
                    last[i] = res["low"]
            if app >= 0:
                items[i][app].update(
                    {k: res[k] for k in ("qg", "n2", "gg", "ug", "act", "dg", "og", "gain2")}
                )
                items[i][app]["att"] = two["att"]
                pend[i] = dict(
                    sums=dev.scatter(res["dkv"]), hg=res["hg"], qg=res["qg"], x=two["x"]
                )
    input_grad = jnp.stack([dev.rows_out(last[i], bound[i]) for i in range(micro)])[None]

    layers = [
        [items[i][a] for a in (2 * layer, 2 * layer + 1) for i in range(micro)]
        for layer in range(2)
    ]
    gains = jnp.stack(
        [
            jnp.concatenate([sum(t["gain1"][0] for t in its), sum(t["gain2"][0] for t in its)])
            for its in layers
        ]
    )
    if fast:
        outs = fast_sums(dev, layers, gains, R, D, FF)
    else:
        outs = plain_sums(layers, gains, R, D)
    return (layer_out, input_grad, *[t.reshape(1, -1) for t in outs])


def fast_sums(dev, layers, gains, R, D, FF):
    core = dev.core
    first = core == 0
    pairs = [weight_grads(its, core, R, D, FF, 16) for its in layers]
    done = [[dev.shares(*pair) for pair in pairs[layer]] for layer in range(2)]
    outs = []
    for zero, one in zip(*done):
        mine = jnp.where(first, zero, one)
        other = lax.ppermute(jnp.where(first, one, zero), "section", SWAP)
        outs.append((jnp.where(first, mine, other), jnp.where(first, other, mine)))
    (gate, up), (down_a, down_b), (query, out), (key, value) = outs
    down = jnp.concatenate([down_a, down_b], axis=0)
    parts = gains.reshape(2, 16, 1, -1)
    gain = dev.shares(jnp.where(first, parts[0], parts[1]), jnp.where(first, parts[1], parts[0]))
    return [gain, query, key, value, out, gate, up, down]


def plain_sums(layers, gains, R, D):
    def inner(pairs):
        left = jnp.concatenate([a for a, _ in pairs], axis=0)
        right = jnp.concatenate([b for _, b in pairs], axis=0)
        return lax.dot_general(left, right, (((0,), (0,)), ((), ())), preferred_element_type=F32)

    flat = []
    wide = lambda t: t.transpose(1, 0, 2).reshape(R, GQ * SLAB)
    for layer in range(2):
        its = layers[layer]
        gq = inner([(t["normed"], wide(t["qg"])) for t in its])
        gq = gq.reshape(D, GQ, SLAB)[:, :, :KVD].reshape(D, GQ, KV, HD).transpose(0, 2, 1, 3)
        gkv = inner([(t["normed"], t["kvg"]) for t in its])
        go = inner([(wide(t["att"]), t["og"]) for t in its])
        go = go.reshape(GQ, SLAB, D)[:, VOFF:, :].reshape(GQ, KV, HD, D).transpose(1, 0, 2, 3)
        gg = inner([(t["n2"], t["gg"]) for t in its])
        gu = inner([(t["n2"], t["ug"]) for t in its])
        gd = inner([(t["act"], t["dg"]) for t in its])
        flat.append(
            [gains[layer]]
            + [t.reshape(-1).astype(BF16) for t in (gq, gkv[:, :KVD], gkv[:, KVD:], go, gg, gu, gd)]
        )
    outs = []
    for a, b in zip(*flat):
        both = lax.psum_scatter(jnp.stack([a, b]), "section", scatter_dimension=0, tiled=True)
        own = lax.psum_scatter(both.reshape(-1), ("seq", "dp"), scatter_dimension=0, tiled=True)
        outs.append(own.astype(F32))
    return outs


def solution(mesh):
    placed = (
        P("dp", "seq", None),
        P("dp", "seq", None),
        P("dp", None),
        P("dp"),
        P("section", None),
        P("section", None, None),
        P("section", None, None),
        P("section", None, None),
        P("section", None, None),
        P("section", None),
        P("section", None, None),
        P("section", None, None),
        P("section", None, None),
    )
    return jax.shard_map(
        per_device,
        mesh=mesh,
        in_specs=placed,
        out_specs=(
            P("section", "dp", "seq", None),
            P("section", "dp", "seq", None),
        )
        + (P("section", ("seq", "dp")),) * 8,
        check_vma=False,
    )
```

time: 2160 us -> 875 us (0.41)
  matrix products: 925 us -> 0 us
  Pallas kernels: 0 us -> 382 us
  waiting for transfers between devices: 438 us -> 118 us
  other arithmetic: 377 us -> 64.4 us
  blocking collectives: 262 us -> 0 us
  starting transfers between devices: 7.6 us -> 199 us
  local copies, waits for them, and re-layouts: 106 us -> 81 us
    dot_general x133 -> x0, matrix products: 925 us -> none  [the longest x6 189 us: block_backward(): jnp.einsum('qngd,knd->ngqk', grouped_grad, values_all.reshape(-1, KV, HD)...]
    pallas_call x0 -> x26, Pallas kernels: none -> 382 us  [the longest x22 352 us: call(): pl.pallas_call(body, out_shape=outs, in_specs=[spec[c]() for c in spaces]...]
    unnamed x14 -> x0, waiting for transfers between devices: 347 us -> none
    all_gather x12 -> x0, blocking collectives: 219 us -> none  [the longest x6 114 us: fetch_first(): lax.all_gather(values_own, 'seq', axis=0, tiled=True)]
    ppermute x4 -> x182, starting transfers between devices: 6.44 us -> 199 us  [the longest x27 57.2 us: shares(): lax.ppermute(pick(self.z ^ m), 'seq', [(i, i ^ m) for i in range(4)])]
    convert_element_type x20 -> x31, other arithmetic: 195 us -> 27.4 us  [the longest x12 7.6 us: shares(): (pick(a, self.d ^ m) + pick(b, self.d ^ m)).astype(keep.dtype)]
    ppermute x4 -> x182, waiting for transfers between devices: 1.58 us -> 118 us  [the longest x25 33.8 us: along_x(): return lax.ppermute(t, 'dp', [(i, i ^ 1) for i in range(4)])]
    reduce_sum x13 -> x2, other arithmetic: 104 us -> 0.79 us  [the longest x1 0.68 us: make_context(): jnp.sum((ends[None, :] <= rows[:, None]).astype(jnp.int32), axis=1)]
  transfers between devices with their start and end apart: 17 -> 182, of which waited for: 8 -> 42; matrix products, arithmetic and copies ran while one was open for 19% -> 15% of each run, Pallas kernels for 0% -> 45%
where the time goes in v1:
time: 875 us; the launch traced here: 859 us
  Pallas kernels  382 us (44%)
  starting transfers between devices  199 us (23%)
  waiting for transfers between devices  118 us (13%)
  local copies, waits for them, and re-layouts  81 us (9%)
  other arithmetic  64.4 us (7%)
  between operations  14.6 us (2%)
    pallas_call x22, Pallas kernels, call(): pl.pallas_call(body, out_shape=outs, in_specs=[spec[c]() for c in spaces]...  352 us
    ppermute x27, starting transfers between devices, shares(): lax.ppermute(pick(self.z ^ m), 'seq', [(i, i ^ m) for i in range(4)])  57.2 us
    ppermute x25, waiting for transfers between devices, along_x(): return lax.ppermute(t, 'dp', [(i, i ^ 1) for i in range(4)])  33.8 us
    ppermute x27, starting transfers between devices, shares(): lax.ppermute(sums[m], 'dp', [(i, i ^ m) for i in range(4)])  32.7 us
    ppermute x16, starting transfers between devices, diagonal(): return lax.ppermute(t, ('seq', 'dp'), pairs)  30.3 us
    pallas_call x4, Pallas kernels, grid_call(): pl.pallas_call(body, out_shape=outs, grid=grid, in_specs=[SM()] + in_spec...  30.2 us
    ppermute x25, starting transfers between devices, along_x(): return lax.ppermute(t, 'dp', [(i, i ^ 1) for i in range(4)])  27.2 us
    ppermute x27, waiting for transfers between devices, shares(): lax.ppermute(sums[m], 'dp', [(i, i ^ m) for i in range(4)])  24.3 us
  transfers between devices with their start and end apart: 182, of which 42 were waited for; matrix products, arithmetic and copies ran while one was open for 15% of the time, Pallas kernels for 45%

profile of v1, /device:TPU:0, one launch (start us, length us, event | category | flops | bytes accessed | tf_op | source)
XLA Modules:
  0.0 859.0 jit_solution(8767425656330965234)
XLA Ops:
  108.5 14.2 %forward.8 = (f32[256,576]{1,0:T(8,128)}, f32[256,576]{1,0:T(8,128)}, bf16[3,256,256]{2,1,0:T(8,128)(2,1)}, bf16[256,1536]{1,0:T(8,128)(2,1)}, bf16[256,1536]{1,...) custom-call(s32[22]{0:T(128)} %stack.108.scal.refs_0_, ...), custom_call_target="tpu_custom_call" | custom-call | flops 3623878656 | bytes 12000000 | tf_op jit(solution)/shard_map/forward/pallas_call | solution.py:442
  125.6 18.0 %forward.12 = (f32[256,576]{1,0:T(8,128)}, f32[256,576]{1,0:T(8,128)}, bf16[3,256,256]{2,1,0:T(8,128)(2,1)}, bf16[256,1536]{1,0:T(8,128)(2,1)}, bf16[256,1536]{1...) custom-call(s32[22]{0:T(128)} %stack.115.scal.refs_0_, ...), custom_call_target="tpu_custom_call" | custom-call | flops 3623878656 | bytes 12000000 | tf_op jit(solution)/shard_map/forward/pallas_call | solution.py:442
  162.3 18.1 %forward.13 = (f32[256,576]{1,0:T(8,128)}, f32[256,576]{1,0:T(8,128)}, bf16[3,256,256]{2,1,0:T(8,128)(2,1)}, bf16[256,1536]{1,0:T(8,128)(2,1)}, bf16[256,1536]{1...) custom-call(s32[22]{0:T(128)} %stack.114.refs_0_, ...), custom_call_target="tpu_custom_call" | custom-call | flops 3623878656 | bytes 12000000 | tf_op jit(solution)/shard_map/forward/pallas_call | solution.py:442
  186.2 14.8 %forward.9 = (f32[256,576]{1,0:T(8,128)}, f32[256,576]{1,0:T(8,128)}, bf16[3,256,256]{2,1,0:T(8,128)(2,1)}, bf16[256,1536]{1,0:T(8,128)(2,1)}, bf16[256,1536]{1,...) custom-call(s32[22]{0:T(128)} %stack.107.refs_0_, ...), custom_call_target="tpu_custom_call" | custom-call | flops 3623878656 | bytes 12000000 | tf_op jit(solution)/shard_map/forward/pallas_call | solution.py:442
  218.5 17.9 %forward.14 = (f32[256,576]{1,0:T(8,128)}, f32[256,576]{1,0:T(8,128)}, bf16[3,256,256]{2,1,0:T(8,128)(2,1)}, bf16[256,1536]{1,0:T(8,128)(2,1)}, bf16[256,1536]{1...) custom-call(s32[22]{0:T(128)} %stack.113.refs_0_, ...), custom_call_target="tpu_custom_call" | custom-call | flops 3623878656 | bytes 12000000 | tf_op jit(solution)/shard_map/forward/pallas_call | solution.py:442
  240.5 14.2 %forward.10 = (f32[256,576]{1,0:T(8,128)}, f32[256,576]{1,0:T(8,128)}, bf16[3,256,256]{2,1,0:T(8,128)(2,1)}, bf16[256,1536]{1,0:T(8,128)(2,1)}, bf16[256,1536]{1...) custom-call(s32[22]{0:T(128)} %stack.104.refs_0_, ...), custom_call_target="tpu_custom_call" | custom-call | flops 3623878656 | bytes 12000000 | tf_op jit(solution)/shard_map/forward/pallas_call | solution.py:442
  269.3 16.7 %forward.15 = (f32[256,576]{1,0:T(8,128)}, f32[256,576]{1,0:T(8,128)}, bf16[3,256,256]{2,1,0:T(8,128)(2,1)}, bf16[256,1536]{1,0:T(8,128)(2,1)}, bf16[256,1536]{1...) custom-call(s32[22]{0:T(128)} %stack.113.refs_0_, ...), custom_call_target="tpu_custom_call" | custom-call | flops 3623878656 | bytes 12000000 | tf_op jit(solution)/shard_map/forward/pallas_call | solution.py:442
  287.2 27.1 %backward.15 = (f32[256,576]{1,0:T(8,128)}, bf16[3,256,256]{2,1,0:T(8,128)(2,1)}, bf16[1024,384]{1,0:T(8,128)(2,1)}, bf16[1024,384]{1,0:T(8,128)(2,1)}, bf16[256...) custom-call(s32[22]{0:T(128)} %stack.113.refs_0_, ...), custom_call_target="tpu_custom_call" | custom-call | flops 7247757312 | bytes 12000000 | tf_op jit(solution)/shard_map/backward/pallas_call | solution.py:442
  315.6 12.7 %forward.11 = (f32[256,576]{1,0:T(8,128)}, f32[256,576]{1,0:T(8,128)}, bf16[3,256,256]{2,1,0:T(8,128)(2,1)}, bf16[256,1536]{1,0:T(8,128)(2,1)}, bf16[256,1536]{1...) custom-call(s32[22]{0:T(128)} %stack.104.refs_0_, ...), custom_call_target="tpu_custom_call" | custom-call | flops 3623878656 | bytes 12000000 | tf_op jit(solution)/shard_map/forward/pallas_call | solution.py:442
  336.4 18.2 %backward.10 = (f32[256,576]{1,0:T(8,128)}, bf16[3,256,256]{2,1,0:T(8,128)(2,1)}, bf16[1024,384]{1,0:T(8,128)(2,1)}, bf16[1024,384]{1,0:T(8,128)(2,1)}, bf16[256...) custom-call(s32[22]{0:T(128)} %stack.104.refs_0_, ...), custom_call_target="tpu_custom_call" | custom-call | flops 7247757312 | bytes 12000000 | tf_op jit(solution)/shard_map/backward/pallas_call | solution.py:442
  370.8 11.5 %collective-permute-done.39 = bf16[256,576]{1,0:T(8,128)(2,1)S(1)} collective-permute-done((bf16[256,576]{1,0:T(8,128)(2,1)S(1)}, bf16[256,576]{1,0:T(8,128)(2,1)S(1)}, u32[]{:S(2)}, u32[]{:S(2)}) %collective-permute-start.39) | collective-permute-done | bytes 294944 | tf_op jit(solution)/shard_map/ppermute | solution.py:652
  387.0 28.9 %backward.16 = (bf16[256,384]{1,0:T(8,128)(2,1)}, bf16[256,576]{1,0:T(8,128)(2,1)}, f32[1,576]{1,0:T(1,128)}, f32[256,576]{1,0:T(8,128)}, bf16[3,256,256]{2,1,0:...) custom-call(s32[22]{0:T(128)} %stack.113.refs_0_, ...), custom_call_target="tpu_custom_call" | custom-call | flops 7247757312 | bytes 12000000 | tf_op jit(solution)/shard_map/backward/pallas_call | solution.py:442
  416.8 20.2 %backward.11 = (bf16[256,384]{1,0:T(8,128)(2,1)}, bf16[256,576]{1,0:T(8,128)(2,1)}, f32[1,576]{1,0:T(1,128)}, f32[256,576]{1,0:T(8,128)}, bf16[3,256,256]{2,1,0:...) custom-call(s32[22]{0:T(128)} %stack.104.refs_0_, ...), custom_call_target="tpu_custom_call" | custom-call | flops 7247757312 | bytes 12000000 | tf_op jit(solution)/shard_map/backward/pallas_call | solution.py:442
  444.7 8.6 %gate_up_grads.3 = (bf16[16,36,1536]{2,1,0:T(8,128)(2,1)}, bf16[16,36,1536]{2,1,0:T(8,128)(2,1)}) custom-call(s32[1]{0:T(128)} %bitcast.69.scal, bf16[256,576]{1,0:T(8,128)(2,1)} %get-tuple-element.372.refs_0_, bf16[256,576]{1,0:T(8,128)(2,1)} %get-tuple-element.373.refs_1_, bf16[256,576]{1,0:T(8,128)(2,1)} %get-tuple-element.374.refs_2_, ...), custom_call_target="tpu_custom_call" | custom-call | flops 3623878656 | bytes 16000000 | tf_op jit(solution)/shard_map/gate_up_grads/pallas_call | solution.py:535
  474.3 29.2 %backward.17 = (bf16[256,384]{1,0:T(8,128)(2,1)}, bf16[256,576]{1,0:T(8,128)(2,1)}, f32[1,576]{1,0:T(1,128)}, bf16[256,576]{1,0:T(8,128)(2,1)}, f32[256,576]{1,0...) custom-call(s32[22]{0:T(128)} %stack.114.refs_0_, ...), custom_call_target="tpu_custom_call" | custom-call | flops 7247757312 | bytes 12000000 | tf_op jit(solution)/shard_map/backward/pallas_call | solution.py:442
  506.3 20.6 %backward.12 = (bf16[256,384]{1,0:T(8,128)(2,1)}, bf16[256,576]{1,0:T(8,128)(2,1)}, f32[1,576]{1,0:T(1,128)}, bf16[256,576]{1,0:T(8,128)(2,1)}, f32[256,576]{1,0...) custom-call(s32[22]{0:T(128)} %stack.107.refs_0_, ...), custom_call_target="tpu_custom_call" | custom-call | flops 7247757312 | bytes 12000000 | tf_op jit(solution)/shard_map/backward/pallas_call | solution.py:442
  527.7 7.3 attention_grads.3
  583.5 29.1 %backward.18 = (bf16[256,384]{1,0:T(8,128)(2,1)}, bf16[256,576]{1,0:T(8,128)(2,1)}, f32[1,576]{1,0:T(1,128)}, f32[256,576]{1,0:T(8,128)}, bf16[3,256,256]{2,1,0:...) custom-call(s32[22]{0:T(128)} %stack.115.scal.refs_0_, ...), custom_call_target="tpu_custom_call" | custom-call | flops 7247757312 | bytes 12000000 | tf_op jit(solution)/shard_map/backward/pallas_call | solution.py:442
  615.5 19.8 %backward.13 = (bf16[256,384]{1,0:T(8,128)(2,1)}, bf16[256,576]{1,0:T(8,128)(2,1)}, f32[1,576]{1,0:T(1,128)}, f32[256,576]{1,0:T(8,128)}, bf16[3,256,256]{2,1,0:...) custom-call(s32[22]{0:T(128)} %stack.108.scal.refs_0_, ...), custom_call_target="tpu_custom_call" | custom-call | flops 7247757312 | bytes 12000000 | tf_op jit(solution)/shard_map/backward/pallas_call | solution.py:442
  641.8 8.8 %gate_up_grads.2 = (bf16[16,36,1536]{2,1,0:T(8,128)(2,1)}, bf16[16,36,1536]{2,1,0:T(8,128)(2,1)}) custom-call(s32[1]{0:T(128)} %bitcast.69.scal, bf16[256,576]{1,0:T(8,128)(2,1)} %get-tuple-element.358.refs_0_, bf16[256,576]{1,0:T(8,128)(2,1)} %get-tuple-element.359.refs_1_, bf16[256,576]{1,0:T(8,128)(2,1)} %get-tuple-element.360.refs_2_, ...), custom_call_target="tpu_custom_call" | custom-call | flops 3623878656 | bytes 16000000 | tf_op jit(solution)/shard_map/gate_up_grads/pallas_call | solution.py:535
  667.3 9.1 %collective-permute-start.180 = (bf16[48,576]{1,0:T(8,128)(2,1)S(1)}, bf16[48,576]{1,0:T(8,128)(2,1)}, u32[]{:S(2)}, u32[]{:S(2)}) collective-permute-start(bf16[48,576]{1,0:T(8,128)(2,1)S(1)} %copy-done.118), channel_id=1, source_target_pairs={{0,12},{4,8},{8,4},{12,0},{1,13},{5,9},{9,5},{13,1},{2,14},{6,10},... | collective-permute-start | bytes 165896 | tf_op jit(solution)/shard_map/ppermute | solution.py:734
  700.6 7.2 attention_grads.2
  793.2 13.7 %collective-permute-start.134 = (bf16[36,576]{1,0:T(8,128)(2,1)S(1)}, bf16[36,576]{1,0:T(8,128)(2,1)S(1)}, u32[]{:S(2)}, u32[]{:S(2)}) collective-permute-start(bf16[36,576]{1,0:T(8,128)(2,1)S(1)} %copy-done.119), channel_id=1, source_target_pairs={{0,8},{4,12},{8,0},{12,4},{1,9},{5,13},{9,1},{13,5},{2,10},{6,14},... | collective-permute-start | bytes 124424 | tf_op jit(solution)/shard_map/ppermute | solution.py:734
  828.3 7.9 collective-permute-done.153
  (929 shorter events, 450.6 us)
Async XLA Ops:
  9.1 58.3 %collective-permute-start.12 = (bf16[768,576]{0,1:T(8,128)(2,1)}, bf16[768,576]{0,1:T(8,128)(2,1)}, u32[]{:S(2)}, u32[]{:S(2)}) collective-permute-start(bf16[768,576]{0,1:T(8,128)(2,1)} %copy.412), channel_id=1, source_target_pairs={{0,16},{16,0},{1,17},{17,1},{2,18},{18,2},{3,19},{19,3},{4,20},{20... | collective-permute-start | bytes 2654216 | tf_op jit(solution)/shard_map/ppermute | solution.py:812
  12.0 43.1 %collective-permute-start.1 = (bf16[128,576]{1,0:T(8,128)(2,1)}, bf16[128,576]{1,0:T(8,128)(2,1)}, u32[]{:S(2)}, u32[]{:S(2)}) collective-permute-start(bf16[128,576]{1,0:T(8,128)(2,1)} %select_bitcast_fusion.5), channel_id=1, source_target_pairs={{0,1},{1,0},{2,3},{3,2},{4,5},{5,4},{6,7},{7,6},{8,9},{9,8},{10,11... | collective-permute-start | bytes 442376 | tf_op jit(solution)/shard_map/ppermute | solution.py:652
  42.4 55.4 %collective-permute-start.15 = (bf16[1536,576]{0,1:T(8,128)(2,1)}, bf16[1536,576]{0,1:T(8,128)(2,1)}, u32[]{:S(2)}, u32[]{:S(2)}) collective-permute-start(bf16[1536,576]{0,1:T(8,128)(2,1)} %bitcast.483), channel_id=1, source_target_pairs={{0,16},{16,0},{1,17},{17,1},{2,18},{18,2},{3,19},{19,3},{4,20},{20... | collective-permute-start | bytes 5308424 | tf_op jit(solution)/shard_map/ppermute | solution.py:812
  55.1 52.8 %collective-permute-start.13 = (bf16[576,1536]{1,0:T(8,128)(2,1)S(1)}, bf16[576,1536]{1,0:T(8,128)(2,1)}, u32[]{:S(2)}, u32[]{:S(2)}) collective-permute-start(bf16[576,1536]{1,0:T(8,128)(2,1)S(1)} %bitcast.439), channel_id=1, source_target_pairs={{0,16},{16,0},{1,17},{17,1},{2,18},{18,2},{3,19},{19,3},{4,20},{20... | collective-permute-start | bytes 5308424 | tf_op jit(solution)/shard_map/ppermute | solution.py:812
  55.4 52.6 %collective-permute-start.14 = (bf16[576,1536]{1,0:T(8,128)(2,1)S(1)}, bf16[576,1536]{1,0:T(8,128)(2,1)}, u32[]{:S(2)}, u32[]{:S(2)}) collective-permute-start(bf16[576,1536]{1,0:T(8,128)(2,1)S(1)} %bitcast.456), channel_id=1, source_target_pairs={{0,16},{16,0},{1,17},{17,1},{2,18},{18,2},{3,19},{19,3},{4,20},{20... | collective-permute-start | bytes 5308424 | tf_op jit(solution)/shard_map/ppermute | solution.py:812
  105.9 40.7 %collective-permute-start.94 = (bf16[128,576]{1,0:T(8,128)(2,1)}, bf16[128,576]{1,0:T(8,128)(2,1)}, u32[]{:S(2)}, u32[]{:S(2)}) collective-permute-start(bf16[128,576]{1,0:T(8,128)(2,1)} %select_bitcast_fusion.2), channel_id=1, source_target_pairs={{0,1},{1,0},{2,3},{3,2},{4,5},{5,4},{6,7},{7,6},{8,9},{9,8},{10,11... | collective-permute-start | bytes 442376 | tf_op jit(solution)/shard_map/ppermute | solution.py:652
  160.9 40.1 %collective-permute-start.73 = (bf16[128,576]{1,0:T(8,128)(2,1)}, bf16[128,576]{1,0:T(8,128)(2,1)S(1)}, u32[]{:S(2)}, u32[]{:S(2)}) collective-permute-start(bf16[128,576]{1,0:T(8,128)(2,1)} %select_bitcast_fusion.3), channel_id=1, source_target_pairs={{0,1},{1,0},{2,3},{3,2},{4,5},{5,4},{6,7},{7,6},{8,9},{9,8},{10,11... | collective-permute-start | bytes 442376 | tf_op jit(solution)/shard_map/ppermute | solution.py:652
  267.6 46.7 %collective-permute-start.33 = (bf16[256,384]{1,0:T(8,128)(2,1)S(1)}, bf16[256,384]{1,0:T(8,128)(2,1)S(1)}, u32[]{:S(2)}, u32[]{:S(2)}) collective-permute-start(bf16[256,384]{1,0:T(8,128)(2,1)S(1)} %copy-done.99), channel_id=1, source_target_pairs={{0,16},{16,0},{1,17},{17,1},{2,18},{18,2},{3,19},{19,3},{4,20},{20... | collective-permute-start | bytes 589832 | tf_op jit(solution)/shard_map/ppermute | solution.py:713
  267.8 47.0 %collective-permute-start.36 = (bf16[256,384]{1,0:T(8,128)(2,1)S(1)}, bf16[256,384]{1,0:T(8,128)(2,1)S(1)}, u32[]{:S(2)}, u32[]{:S(2)}) collective-permute-start(bf16[256,384]{1,0:T(8,128)(2,1)S(1)} %collective-permute-done.32.refs_12_.refs_15_), channel_id=1, source_target_pairs={{0,16},{16,0},{1,17},{17,1},{2,18},{18,2},{3,19},{19,3},{4,20},{20... | collective-permute-start | bytes 589832 | tf_op jit(solution)/shard_map/ppermute | solution.py:713
  268.2 46.7 %collective-permute-start.35 = (bf16[256,384]{1,0:T(8,128)(2,1)S(1)}, bf16[256,384]{1,0:T(8,128)(2,1)S(1)}, u32[]{:S(2)}, u32[]{:S(2)}) collective-permute-start(bf16[256,384]{1,0:T(8,128)(2,1)S(1)} %collective-permute-done.31.refs_11_.refs_14_), channel_id=1, source_target_pairs={{0,16},{16,0},{1,17},{17,1},{2,18},{18,2},{3,19},{19,3},{4,20},{20... | collective-permute-start | bytes 589832 | tf_op jit(solution)/shard_map/ppermute | solution.py:713
  268.3 46.5 %collective-permute-start.34 = (bf16[256,384]{1,0:T(8,128)(2,1)S(1)}, bf16[256,384]{1,0:T(8,128)(2,1)S(1)}, u32[]{:S(2)}, u32[]{:S(2)}) collective-permute-start(bf16[256,384]{1,0:T(8,128)(2,1)S(1)} %collective-permute-done.30.refs_10_.refs_13_), channel_id=1, source_target_pairs={{0,16},{16,0},{1,17},{17,1},{2,18},{18,2},{3,19},{19,3},{4,20},{20... | collective-permute-start | bytes 589832 | tf_op jit(solution)/shard_map/ppermute | solution.py:713
  287.1 42.3 %collective-permute-start.70 = (bf16[256,576]{1,0:T(8,128)(2,1)S(1)}, bf16[256,576]{1,0:T(8,128)(2,1)S(1)}, u32[]{:S(2)}, u32[]{:S(2)}) collective-permute-start(bf16[256,576]{1,0:T(8,128)(2,1)S(1)} %broadcast_select_fusion.11), channel_id=1, source_target_pairs={{0,16},{16,0},{1,17},{17,1},{2,18},{18,2},{3,19},{19,3},{4,20},{20... | collective-permute-start | bytes 884744 | tf_op jit(solution)/shard_map/ppermute | solution.py:688
  314.3 44.2 %collective-permute-start.96 = (bf16[1024,384]{1,0:T(8,128)(2,1)}, bf16[1024,384]{1,0:T(8,128)(2,1)S(1)}, u32[]{:S(2)}, u32[]{:S(2)}) collective-permute-start(bf16[1024,384]{1,0:T(8,128)(2,1)} %get-tuple-element.278), channel_id=1, source_target_pairs={{0,16},{16,0},{1,17},{17,1},{2,18},{18,2},{3,19},{19,3},{4,20},{20... | collective-permute-start | bytes 2359304 | tf_op jit(solution)/shard_map/ppermute | solution.py:718
  370.5 45.4 %collective-permute-start.78 = (bf16[256,384]{1,0:T(8,128)(2,1)S(1)}, bf16[256,384]{1,0:T(8,128)(2,1)S(1)}, u32[]{:S(2)}, u32[]{:S(2)}) collective-permute-start(bf16[256,384]{1,0:T(8,128)(2,1)S(1)} %get-tuple-element.539), channel_id=1, source_target_pairs={{0,5},{1,4},{2,7},{3,6},{4,1},{5,0},{6,3},{7,2},{8,13},{9,12},{10,... | collective-permute-start | bytes 589832 | tf_op jit(solution)/shard_map/ppermute | solution.py:659
  415.8 40.1 %collective-permute-start.100 = (bf16[1024,384]{1,0:T(8,128)(2,1)}, bf16[1024,384]{1,0:T(8,128)(2,1)S(1)}, u32[]{:S(2)}, u32[]{:S(2)}) collective-permute-start(bf16[1024,384]{1,0:T(8,128)(2,1)} %get-tuple-element.287), channel_id=1, source_target_pairs={{0,16},{16,0},{1,17},{17,1},{2,18},{18,2},{3,19},{19,3},{4,20},{20... | collective-permute-start | bytes 2359304 | tf_op jit(solution)/shard_map/ppermute | solution.py:718
  455.5 98.9 %collective-permute-start.159 = (bf16[16,36,1536]{2,0,1:T(8,128)(2,1)S(1)}, bf16[16,36,1536]{2,0,1:T(8,128)(2,1)}, u32[]{:S(2)}, u32[]{:S(2)}) collective-permute-start(bf16[16,36,1536]{2,0,1:T(8,128)(2,1)S(1)} %copy.496), channel_id=1, source_target_pairs={{0,16},{16,0},{1,17},{17,1},{2,18},{18,2},{3,19},{19,3},{4,20},{20... | collective-permute-start | bytes 5308424 | tf_op jit(solution)/shard_map/ppermute | solution.py:724
  473.5 62.8 %collective-permute-start.177 = (bf16[4,48,576]{2,1,0:T(8,128)(2,1)}, bf16[4,48,576]{2,1,0:T(8,128)(2,1)}, u32[]{:S(2)}, u32[]{:S(2)}) collective-permute-start(bf16[4,48,576]{2,1,0:T(8,128)(2,1)} %fusion.21), channel_id=1, source_target_pairs={{0,3},{1,2},{2,1},{3,0},{4,7},{5,6},{6,5},{7,4},{8,11},{9,10},{10,... | collective-permute-start | bytes 663560 | tf_op jit(solution)/shard_map/ppermute | solution.py:729
  546.1 186.1 %collective-permute-start.178 = (bf16[48,576]{1,0:T(8,128)(2,1)}, bf16[48,576]{1,0:T(8,128)(2,1)}, u32[]{:S(2)}, u32[]{:S(2)}) collective-permute-start(bf16[48,576]{1,0:T(8,128)(2,1)} %get-tuple-element.616), channel_id=1, source_target_pairs={{0,4},{4,0},{8,12},{12,8},{1,5},{5,1},{9,13},{13,9},{2,6},{6,2},{1... | collective-permute-start | bytes 165896 | tf_op jit(solution)/shard_map/ppermute | solution.py:734
  582.2 71.9 %collective-permute-start.162 = (bf16[4,36,1536]{2,1,0:T(8,128)(2,1)}, bf16[4,36,1536]{2,1,0:T(8,128)(2,1)S(1)}, u32[]{:S(2)}, u32[]{:S(2)}) collective-permute-start(bf16[4,36,1536]{2,1,0:T(8,128)(2,1)} %fusion.9), channel_id=1, source_target_pairs={{0,3},{1,2},{2,1},{3,0},{4,7},{5,6},{6,5},{7,4},{8,11},{9,10},{10,... | collective-permute-start | bytes 1327112 | tf_op jit(solution)/shard_map/ppermute | solution.py:729
  613.4 41.3 %collective-permute-start.160 = (bf16[4,36,1536]{2,1,0:T(8,128)(2,1)S(1)}, bf16[4,36,1536]{2,1,0:T(8,128)(2,1)S(1)}, u32[]{:S(2)}, u32[]{:S(2)}) collective-permute-start(bf16[4,36,1536]{2,1,0:T(8,128)(2,1)S(1)} %get-tuple-element.489), channel_id=1, source_target_pairs={{0,1},{1,0},{2,3},{3,2},{4,5},{5,4},{6,7},{7,6},{8,9},{9,8},{10,11... | collective-permute-start | bytes 1327112 | tf_op jit(solution)/shard_map/ppermute | solution.py:729
  614.1 41.4 %collective-permute-start.161 = (bf16[4,36,1536]{2,1,0:T(8,128)(2,1)S(1)}, bf16[4,36,1536]{2,1,0:T(8,128)(2,1)}, u32[]{:S(2)}, u32[]{:S(2)}) collective-permute-start(bf16[4,36,1536]{2,1,0:T(8,128)(2,1)S(1)} %get-tuple-element.490), channel_id=1, source_target_pairs={{0,2},{1,3},{2,0},{3,1},{4,6},{5,7},{6,4},{7,5},{8,10},{9,11},{10,... | collective-permute-start | bytes 1327112 | tf_op jit(solution)/shard_map/ppermute | solution.py:729
  615.5 42.5 %collective-permute-start.108 = (bf16[1024,384]{1,0:T(8,128)(2,1)}, bf16[1024,384]{1,0:T(8,128)(2,1)}, u32[]{:S(2)}, u32[]{:S(2)}) collective-permute-start(bf16[1024,384]{1,0:T(8,128)(2,1)} %get-tuple-element.306), channel_id=1, source_target_pairs={{0,16},{16,0},{1,17},{17,1},{2,18},{18,2},{3,19},{19,3},{4,20},{20... | collective-permute-start | bytes 2359304 | tf_op jit(solution)/shard_map/ppermute | solution.py:718
  667.3 68.5 %collective-permute-start.180 = (bf16[48,576]{1,0:T(8,128)(2,1)S(1)}, bf16[48,576]{1,0:T(8,128)(2,1)}, u32[]{:S(2)}, u32[]{:S(2)}) collective-permute-start(bf16[48,576]{1,0:T(8,128)(2,1)S(1)} %copy-done.118), channel_id=1, source_target_pairs={{0,12},{4,8},{8,4},{12,0},{1,13},{5,9},{9,5},{13,1},{2,14},{6,10},... | collective-permute-start | bytes 165896 | tf_op jit(solution)/shard_map/ppermute | solution.py:734
  753.5 56.2 %collective-permute-start.133 = (bf16[36,576]{1,0:T(8,128)(2,1)}, bf16[36,576]{1,0:T(8,128)(2,1)}, u32[]{:S(2)}, u32[]{:S(2)}) collective-permute-start(bf16[36,576]{1,0:T(8,128)(2,1)} %get-tuple-element.622), channel_id=1, source_target_pairs={{0,4},{4,0},{8,12},{12,8},{1,5},{5,1},{9,13},{13,9},{2,6},{6,2},{1... | collective-permute-start | bytes 124424 | tf_op jit(solution)/shard_map/ppermute | solution.py:734
  (335 other events, 3879.0 us)

commit v2 on v1

v2 whole, which is shorter than its diff:
```python
import functools

import jax
import jax.numpy as jnp
from jax import lax
from jax.experimental import pallas as pl
from jax.experimental.pallas import tpu as pltpu
from jax.sharding import PartitionSpec as P

H = 9
KV = 3
HD = 64
GQ = H // KV
EPS = 1e-05
THETA = 10000.0
NEG = -1e30
LOG2E = 1.4426950408889634
LN2 = 0.6931471805599453
SCALE = HD**-0.5
KB = 256
SLAB = 256
KVD = KV * HD
SEG0 = KVD
LIVE = SEG0 + 9
LSE0 = SEG0 + 10
DOCS = 8
VOFF = 64
F32 = jnp.float32
BF16 = jnp.bfloat16


def dot(a, b):
    return jnp.dot(a, b, preferred_element_type=F32)


def dot_t(a, b):
    return lax.dot_general(a, b, (((1,), (1,)), ((), ())), preferred_element_type=F32)


def head_lanes(n, offset=0):
    lane = lax.broadcasted_iota(jnp.int32, (1, SLAB), 1) - offset
    return jnp.where((lane >= n * HD) & (lane < (n + 1) * HD), 1.0, 0.0).astype(BF16)


def three_lanes(at, width):
    lane = lax.broadcasted_iota(jnp.int32, (1, width), 1)
    return jnp.where((lane >= at) & (lane < at + 3), 1.0, 0.0).astype(BF16)


def swapped(t):
    lane = lax.broadcasted_iota(jnp.int32, (t.shape[0], 128), 1)
    first = (lane % HD) < HD // 2
    parts = []
    for at in range(0, t.shape[1], 128):
        u = t[:, at : at + 128]
        parts.append(
            jnp.where(first, pltpu.roll(u, 128 - HD // 2, 1), pltpu.roll(u, HD // 2, 1))
        )
    return jnp.concatenate(parts, axis=1)


def split_three(v):
    hi = v.astype(BF16).astype(F32)
    rest = v - hi
    mid = rest.astype(BF16).astype(F32)
    return hi, mid, rest - mid


class Copies:
    def __init__(self, sem):
        self.sem = sem
        self.used = 0
        self.open = []

    def start(self, src, dst):
        c = pltpu.make_async_copy(src, dst, self.sem.at[self.used])
        self.used += 1
        c.start()
        return c

    def load(self, src, dst):
        c = self.start(src, dst)

        def ready():
            c.wait()
            return dst

        return ready

    def load_either(self, flag, mine, theirs, dst):
        sem = self.sem.at[self.used]
        self.used += 1

        @pl.when(flag)
        def _():
            pltpu.make_async_copy(mine, dst, sem).start()

        @pl.when(jnp.logical_not(flag))
        def _():
            pltpu.make_async_copy(theirs, dst, sem).start()

        def ready():
            pltpu.make_async_copy(mine, dst, sem).wait()
            return dst

        return ready

    def store(self, src, dst):
        self.open.append(self.start(src, dst))

    def finish(self):
        for c in self.open:
            c.wait()


def doc_start(docs, first):
    end, start = jnp.int32(0), jnp.int32(0)
    for k in range(DOCS):
        end = end + docs(k)
        start = jnp.where(end <= first, end, start)
    return start


def load_keys(io, pieces, refs, into, offsets):
    ready = []
    for (part, row, rows), at in zip(pieces, offsets):
        at = pl.multiple_of(at, rows if rows in (128, 2048) else 16)
        ready.append(io.load(refs[part].at[pl.ds(row, rows)], into.at[pl.ds(at, rows)]))
    return ready


def qkv_out(y, gain, wqkv, cos, sin, q_out, kv_out):
    r = lax.rsqrt(jnp.mean(y * y, axis=-1, keepdims=True) + EPS)
    normed = (y * r * gain).astype(BF16)
    for j in range(GQ):
        t = dot(normed, wqkv[:, j * SLAB : (j + 1) * SLAB])
        t = (t * cos + swapped(t) * sin) * (SCALE * LOG2E)
        q_out[j] = t.astype(BF16)
    t = dot(normed, wqkv[:, GQ * SLAB :])
    u = t[:, :SLAB]
    u = u * cos + swapped(u) * sin
    kv_out[:, :SLAB] = u.astype(BF16)
    kv_out[:, SLAB:] = t[:, SLAB:].astype(BF16)


def load_rows(io, parts, near, into, scratch):
    if len(parts) == 1:
        ready = io.load(parts[0], into)
        return lambda: ready()[...]
    stay, moved = parts
    early = io.load_either(near, stay, moved, scratch[0])
    late = io.load_either(near, moved, stay, scratch[1])
    return lambda: jnp.concatenate([early()[...].T, late()[...].T], axis=0)


def first_kernel(dev, n_x, scal, *refs):
    it = iter(refs)
    take = lambda n: [next(it) for _ in range(n)]
    xs = take(n_x)
    cos, sin, wm, wt, gm, gt, x_out, q_out, kv_out = take(9)
    x_v, cos_v, sin_v, wv, gv, q_v, kv_v = take(7)
    turned = take(n_x) if n_x > 1 else None
    (sem,) = take(1)
    place = dev.place(scal)
    io = Copies(sem)
    x = load_rows(io, xs, place["near"], x_v, turned)
    gain = io.load_either(place["core"] == 0, gm, gt, gv)
    w = io.load_either(place["core"] == 0, wm, wt, wv)
    cos, sin = io.load(cos, cos_v), io.load(sin, sin_v)
    x = x()
    x_v[...] = x
    io.store(x_v, x_out)
    gain = gain()[0:1, :]
    qkv_out(x.astype(F32), gain, w(), cos()[...], sin()[...], q_v, kv_v)
    io.store(kv_v, kv_out)
    io.store(q_v, q_out)
    io.finish()


def setup_kernel(dev, micro, total, R, G, scal, own, hopped, kcode, qcode, bias):
    place = dev.place(scal)
    RG = R // G
    for i in range(micro):
        docs = lambda k: jnp.where(place["own"], own[i, k], hopped[i, k])
        pad = docs(DOCS)

        def segment(pos):
            end, seg = jnp.int32(0), jnp.zeros(pos.shape, jnp.int32)
            for k in range(DOCS):
                end = end + docs(k)
                seg = seg + jnp.where(pos >= end, 1, 0)
            return seg

        def tile(shape, first, axis):
            return lax.broadcasted_iota(jnp.int32, shape, axis) + first

        shape = (total, 128)
        lane = tile(shape, 128, 1)
        pos = tile(shape, 0, 0)
        in_seg = (lane >= SEG0) & (lane < LIVE)
        wrong = in_seg & (lane - SEG0 != segment(pos))
        dead = (lane == LIVE) & (pos >= total - pad)
        kcode[i] = jnp.where(wrong | dead, NEG, 0.0).astype(BF16)
        for g in range(G):
            first = place["starts"][g]
            shape = (RG, 128)
            lane = tile(shape, 128, 1)
            right = (lane >= SEG0) & (lane < LIVE) & (lane - SEG0 == segment(tile(shape, first, 0)))
            qcode[i, g * RG : (g + 1) * RG] = jnp.where(
                right | (lane == LIVE), 1.0, 0.0
            ).astype(BF16)
            shape = (RG, KB)
            row = tile(shape, first, 0)
            col = tile(shape, (first // KB) * KB, 1)
            good = (col < row) & (segment(row) == segment(col)) & (col < total - pad)
            bias[i, g] = jnp.where(good | (col == row), 0.0, NEG)


def pack_kernel(turned, wq, wk, wv, wo, ga, gf, wqkv, wout, gains):
    zero = jnp.zeros((wq.shape[0], SLAB - KVD), BF16)
    cols = []
    for j in range(GQ):
        for n in range(KV):
            h = n * GQ + j
            cols.append(wq[:, h * HD : (h + 1) * HD])
        cols.append(zero)
    for w in (wk, wv):
        cols.append(w[...].T if turned else w[...])
    wqkv[...] = jnp.concatenate(cols, axis=1)
    for j in range(GQ):
        wout[j * SLAB : j * SLAB + VOFF, :] = jnp.zeros((VOFF, wout.shape[1]), BF16)
        for n in range(KV):
            h = n * GQ + j
            at = j * SLAB + VOFF + n * HD
            wout[at : at + HD, :] = wo[h * HD : (h + 1) * HD, :]
    gains[...] = jnp.concatenate(
        [ga[...].astype(F32), gf[...].astype(F32), jnp.zeros((6, ga.shape[1]), F32)], axis=0
    )


def keys_of(kvs, b):
    return kvs[pl.ds(pl.multiple_of(b * KB, KB), KB), 0:SLAB]


def values_of(kvs, b):
    return kvs[pl.ds(pl.multiple_of(b * KB, KB), KB), 128 : 128 + SLAB]


def in_pairs(low, high, body):
    pairs = (high - low) // 2

    def step(i, carry):
        body(low + 2 * i, 2)
        return carry

    lax.fori_loop(0, pairs, step, 0)

    @pl.when(high - low > 2 * pairs)
    def _():
        body(high - 1, 1)


def forward_kernel(dev, cfg, *refs):
    (i_seq, layer, layer_n, R, G, pieces, n_parts, has_next, rounded) = cfg
    RG = R // G
    M = GQ * RG
    it = iter(refs)
    take = lambda n: [next(it) for _ in range(n)]
    scal, own, hopped, x, q, kcode, bias, cos, sin, qcode = take(10)
    parts = take(n_parts)
    mine, theirs = take(5), take(5)
    if has_next:
        mine_n, theirs_n = take(2), take(2)
    y_out, h_out, att_out, gate_out, up_out, qb_out = take(6)
    if has_next:
        q_out, kv_out = take(2)
    if rounded:
        low_out = next(it)
    x_v, q_v, kc_v, bias_v, qc_v, y_v, h_v, att_v, gate_v, up_v, qb_v = take(11)
    kvs, s_scr, m_scr, l_scr, acc, act = take(6)
    w_v = take(5)
    if has_next:
        cos_v, sin_v, wqkv_v, gn_v, q2_v, kv2_v = take(6)
    if rounded:
        (low_v,) = take(1)
    (sem,) = take(1)
    place = dev.place(scal)
    docs = lambda k: jnp.where(place["own"], own[i_seq, k], hopped[i_seq, k])
    io = Copies(sem)
    q, qcode = io.load(q, q_v), io.load(qcode.at[i_seq], qc_v)
    bias = io.load(bias.at[i_seq], bias_v)
    kv_ready = load_keys(io, pieces, parts, kvs, place["rows"])
    kcode = io.load(kcode.at[i_seq], kc_v)
    x = io.load(x, x_v)
    here = place["core"] == layer
    wout, wg, wu, wd, gains = [io.load_either(here, *t) for t in zip(mine, theirs, w_v)]
    if has_next:
        cos, sin = io.load(cos, cos_v), io.load(sin, sin_v)
        there = place["core"] == layer_n
        wqkv, gain_n = [
            io.load_either(there, *t) for t in zip(mine_n, theirs_n, (wqkv_v, gn_v))
        ]

    halves = lambda t: functools.reduce(
        jnp.maximum, [t[:, i : i + 128] for i in range(0, t.shape[1], 128)]
    )
    key_lanes = [head_lanes(n) for n in range(KV)]
    value_lanes = [head_lanes(n, VOFF) for n in range(KV)]
    lane = lax.broadcasted_iota(jnp.int32, (1, 128), 1) + 128
    q, bias, qcode = q(), bias(), qcode()
    for ready in kv_ready:
        ready()
    kcode = kcode()
    for g in range(G):
        rows = slice(g * RG, (g + 1) * RG)
        qg = jnp.concatenate([q[j, rows, :] for j in range(GQ)], axis=0)
        code = jnp.concatenate([qcode[rows, :]] * GQ, axis=0)
        qg = jnp.concatenate([qg[:, :128], qg[:, 128:] + code], axis=1)
        db = place["starts"][g] // KB
        lb = doc_start(docs, place["starts"][g]) // KB

        k_d = keys_of(kvs, db)
        tile_bias = jnp.concatenate([bias[g]] * GQ, axis=0)
        for n in range(KV):
            s = dot_t(qg, k_d * key_lanes[n]) + tile_bias
            s_scr[n, db] = s
            m_scr[n] = halves(s)

        def first_pass(b, count):
            tops = [None] * KV
            for c in range(count):
                k = keys_of(kvs, b + c)
                code = kcode[pl.ds(pl.multiple_of((b + c) * KB, KB), KB), :]
                for n in range(KV):
                    kn = k * key_lanes[n]
                    kn = jnp.concatenate([kn[:, :128], kn[:, 128:] + code], axis=1)
                    s = dot_t(qg, kn)
                    s_scr[n, b + c] = s
                    top = halves(s)
                    tops[n] = top if c == 0 else jnp.maximum(tops[n], top)
            for n in range(KV):
                m_scr[n] = jnp.maximum(m_scr[n], tops[n])

        in_pairs(lb, db, first_pass)
        for n in range(KV):
            m = jnp.max(m_scr[n], axis=1, keepdims=True)
            m_scr[n] = jnp.broadcast_to(m, (M, 128))
        l_scr[...] = jnp.zeros_like(l_scr)
        acc[...] = jnp.zeros_like(acc)

        def second_pass(b, count):
            values = [values_of(kvs, b + c) for c in range(count)]
            for n in range(KV):
                m = m_scr[n]
                ps, l = [], l_scr[n]
                for c in range(count):
                    s = s_scr[n, b + c]
                    for half in (s[:, :128], s[:, 128:]):
                        p = jnp.exp2(half - m)
                        l = l + p
                        ps.append(p.astype(BF16))
                l_scr[n] = l
                vn = jnp.concatenate([v * value_lanes[n] for v in values], axis=0)
                acc[n] += dot(jnp.concatenate(ps, axis=1), vn)

        in_pairs(lb, db + 1, second_pass)
        out = jnp.zeros((M, SLAB), F32)
        code = jnp.zeros((M, 128), F32)
        for n in range(KV):
            l = jnp.sum(l_scr[n], axis=1, keepdims=True)
            out = out + acc[n] * (1.0 / l)
            lse = m_scr[n][:, :1] + jnp.log2(l)
            for i, part in enumerate(split_three(-lse)):
                code = code + jnp.where(lane == LSE0 + 3 * n + i, part, 0.0)
        out = out.astype(BF16)
        qb = jnp.concatenate([qg[:, :128], qg[:, 128:] + code.astype(BF16)], axis=1)
        for j in range(GQ):
            att_v[j, rows, :] = out[j * RG : (j + 1) * RG]
            qb_v[j, rows, :] = qb[j * RG : (j + 1) * RG]

    io.store(att_v, att_out)
    io.store(qb_v, qb_out)
    h = x()[...].astype(F32)
    wout = wout()
    h = h + dot(
        jnp.concatenate([att_v[j] for j in range(GQ)], axis=1),
        wout[...],
    )
    h_v[...] = h
    io.store(h_v, h_out)
    r2 = lax.rsqrt(jnp.mean(h * h, axis=-1, keepdims=True) + EPS)
    wg, wu, wd, gains = wg(), wu(), wd(), gains()
    n2 = (h * r2 * gains[1:2, :]).astype(BF16)
    FF = wg.shape[1]
    for f in range(0, FF, 512):
        cols = slice(f, f + 512)
        gate = dot(n2, wg[:, cols])
        up = dot(n2, wu[:, cols])
        gate_v[:, cols] = gate.astype(BF16)
        up_v[:, cols] = up.astype(BF16)
        act[:, cols] = (gate * jax.nn.sigmoid(gate) * up).astype(BF16)
    io.store(gate_v, gate_out)
    io.store(up_v, up_out)
    y = h + dot_t(act[...], wd[...])
    if rounded:
        low = y.astype(BF16)
        low_v[...] = low.T if dev.turned else low
        io.store(low_v, low_out)
        y = low.astype(F32)
    if has_next:
        y_v[...] = y
        io.store(y_v, y_out)
        qkv_out(y, gain_n()[0:1, :], wqkv(), cos()[...], sin()[...], q2_v, kv2_v)
        io.store(kv2_v, kv_out)
        io.store(q2_v, q_out)
    io.finish()


def backward_kernel(dev, cfg, *refs):
    (i_seq, layer, layer_n, R, G, pieces, dests, n_parts, n_sums, n_g, part_one, ffn, attn, rounded) = cfg
    n_dests = 1 + max(d for d, _, _ in dests)
    RG = R // G
    M = GQ * RG
    it = iter(refs)
    take = lambda n: [next(it) for _ in range(n)]
    scal, own, hopped, cos, sin = take(5)
    if part_one:
        sums = take(n_sums)
        hg_in, qg_in, x1 = take(3)
        mine_n, theirs_n = take(2), take(2)
    elif ffn:
        g_in = take(n_g)
    if ffn:
        h, gate, up, att = take(4)
        mine, theirs = take(5), take(5)
    if attn:
        qb, kcode, bias = take(3)
        parts = take(n_parts)
        if not ffn:
            (dos_in,) = take(1)
    if part_one:
        kvg_out, normed_out, gain1_out = take(3)
        if rounded or not ffn:
            low_out = next(it)
    if ffn:
        hg_out, n2_out, gg_out, ug_out, act_out, dg_out, og_out, gain2_out = take(8)
        if not attn:
            (dos_out,) = take(1)
    if attn:
        (qg_out,) = take(1)
        dkv_out = take(n_dests)
    cos_v, sin_v = take(2)
    if part_one:
        sums_v = take(n_sums)
        hgi_v, qgi_v, x1_v, wqkv_v, gn_v, kvg_v, normed_v, gain1_v = take(8)
        if rounded or not ffn:
            (low_v,) = take(1)
    elif ffn:
        g_v = take(n_g)
    if ffn:
        h_v, gate_v, up_v, att_v = take(4)
        hg_v, n2_v, gg_v, ug_v, act_v, dg_v, og_v, gain2_v = take(8)
        w_v = take(5)
    if ffn or attn:
        (dos,) = take(1)
    if attn:
        qb_v, kc_v, bias_v, qg_v = take(4)
        dkv_v = take(n_dests)
        kvs, dq_scr, dkv_scr = take(3)
    (sem,) = take(1)
    place = dev.place(scal)
    docs = lambda k: jnp.where(place["own"], own[i_seq, k], hopped[i_seq, k])
    io = Copies(sem)
    if part_one:
        sums = [io.load(*t) for t in zip(sums, sums_v)]
    cos, sin = io.load(cos, cos_v), io.load(sin, sin_v)
    if part_one:
        wqkv, gain_n = [
            io.load_either(place["core"] == layer_n, *t)
            for t in zip(mine_n, theirs_n, (wqkv_v, gn_v))
        ]
        qg_in, x1, hg_in = io.load(qg_in, qgi_v), io.load(x1, x1_v), io.load(hg_in, hgi_v)
    elif ffn:
        g_in = load_rows(io, g_in, place["near"], g_v[0], g_v)
    if ffn:
        here = place["core"] == layer
        wd = io.load_either(here, mine[3], theirs[3], w_v[3])
        gate, up = io.load(gate, gate_v), io.load(up, up_v)
        wout, wg, wu, gains = [
            io.load_either(here, mine[t], theirs[t], w_v[t]) for t in (0, 1, 2, 4)
        ]
        h, att = io.load(h, h_v), io.load(att, att_v)
    if attn:
        if not ffn:
            dos_ready = io.load(dos_in, dos)
        qb = io.load(qb, qb_v)
        bias = io.load(bias.at[i_seq], bias_v)
        kv_ready = load_keys(io, pieces, parts, kvs, place["rows"])
        kcode = io.load(kcode.at[i_seq], kc_v)
        dkv_scr[...] = jnp.zeros_like(dkv_scr)

    key_lanes = [head_lanes(n) for n in range(KV)]
    value_lanes = [head_lanes(n, VOFF) for n in range(KV)]
    total_lanes = [three_lanes(LSE0 - 128 + 3 * n, 128) for n in range(KV)]
    delta_lanes = [three_lanes(3 * n, SLAB) for n in range(KV)]
    cos, sin = cos()[...], sin()[...]
    if part_one:
        total = sums[0]()[...].astype(F32)
        for s in sums[1:]:
            total = total + s()[...].astype(F32)
        u = total[:, :SLAB]
        u = u * cos - swapped(u) * sin
        kvg = jnp.concatenate([u.astype(BF16), total[:, SLAB:].astype(BF16)], axis=1)
        kvg_v[...] = kvg
        io.store(kvg_v, kvg_out)
        wqkv, gain, qg_in = wqkv(), gain_n()[0:1, :], qg_in()
        ng = dot_t(
            jnp.concatenate([qg_in[j] for j in range(GQ)] + [kvg], axis=1), wqkv[...]
        )
        x = x1()[...].astype(F32)
        r = lax.rsqrt(jnp.mean(x * x, axis=-1, keepdims=True) + EPS)
        xr = x * r
        normed_v[...] = (xr * gain).astype(BF16)
        io.store(normed_v, normed_out)
        gain1_v[...] = jnp.broadcast_to(jnp.sum(ng * xr, axis=0, keepdims=True), gain1_v.shape)
        io.store(gain1_v, gain1_out)
        scaled = ng * gain
        g = hg_in()[...] + r * (
            scaled - xr * (r * jnp.mean(scaled * x, axis=-1, keepdims=True))
        )
        if rounded or not ffn:
            low = g.astype(BF16)
            low_v[...] = low.T if dev.turned else low
            io.store(low_v, low_out)
            g = low.astype(F32)
    elif ffn:
        g = g_in().astype(F32)
    def feed_forward_back():
        dg = g.astype(BF16)
        dg_v[...] = dg
        io.store(dg_v, dg_out)
        wd_r, wg_r, wu_r = wd(), wg(), wu()
        gate_r, up_r = gate(), up()
        FF = wg_r.shape[1]
        for f in range(0, FF, 512):
            cols = slice(f, f + 512)
            ig = dot(dg, wd_r[:, cols])
            gt = gate_r[:, cols].astype(F32)
            ut = up_r[:, cols].astype(F32)
            s = jax.nn.sigmoid(gt)
            gs = gt * s
            act_v[:, cols] = (gs * ut).astype(BF16)
            gg_v[:, cols] = (ig * ut * (s + gs * (1.0 - s))).astype(BF16)
            ug_v[:, cols] = (ig * gs).astype(BF16)
        io.store(act_v, act_out)
        io.store(gg_v, gg_out)
        io.store(ug_v, ug_out)
        ng = dot_t(gg_v[...], wg_r[...]) + dot_t(ug_v[...], wu_r[...])
        gain = gains()[1:2, :]
        hh = h()[...]
        r = lax.rsqrt(jnp.mean(hh * hh, axis=-1, keepdims=True) + EPS)
        xr = hh * r
        n2_v[...] = (xr * gain).astype(BF16)
        io.store(n2_v, n2_out)
        gain2_v[...] = jnp.broadcast_to(jnp.sum(ng * xr, axis=0, keepdims=True), gain2_v.shape)
        io.store(gain2_v, gain2_out)
        scaled = ng * gain
        hg = g + r * (scaled - xr * (r * jnp.mean(scaled * hh, axis=-1, keepdims=True)))
        hg_v[...] = hg
        io.store(hg_v, hg_out)
        og = hg.astype(BF16)
        og_v[...] = og
        io.store(og_v, og_out)
        wout_r, att_r = wout(), att()
        lane = lax.broadcasted_iota(jnp.int32, (1, 128), 1)
        for j in range(GQ):
            do = dot_t(og, wout_r[j * SLAB : (j + 1) * SLAB, :]).astype(BF16)
            prod = do.astype(F32) * att_r[j].astype(F32)
            code = jnp.zeros((R, 128), F32)
            for n in range(KV):
                delta = jnp.sum(prod * value_lanes[n].astype(F32), axis=1, keepdims=True)
                for i, part in enumerate(split_three(-delta)):
                    code = code + jnp.where(lane == 3 * n + i, part, 0.0)
            dos[j] = jnp.concatenate([do[:, :128] + code.astype(BF16), do[:, 128:]], axis=1)
        if not attn:
            io.store(dos, dos_out)

    def attention_back():
        qb_r, bias_r = qb(), bias()
        if not ffn:
            dos_ready()
        for ready in kv_ready:
            ready()
        kcode_r = kcode()

        lane_all = lax.broadcasted_iota(jnp.int32, (1, SLAB), 1)
        for gi in range(G):
            rows = slice(gi * RG, (gi + 1) * RG)
            qg = jnp.concatenate([qb_r[j, rows, :] for j in range(GQ)], axis=0)
            dog = jnp.concatenate([dos[j, rows, :] for j in range(GQ)], axis=0)
            qt, dot_out = qg.T, dog.T
            db = place["starts"][gi] // KB
            lb = doc_start(docs, place["starts"][gi]) // KB

            def block(b, count, diagonal=False):
                ds_all, k_all = [], []
                for c in range(count):
                    at = pl.ds(pl.multiple_of((b + c) * KB, KB), KB)
                    k = keys_of(kvs, b + c)
                    v = values_of(kvs, b + c)
                    code = None if diagonal else kcode_r[at, :]
                    for n in range(KV):
                        kn = k * key_lanes[n]
                        high = kn[:, 128:] + total_lanes[n]
                        if not diagonal:
                            high = high + code
                        kn = jnp.concatenate([kn[:, :128], high], axis=1)
                        vn = v * value_lanes[n] + delta_lanes[n]
                        s = dot_t(qg, kn)
                        if diagonal:
                            s = s + jnp.concatenate([bias_r[gi]] * GQ, axis=0)
                        p = jnp.exp2(s)
                        dp = dot_t(dog, vn)
                        ds = (p * dp).astype(BF16)
                        ds_all.append(ds)
                        k_all.append(kn)
                        dkv_scr[n * HD : (n + 1) * HD, at] += dot(qt[n * HD : (n + 1) * HD], ds)
                        dv = dot(dot_out[VOFF + n * HD : VOFF + (n + 1) * HD], p.astype(BF16))
                        dkv_scr[KVD + n * HD : KVD + (n + 1) * HD, at] += dv
                dq = dot(jnp.concatenate(ds_all, axis=1), jnp.concatenate(k_all, axis=0))
                if diagonal:
                    dq_scr[...] = dq
                else:
                    dq_scr[...] += dq

            block(db, 1, True)
            in_pairs(lb, db, block)
            for j in range(GQ):
                t = dq_scr[j * RG : (j + 1) * RG, :]
                t = jnp.where(lane_all < KVD, t, 0.0) * SCALE
                t = t * cos[rows, :] - swapped(t) * sin[rows, :]
                qg_v[j, rows, :] = t.astype(BF16)
        io.store(qg_v, qg_out)
        for (into, row, n_rows), at in zip(dests, place["rows"]):
            at = pl.multiple_of(at, 128)
            t = dkv_scr[:, pl.ds(at, n_rows)]
            t = jnp.concatenate([t[:KVD] * LN2, t[KVD:]], axis=0)
            dkv_v[into][row : row + n_rows] = t.T.astype(BF16)
        for v, out in zip(dkv_v, dkv_out):
            io.store(v, out)

    if ffn:
        feed_forward_back()
    if attn:
        attention_back()
    io.finish()


VM = lambda: pl.BlockSpec(memory_space=pltpu.VMEM)
SM = lambda: pl.BlockSpec(memory_space=pltpu.SMEM)
HB = lambda: pl.BlockSpec(memory_space=pl.ANY)
S = jax.ShapeDtypeStruct


def with_token(body, n):
    return lambda *refs: body(*refs[:n], *refs[n + 1 :])


def call(body, args, spaces, outs, scratch, flops, name, in_vmem=False, token=None):
    if token is not None:
        body = with_token(body, len(args))
        args, spaces = [*args, token], spaces + "h"
    spec = {"v": VM, "s": SM, "h": HB}
    return pl.pallas_call(
        body,
        out_shape=outs,
        in_specs=[spec[c]() for c in spaces],
        out_specs=[(VM if in_vmem else HB)() for _ in outs],
        scratch_shapes=scratch,
        compiler_params=pltpu.CompilerParams(vmem_limit_bytes=60 * 1024 * 1024),
        cost_estimate=pl.CostEstimate(flops=flops // 64, bytes_accessed=1000, transcendentals=0),
        name=name,
    )(*args)


def like(*shapes):
    return [pltpu.VMEM(t.shape, t.dtype) for t in shapes]


def sems(n):
    return [pltpu.SemaphoreType.DMA((n,))]


def gate_up_kernel(scal, *refs):
    n2, gg, ug = refs[0:4], refs[4:8], refs[8:12]
    keep, give, left = refs[12:15]
    R = n2[0].shape[0]

    @pl.when(pl.program_id(0) == 0)
    def _():
        for i in range(4):
            left[:, i * R : (i + 1) * R] = n2[i][...].T

    a = dot(left[...], jnp.concatenate([t[...] for t in gg], axis=0))
    b = dot(left[...], jnp.concatenate([t[...] for t in ug], axis=0))
    share(scal, a, b, keep, give)


def down_kernel(scal, *refs):
    act, dg = refs[0:4], refs[4:8]
    keep, give = refs[8:10]
    left = jnp.concatenate([t[...].T for t in act], axis=1)
    w = dot(left, jnp.concatenate([t[...] for t in dg], axis=0))
    zero = scal[0] == 0
    chunks, rows = keep.shape[0], keep.shape[1]
    for c in range(chunks):
        a = w[2 * c * rows : (2 * c + 1) * rows]
        b = w[(2 * c + 1) * rows : (2 * c + 2) * rows]
        keep[c] = jnp.where(zero, a, b).astype(BF16)
        give[c] = jnp.where(zero, b, a).astype(BF16)


def out_grads_kernel(scal, *refs):
    att, og = refs[0:4], refs[4:8]
    keep, give = refs[8:10]
    grads = jnp.concatenate([t[...] for t in og], axis=0)
    outs = []
    for j in range(GQ):
        left = jnp.concatenate([t[j].T for t in att], axis=1)
        outs.append(dot(left, grads))
    o = jnp.concatenate(
        [outs[j][VOFF + n * HD : VOFF + (n + 1) * HD] for n in range(KV) for j in range(GQ)],
        axis=0,
    )
    half = o.shape[1] // 2
    share(scal, o[:, :half], o[:, half:], keep, give)


def share(scal, a, b, keep, give):
    zero = scal[0] == 0
    chunks, rows = keep.shape[0], a.shape[0] // keep.shape[0]
    if a.shape[1] < keep.shape[2]:
        pad = jnp.zeros((a.shape[0], keep.shape[2] - a.shape[1]), F32)
        a, b = jnp.concatenate([a, pad], axis=1), jnp.concatenate([b, pad], axis=1)
    k, g = jnp.where(zero, a, b), jnp.where(zero, b, a)
    for c in range(chunks):
        keep[c, :rows] = k[c * rows : (c + 1) * rows].astype(BF16)
        give[c, :rows] = g[c * rows : (c + 1) * rows].astype(BF16)
        if rows < keep.shape[1]:
            for t in (keep, give):
                t[c, rows:] = jnp.zeros((keep.shape[1] - rows, keep.shape[2]), BF16)


def qkv_grads_kernel(scal, *refs):
    normed, qg, kvg, gain1, gain2 = refs[0:4], refs[4:8], refs[8:12], refs[12:16], refs[16:20]
    keep, give = refs[20:22]
    left = jnp.concatenate([t[...].T for t in normed], axis=1)
    slabs = [dot(left, jnp.concatenate([t[j] for t in qg], axis=0)) for j in range(GQ)]
    cols = [slabs[j][:, n * HD : (n + 1) * HD] for n in range(KV) for j in range(GQ)]
    cols.append(dot(left, jnp.concatenate([t[...] for t in kvg], axis=0)))
    w = jnp.concatenate(cols, axis=1)
    half = w.shape[1] // 2
    share(scal, w[:, :half], w[:, half:], keep, give)
    chunks, rows = keep.shape[0], w.shape[0] // keep.shape[0]
    zero = scal[0] == 0
    n = 2 * gain1[0].shape[1] // chunks
    for c in range(chunks):
        refs_c = gain1 if c < chunks // 2 else gain2
        at = (c % (chunks // 2)) * n
        total = refs_c[0][0:1, at : at + n]
        for t in refs_c[1:]:
            total = total + t[0:1, at : at + n]
        total = jnp.concatenate([total, jnp.zeros((1, keep.shape[2] - n), F32)], axis=1)
        keep[c, rows : rows + 1] = jnp.where(zero, total, 0.0).astype(BF16)
        give[c, rows : rows + 1] = jnp.where(zero, 0.0, total).astype(BF16)


def section_sums_kernel(n, scal, *refs):
    keep, got, outs = refs[:n], refs[n : 2 * n], refs[2 * n :]
    d = scal[2]
    for i in range(n):
        for m in range(4):
            for z in range(4):
                at = z * 4 + lax.bitwise_xor(d, jnp.int32(m))
                total = keep[i][at].astype(F32) + got[i][at].astype(F32)
                outs[4 * i + m][z] = total.astype(BF16)


def pair_sums_kernel(n, scal, *refs):
    keep, got, out = refs[:n], refs[n : 2 * n], refs[2 * n]
    tiles = list(lane_tiles([t.shape[1:] for t in keep]))
    for c in range(16):
        for i, row, rows, col, cols in tiles:
            span = slice(col, col + cols)
            total = keep[i][c, :, span].astype(F32) + got[i][c, :, span].astype(F32)
            out[(c % 4) * 4 + c // 4, row : row + rows, :cols] = total.astype(BF16)


def unpack_kernel(scal, *refs):
    packed, outs = refs[0], refs[1:]
    for i, row, rows, col, cols in lane_tiles([t.shape for t in outs]):
        total = packed[row : row + rows, :cols].astype(F32)
        outs[i][:, col : col + cols] = total


def lane_tiles(shapes):
    at = 0
    for i, (rows, cols) in enumerate(shapes):
        for col in range(0, cols, 128):
            yield i, at, rows, col, min(128, cols - col)
            at += rows


def halving_kernel(n, stage, scal, *refs):
    own, got, outs = refs[:n], refs[n : 2 * n], refs[2 * n :]
    axis, bit, inner = stage
    mine = lax.bitwise_and(lax.shift_right_logical(scal[axis], jnp.int32(bit)), 1)
    tiles = list(lane_tiles([t.shape[1:] for t in own]))
    for c in range(outs[0].shape[0]):
        base = (c // inner) * 2 * inner + c % inner
        for k, out in enumerate(outs):
            at = base + inner * (mine if k == 0 else 1 - mine)
            for i, row, rows, col, cols in tiles:
                span = slice(col, col + cols)
                total = own[i][at, :, span].astype(F32) + got[i][at, :, span].astype(F32)
                out[c, row : row + rows, :cols] = total.astype(BF16)


def last_kernel(scal, *refs):
    own, got, outs = refs[0], refs[1], refs[2:]
    for i, row, rows, col, cols in lane_tiles([t.shape for t in outs]):
        span = slice(row, row + rows)
        total = own[0, span, :cols].astype(F32) + got[0, span, :cols].astype(F32)
        outs[i][:, col : col + cols] = total


def dp_sums_kernel(n, scal, *refs):
    ins, outs = refs[: 4 * n], refs[4 * n :]
    for i in range(n):
        for m in range(4):
            at = lax.bitwise_xor(scal[1], jnp.int32(m))
            total = ins[4 * i][at].astype(F32)
            for t in ins[4 * i + 1 : 4 * i + 4]:
                total = total + t[at].astype(F32)
            out = outs[4 * i + m]
            out[...] = total.astype(out.dtype)


def seq_sums_kernel(n, scal, *refs):
    ins, outs = refs[: 4 * n], refs[4 * n :]
    for i in range(n):
        total = ins[4 * i][...]
        for t in ins[4 * i + 1 : 4 * i + 4]:
            total = total + t[...].astype(F32)
        outs[i][...] = total


def grid_call(body, scal, args, in_specs, outs, out_specs, scratch, grid, flops, name, token):
    if token is not None:
        body = with_token(body, 1 + len(args))
        args, in_specs = [*args, token], in_specs + [HB()]
    return pl.pallas_call(
        body,
        out_shape=outs,
        grid=grid,
        in_specs=[SM()] + in_specs,
        out_specs=out_specs,
        scratch_shapes=scratch,
        compiler_params=pltpu.CompilerParams(vmem_limit_bytes=60 * 1024 * 1024),
        cost_estimate=pl.CostEstimate(flops=flops // 64, bytes_accessed=1000, transcendentals=0),
        name=name,
    )(scal, *args)


def padded(n, to=8):
    return -(-n // to) * to


class Early:
    def __init__(self, its, scal, R, D, FF, chunks, order):
        self.its, self.scal, self.order = its, scal, order
        self.sizes = R, D, FF, chunks

    def get(self, key):
        refs = [t[key] for t in self.its]
        return refs

    def gate_up(self):
        R, D, FF, chunks = self.sizes
        rows = padded(D // chunks)
        tile = 512
        out = pl.BlockSpec((chunks, rows, tile), lambda i: (0, 0, i))
        pair = grid_call(
            gate_up_kernel,
            self.scal,
            self.get("n2") + self.get("gg") + self.get("ug"),
            [pl.BlockSpec((R, D), lambda i: (0, 0))] * 4
            + [pl.BlockSpec((R, tile), lambda i: (0, i))] * 8,
            [S((chunks, rows, FF), BF16)] * 2,
            [out] * 2,
            [pltpu.VMEM((D, 4 * R), BF16)],
            (FF // tile,),
            16 * R * D * FF,
            "gate_up_grads",
            self.order.token,
        )
        self.order.done(pair[0])
        return tuple(pair)

    def down(self):
        R, D, FF, chunks = self.sizes
        rows = FF // chunks
        step = 4
        out = pl.BlockSpec((step, rows // 2, D), lambda i: (i, 0, 0))
        pair = grid_call(
            down_kernel,
            self.scal,
            self.get("act") + self.get("dg"),
            [pl.BlockSpec((R, step * rows), lambda i: (0, i))] * 4
            + [pl.BlockSpec((R, D), lambda i: (0, 0))] * 4,
            [S((chunks, rows // 2, D), BF16)] * 2,
            [out] * 2,
            [],
            (chunks // step,),
            8 * R * D * FF,
            "down_grads",
            self.order.token,
        )
        self.order.done(pair[0])
        return tuple(pair)

    def out(self):
        R, D, FF, chunks = self.sizes
        pair = call(
            out_grads_kernel,
            [self.scal, *self.get("att"), *self.get("og")],
            "s" + "v" * 8,
            [S((chunks, padded(D // chunks), padded(D // 2, 128)), BF16)] * 2,
            [],
            8 * R * D * D,
            "out_grads",
            True,
            self.order.token,
        )
        self.order.done(pair[0])
        return tuple(pair)


def early_grads(its, scal, R, D, FF, chunks, order):
    grads = Early(its, scal, R, D, FF, chunks, order)
    return grads.gate_up(), grads.down(), grads.out()


def late_grads(its, scal, R, D, chunks, order):
    get = lambda key: [t[key] for t in its]
    pair = call(
        qkv_grads_kernel,
        [scal, *get("normed"), *get("qg"), *get("kvg"), *get("gain1"), *get("gain2")],
        "s" + "v" * 20,
        [S((chunks, padded(D // chunks + 1, 16), padded((D + 2 * KVD) // 2, 128)), BF16)] * 2,
        [],
        14 * R * D * D,
        "qkv_grads",
        True,
        order.token,
    )
    order.done(pair[0])
    return tuple(pair)


def vm_call(body, scal, args, outs, name, token):
    args = [scal, *args]
    spaces = "s" + "v" * (len(args) - 1)
    return call(body, args, spaces, outs, [], 10_000_000, name, True, token)


class Offloaded:
    def __init__(self, pairs, scal):
        self.scal = scal
        self.keep = [k for k, _ in pairs]
        self.ins = [lax.ppermute(g, "section", SWAP) for _, g in pairs]

    def step(self, order):
        shapes = [k.shape[1:] for k in self.keep]
        rows = sum(r * padded(c, 128) // 128 for r, c in shapes)
        (t,) = vm_call(
            functools.partial(pair_sums_kernel, len(shapes)),
            self.scal,
            [*self.keep, *self.ins],
            [S((16, rows, 128), BF16)],
            "sum_pairs",
            order.token,
        )
        order.done(t)
        t = t.reshape(16 * rows, 128)
        for axis in ("dp", "seq"):
            t = lax.psum_scatter(t, axis, scatter_dimension=0, tiled=True)
        self.packed = t

    def last(self, order):
        outs = [S(k.shape[1:], F32) for k in self.keep]
        self.result = vm_call(
            unpack_kernel, self.scal, [self.packed], outs, "sum_unpack", order.token
        )
        order.done(self.result[0])


class Halving:
    def __init__(self, pairs, scal, first):
        self.scal = scal
        self.own = [k for k, _ in pairs]
        self.shapes = [k.shape[1:] for k in self.own]
        self.ins = [lax.ppermute(g, "section", SWAP) for _, g in pairs]
        self.stages = [(2, 0, 1), (2, 1, 1)] if first == "x" else [(2, 1, 2), (2, 0, 1)]
        self.stages += [(1, 0, 1), (1, 1, 1)]

    def step(self, order):
        n = len(self.own)
        ins = [*self.own, *self.ins]
        rows = sum(r * padded(c, 128) // 128 for r, c in self.shapes)
        if not self.stages:
            outs = [S(k, F32) for k in self.shapes]
            self.result = vm_call(last_kernel, self.scal, ins, outs, "sum_last", order.token)
            order.done(self.result[0])
            return
        stage = self.stages.pop(0)
        chunks = self.own[0].shape[0] // 2
        parts = vm_call(
            functools.partial(halving_kernel, n, stage),
            self.scal,
            ins,
            [S((chunks, rows, 128), BF16)] * 2,
            "sum_halves",
            order.token,
        )
        order.done(parts[0])
        axis, bit, _ = stage
        pairs = [(j, j ^ (1 << bit)) for j in range(4)]
        self.own = [parts[0]]
        self.ins = [lax.ppermute(parts[1], ("seq", "dp")[axis - 1], pairs)]


class Sum:
    def __init__(self, pairs, scal):
        self.n = len(pairs)
        self.scal = scal
        self.stage = 0
        keep = [k for k, _ in pairs]
        self.shapes = [k.shape for k in keep]
        self.ins = keep + [lax.ppermute(g, "section", SWAP) for _, g in pairs]

    def step(self, order):
        n, stage = self.n, self.stage
        body = (section_sums_kernel, dp_sums_kernel, seq_sums_kernel)[stage]
        cut = lambda k: ((4,) + k[1:], k[1:], k[1:])[stage]
        kinds = ((BF16,) * 4, (F32, BF16, BF16, BF16), (F32,))[stage]
        parts = call(
            functools.partial(body, n),
            [self.scal, *self.ins],
            "s" + "v" * len(self.ins),
            [S(cut(k), kind) for k in self.shapes for kind in kinds],
            [],
            10_000_000,
            ("sum_sections", "sum_dp", "sum_seq")[stage],
            True,
            order.token,
        )
        order.done(parts[0])
        self.stage += 1
        if stage == 2:
            self.result = parts
            return
        axis = ("dp", "seq")[stage]
        self.ins = []
        for i in range(n):
            self.ins.append(parts[4 * i])
            for m in range(1, 4):
                pairs = [(j, j ^ m) for j in range(4)]
                self.ins.append(lax.ppermute(parts[4 * i + m], axis, pairs))


class Order:
    def __init__(self):
        self.token = None
        self.flights = []

    def expect(self, arrivals, first=0):
        self.flights.append((arrivals, first))

    def landed(self, t):
        flat = [a for arrivals, first in self.flights for a in arrivals[first:]]
        t, *flat = lax.optimization_barrier((t, *flat))
        for arrivals, first in self.flights:
            n = len(arrivals) - first
            arrivals[first:] = flat[:n]
            flat = flat[n:]
        self.flights = []
        return t

    def arrive(self):
        self.token = self.landed(self.token)

    def done(self, token):
        self.token = token


class Device:
    turned = False

    def __init__(self, shard_len):
        self.shard_len = shard_len
        self.seq_total = shard_len * lax.axis_size("seq")
        self.core = lax.axis_index("section")
        self.z = lax.axis_index("seq")
        self.d = lax.axis_index("dp")
        self.R = shard_len // 2
        self.G = 1

    def place(self, scal):
        core, z = scal[0], scal[1]
        start = z * self.shard_len + core * self.R
        return dict(core=core, near=core == 0, own=core >= 0, starts=[start], rows=[jnp.int32(0)])

    def rows_in(self, tokens):
        return [[lax.dynamic_slice_in_dim(t, self.core * self.R, self.R, 0)] for t in tokens]

    def rows_out(self, low0, low1):
        low0, low1 = jnp.stack(low0), jnp.stack(low1)
        give = jnp.where(self.core == 0, low1, low0)
        keep = jnp.where(self.core == 0, low0, low1)
        got = lax.ppermute(give, "section", SWAP)
        first = jnp.where(self.core == 0, keep, got)
        second = jnp.where(self.core == 0, got, keep)
        return jnp.concatenate([first, second], axis=1)

    def documents(self, both):
        return both

    def kv_pieces(self):
        whole = ((0, 0, self.seq_total),)
        return whole, whole

    def send(self, kv):
        return kv

    def gather(self, kv, order):
        return [lax.all_gather(kv, ("seq", "section"), axis=0, tiled=True)]

    def scatter(self, dkv, order):
        return dkv[0]

    def scattered(self, dkv, order):
        return [lax.psum_scatter(dkv, ("seq", "section"), scatter_dimension=0, tiled=True)]


SWAP = [(0, 1), (1, 0)]


class Squares(Device):
    turned = True

    def __init__(self, shard_len):
        super().__init__(shard_len)
        self.x = self.d % 2
        self.near = self.z < 2
        self.half = shard_len // 4
        self.G = 2
        self.crossing = self.near == (self.x == 1)

    def place(self, scal):
        core, z, d = scal[0], scal[1], scal[2]
        x = d % 2
        near = z < 2
        role = jnp.where(near, 2 * z + x, 2 * (3 - z) + 1 - x)
        rows = []
        for p in range(8):
            other = lax.bitwise_xor(role, jnp.int32(p % 4))
            rows += self.positions(other, core if p < 4 else 1 - core)
        return dict(core=core, near=near, own=x == z // 2, starts=rows[:2], rows=rows)

    def positions(self, role, core):
        block = 2 * self.half
        return [role * block + core * self.half, (7 - role) * block + (1 - core) * self.half]

    def along_x(self, t):
        return lax.ppermute(t, "dp", [(i, i ^ 1) for i in range(4)])

    def along_z(self, t):
        return lax.ppermute(t, "seq", [(i, i ^ 1) for i in range(4)])

    def diagonal(self, t):
        pairs = [(z * 4 + d, (z ^ 1) * 4 + (d ^ 1)) for z in range(4) for d in range(4)]
        return lax.ppermute(t, ("seq", "dp"), pairs)

    def mirrored(self, t):
        return lax.ppermute(t, "seq", [(i, 3 - i) for i in range(4)])

    def documents(self, both):
        return self.along_x(both)

    def rows_in(self, tokens):
        at = jnp.where(self.near, self.core, 1 - self.core) * self.half
        far = at + 2 * self.half
        out = []
        for t in tokens:
            part = lambda start: lax.dynamic_slice_in_dim(t.T, start, self.half, 1)
            hopped = self.along_x(part(jnp.where(self.near, far, at)))
            kept = part(jnp.where(self.near, at, far))
            moved = self.mirrored(jnp.where(self.crossing, kept, hopped))
            out.append([jnp.where(self.crossing, hopped, kept), moved])
        return out

    def kv_pieces(self):
        n = self.half
        pieces, dests = [], []
        for p in range(8):
            pieces += [(p, 0, n), (p, n, n)]
            dests += [(p // 4, (p % 4) * 2 * n, n), (p // 4, (p % 4) * 2 * n + n, n)]
        return tuple(pieces), tuple(dests)

    def send(self, kv):
        return [kv, self.along_x(kv), self.along_z(kv), self.diagonal(kv)]

    def gather(self, sent, order):
        *there, order.token = lax.optimization_barrier((*sent[1:], order.token))
        sent = sent[:1] + there
        return sent + [lax.ppermute(t, "section", SWAP) for t in sent]

    def scatter(self, dkv, order):
        give, order.token = lax.optimization_barrier((order.landed(dkv[1]), order.token))
        return dkv[0], lax.ppermute(give, "section", SWAP)

    def scattered(self, parts, order):
        keep, got = parts
        n = 2 * self.half
        at = lambda t, m: t[m * n : (m + 1) * n].astype(F32)
        part = [(at(keep, m) + at(got, m)).astype(BF16) for m in range(4)]
        part[0], order.token = lax.optimization_barrier((part[0], order.token))
        sums = [part[0], self.along_x(part[1]), self.along_z(part[2]), self.diagonal(part[3])]
        order.expect(sums, 1)
        return sums


class RowsOut:
    def __init__(self, dev, rows, layer=None):
        self.dev, self.layer = dev, layer
        self.rows = [jnp.stack(r) for r in rows]
        self.stage = 0
        self.arrivals = []

    def along(self, t, axis, pairs):
        if self.layer is not None:
            pairs = [(self.layer * 4 + a, self.layer * 4 + b) for a, b in pairs]
            axis = ("section", axis)
        self.arrivals = [lax.ppermute(t, axis, pairs)]

    def step(self, order=None):
        dev, n = self.dev, self.dev.half
        first = dev.core == 0
        if self.stage == 0:
            if self.layer is None:
                give = jnp.where(first, self.rows[1], self.rows[0])
                self.keep = jnp.where(first, self.rows[0], self.rows[1])
                pairs = SWAP
            else:
                give = self.keep = self.rows[0]
                pairs = [(1 - self.layer, self.layer)]
            self.arrivals = [lax.ppermute(give, "section", pairs)]
        elif self.stage == 1:
            (got,) = self.arrivals
            zero = jnp.where(first, self.keep, got)
            one = jnp.where(first, got, self.keep)
            early = jnp.concatenate([zero[:, :, :n], one[:, :, :n]], axis=2)
            late = jnp.concatenate([one[:, :, n:], zero[:, :, n:]], axis=2)
            self.stay = jnp.where(dev.near, early, late)
            give = jnp.where(dev.near, late, early)
            self.along(give, "seq", [(z, 3 - z) for z in range(4)])
        elif self.stage == 2:
            (moved,) = self.arrivals
            self.kept = jnp.where(dev.crossing, moved, self.stay)
            give = jnp.where(dev.crossing, self.stay, moved)
            self.along(give, "dp", [(d, d ^ 1) for d in range(4)])
        else:
            (hopped,) = self.arrivals
            lower = jnp.where(dev.near, self.kept, hopped)
            upper = jnp.where(dev.near, hopped, self.kept)
            self.result = jnp.concatenate([lower, upper], axis=2).transpose(0, 2, 1)
            return
        self.stage += 1
        if order is not None:
            order.expect(self.arrivals)


def per_device(
    tokens,
    cotangent,
    doc_lengths,
    pad_count,
    attn_gain,
    w_query,
    w_key,
    w_value,
    w_out,
    ffn_gain,
    w_gate,
    w_up,
    w_down,
):
    micro, shard_len, D = tokens.shape
    FF = w_gate.shape[-1]
    fast = (lax.axis_size("seq"), lax.axis_size("dp"), shard_len) == (4, 4, 512)
    dev = Squares(shard_len) if fast else Device(shard_len)
    R, G, total = dev.R, dev.G, dev.seq_total
    RG = R // G
    M = GQ * RG
    NB = total // KB
    core = dev.core

    scal = jnp.stack([core, dev.z, dev.d]).astype(jnp.int32)
    own = jnp.concatenate([doc_lengths, pad_count[:, None]], axis=1).astype(jnp.int32)
    hopped = dev.documents(own)
    xs = dev.rows_in([tokens[i] for i in range(micro)])

    turn = lambda t: t.T if fast else t
    wqkv_m, wout_m, gains_m = call(
        functools.partial(pack_kernel, fast),
        [w_query[0], turn(w_key[0]), turn(w_value[0]), w_out[0], attn_gain, ffn_gain],
        "v" * 6,
        [S((D, GQ * SLAB + 2 * KVD), BF16), S((GQ * SLAB, D), BF16), S((8, D), F32)],
        [],
        1_000_000,
        "pack_weights",
        in_vmem=True,
    )
    swap = lambda t: lax.ppermute(t, "section", SWAP)
    mine = [wout_m, w_gate[0], w_up[0], w_down[0].T, gains_m]
    mine_n = [wqkv_m, gains_m]
    theirs_n = [swap(t) for t in mine_n]
    theirs = [swap(t) for t in mine[:4]] + theirs_n[1:]

    RG = R // G
    start = dev.place([core, dev.z, dev.d])["starts"]
    rows = jnp.concatenate([s + jnp.arange(RG, dtype=jnp.int32) for s in start])
    lane = jnp.arange(SLAB, dtype=jnp.int32)
    frequency = THETA ** (-2.0 * (lane % (HD // 2)).astype(F32) / HD)
    frequency = jnp.where(lane < KVD, frequency, 0.0)
    angles = rows.astype(F32)[:, None] * frequency[None, :]
    sign = jnp.where(lane % HD < HD // 2, -1.0, 1.0)
    cos, sin = jnp.cos(angles), jnp.sin(angles) * sign[None, :]
    pieces, dests = dev.kv_pieces()
    dest_rows = [0] * (1 + max(d for d, _, _ in dests))
    for d, row, n_rows in dests:
        dest_rows[d] = max(dest_rows[d], row + n_rows)
    n_pieces = len(pieces)
    kcode, qcode, bias = call(
        functools.partial(setup_kernel, dev, micro, total, R, G),
        [scal, own, hopped],
        "sss",
        [S((micro, total, 128), BF16), S((micro, R, 128), BF16), S((micro, G, RG, KB), F32)],
        [],
        1_000_000,
        "setup",
        in_vmem=True,
    )
    head = [scal, own, hopped]
    one_of = lambda t: S(t.shape[1:], t.dtype)

    sds = lambda shape, kind: S(shape, kind)
    dense_flops = 2 * R * (D * D * 2 + D * KVD * 2 + 3 * D * FF)

    def first(parts, token):
        outs = [sds((R, D), BF16), sds((GQ, R, SLAB), BF16), sds((R, 2 * KVD), BF16)]
        scratch = like(outs[0], cos, sin, wqkv_m, gains_m, *outs[1:])
        if len(parts) > 1:
            scratch += like(*parts)
        args = [scal, *parts, cos, sin, wqkv_m, theirs_n[0], gains_m, theirs_n[1]]
        return call(
            functools.partial(first_kernel, dev, len(parts)),
            args,
            "s" + "h" * (len(args) - 1),
            outs,
            scratch + sems(9),
            dense_flops // 5,
            "qkv_first",
            token=token,
        )

    def forward(x, q, kv_parts, i, layer, layer_n, rounded):
        has_next = layer_n is not None
        cfg = (i, layer, layer_n, R, G, pieces, len(kv_parts), has_next, rounded)
        args = [*head, x, q, kcode, bias, cos, sin, qcode, *kv_parts, *mine, *theirs]
        outs = [
            sds((R, D), F32),
            sds((R, D), F32),
            sds((GQ, R, SLAB), BF16),
            sds((R, FF), BF16),
            sds((R, FF), BF16),
            sds((GQ, R, SLAB), BF16),
        ]
        scratch = like(x, q, one_of(kcode), one_of(bias), one_of(qcode), *outs)
        scratch += [
            pltpu.VMEM((total, 2 * KVD), BF16),
            pltpu.VMEM((KV, NB, M, KB), F32),
            pltpu.VMEM((KV, M, 128), F32),
            pltpu.VMEM((KV, M, 128), F32),
            pltpu.VMEM((KV, M, SLAB), F32),
            pltpu.VMEM((R, FF), BF16),
            *like(*mine),
        ]
        if has_next:
            args += mine_n + theirs_n
            more = [sds((GQ, R, SLAB), BF16), sds((R, 2 * KVD), BF16)]
            outs += more
            scratch += like(cos, sin, *mine_n, *more)
        if rounded:
            outs.append(sds((D, R) if fast else (R, D), BF16))
            scratch += like(outs[-1])
        return call(
            functools.partial(forward_kernel, dev, cfg),
            args,
            "sss" + "h" * (len(args) - 3),
            outs,
            scratch + sems(n_pieces + 24),
            dense_flops * 2,
            "forward",
            token=order.token,
        )

    def backward(i, one, two, layer_n, layer, rounded=False, attn=None):
        part_one = "sums" in one
        ffn = two is not None and not (one == {})
        attn = two is not None if attn is None else attn
        args = [*head, cos, sin]
        outs, scratch = [], like(cos, sin)
        keys = []
        n_sums = n_g = n_parts = 0
        if part_one:
            n_sums = len(one["sums"])
            ins = [*one["sums"], one["hg"], one["qg"], one["x"]]
            args += ins + mine_n + theirs_n
            more = [sds((R, 2 * KVD), BF16), sds((R, D), BF16), sds((8, D), F32)]
            keys += ["kvg", "normed", "gain1"]
            if rounded or not ffn:
                more.append(sds((D, R) if fast else (R, D), BF16))
                keys.append("low")
            scratch += like(*ins, *mine_n, *more)
            outs += more
        elif ffn:
            n_g = len(one["g"])
            args += one["g"]
            scratch += like(*one["g"])
        slabs = sds((GQ, R, SLAB), BF16)
        if ffn:
            ins = [two["h"], two["gate"], two["up"], two["att"]]
            args += [*ins, *mine, *theirs]
            wide, slim = sds((R, FF), BF16), sds((R, D), BF16)
            more = [sds((R, D), F32), slim, wide, wide, wide, slim, slim, sds((8, D), F32)]
            keys += ["hg", "n2", "gg", "ug", "act", "dg", "og", "gain2"]
            scratch += like(*ins, *more, *mine)
            outs += more
            if not attn:
                keys.append("dos")
                outs.append(slabs)
        if ffn or attn:
            scratch += like(slabs)
        if attn:
            n_parts = len(two["parts"])
            args += [two["qb"], kcode, bias, *two["parts"]]
            if not ffn:
                args.append(two["dos"])
            more = [slabs, *[sds((n, 2 * KVD), BF16) for n in dest_rows]]
            keys += ["qg"] + ["dkv%d" % n for n in range(len(dest_rows))]
            scratch += like(two["qb"], one_of(kcode), one_of(bias), *more)
            scratch += [
                pltpu.VMEM((total, 2 * KVD), BF16),
                pltpu.VMEM((M, SLAB), F32),
                pltpu.VMEM((2 * KVD, total), F32),
            ]
            outs += more
        cfg = (i, layer, layer_n, R, G, pieces, dests, n_parts, n_sums, n_g)
        cfg += (part_one, ffn, attn, rounded)
        res = call(
            functools.partial(backward_kernel, dev, cfg),
            args,
            "sss" + "h" * (len(args) - 3),
            outs,
            scratch + sems(n_pieces + 45),
            dense_flops * 4,
            "backward",
            token=order.token,
        )
        out = dict(zip(keys, res))
        if attn:
            out["dkv"] = [out.pop("dkv%d" % n) for n in range(len(dest_rows))]
        return out

    state = [[None] * 4 for _ in range(micro)]
    lows = [None] * micro
    tops = [None] * micro
    qkv, cur, sent = [None] * micro, [None] * micro, [None] * micro
    order = Order()
    if fast:
        order.done(kcode)
        xs[0][0], *there = lax.optimization_barrier((xs[0][0], *theirs, theirs_n[0]))
        theirs, theirs_n = there[:5], [there[5], there[4]]
    for i in range(micro):
        cur[i], *qkv[i] = first(xs[i], order.token)
        order.done(qkv[i][1])
        sent[i] = dev.send(qkv[i][1])
    order.done(qkv[-1][1])
    cots = dev.rows_in([cotangent[i] for i in range(micro)])

    def forward_step(app, i):
        layer = app // 2
        nxt = None if app == 3 else (app + 1) // 2
        rounded = app in (1, 3)
        parts = dev.gather(sent[i], order)
        res = forward(cur[i], qkv[i][0], parts, i, layer, nxt, rounded)
        y, h, att, gate, up, qb = res[:6]
        order.done(h)
        state[i][app] = dict(x=cur[i], h=h, att=att, gate=gate, up=up, qb=qb, parts=parts)
        if rounded:
            (lows if app == 1 else tops)[i] = res[-1]
        cur[i] = y
        if nxt is not None:
            qkv[i] = (res[6], res[7])
            sent[i] = dev.send(res[7])

    items = [[{} for _ in range(4)] for _ in range(micro)]
    bound = [None] * micro
    last = [None] * micro
    pend = [dict(g=cots[i]) for i in range(micro)]

    def send_on(i):
        pend[i]["sums"] = dev.scattered(pend[i].pop("parts"), order)

    def backward_step(app, i, attn=None):
        two = state[i][app] if app >= 0 else None
        layer_n = (app + 1) // 2 if app < 3 else None
        rounded = app == 1
        res = backward(i, pend[i], two, layer_n, app // 2 if app >= 0 else None, rounded, attn)
        if app < 3:
            items[i][app + 1].update({k: res[k] for k in ("kvg", "normed", "gain1")})
            order.done(res["normed"])
            if rounded:
                bound[i] = res["low"]
            if app < 0:
                last[i] = res["low"]
        if app >= 0:
            items[i][app].update(
                {k: res[k] for k in ("n2", "gg", "ug", "act", "dg", "og", "gain2")}
            )
            items[i][app]["att"] = two["att"]
            order.done(res["hg"])
            pend[i] = dict(hg=res["hg"], x=two["x"])
            if attn is False:
                two["dos"] = res["dos"]
            else:
                take_attention(app, i, res)

    def take_attention(app, i, res):
        items[i][app]["qg"] = pend[i]["qg"] = res["qg"]
        order.done(res["qg"])
        pend[i]["parts"] = dev.scatter(res["dkv"], order)

    def attention_step(app, i):
        two = state[i][app]
        take_attention(app, i, backward(i, {}, two, None, app // 2))

    for app in range(3):
        for i in range(micro):
            forward_step(app, i)
    for i in range(micro):
        forward_step(3, i)
        backward_step(3, i)
        send_on(i)
    pairs_of = lambda layer: [items[i][a] for a in (2 * layer, 2 * layer + 1) for i in range(micro)]
    if not fast:
        for app in (2, 1, 0, -1):
            for i in range(micro):
                backward_step(app, i)
                if app >= 0:
                    send_on(i)
        outs = plain_sums([pairs_of(0), pairs_of(1)], R, D)
        layer_out = dev.rows_out(lows, tops)
        input_grad = dev.rows_out(last, bound)
    else:
        outputs = RowsOut(dev, [lows, tops])
        outputs.step(order)
        backward_step(2, 0)
        outputs.step(order)
        send_on(0)
        backward_step(2, 1)
        outputs.step()
        send_on(1)
        a1 = Offloaded(early_grads(pairs_of(1), scal, R, D, FF, 16, order), scal)
        order.expect(a1.ins)
        backward_step(1, 0)
        a1.step(order)
        send_on(0)
        order.expect(outputs.arrivals)
        backward_step(1, 1)
        outputs.step()
        layer_out = outputs.result
        c1 = Offloaded([late_grads(pairs_of(1), scal, R, D, 16, order)], scal)
        send_on(1)
        order.expect(c1.ins)
        backward_step(0, 0)
        c1.step(order)
        bounds = RowsOut(dev, [bound], 1)
        bounds.step(order)
        send_on(0)
        backward_step(0, 1)
        bounds.step(order)
        grads = Early(pairs_of(0), scal, R, D, FF, 16, order)
        a0 = Halving([grads.gate_up()], scal, "x")
        send_on(1)
        order.expect(a0.ins)
        backward_step(-1, 0)
        down = grads.down()
        order.arrive()
        bounds.step(order)
        a0.step(order)
        backward_step(-1, 1)
        lasts = RowsOut(dev, [last], 0)
        lasts.step(order)
        c0 = Halving([late_grads(pairs_of(0), scal, R, D, 16, order)], scal, "y")
        b0 = Halving([down, grads.out()], scal, "x")
        for t in (a0, b0, c0):
            order.expect(t.ins)
        order.arrive()
        lasts.step(order)
        bounds.step()
        for turn in range(3):
            if turn == 2:
                a1.last(order)
                c1.last(order)
            for t in (a0, c0, b0):
                t.step(order)
                order.expect(t.ins)
            order.arrive()
            if lasts.stage < 3:
                lasts.step(order)
        a0.step(order)
        c0.step(order)
        b0.step(order)
        order.expect(b0.ins)
        order.expect(c0.ins)
        order.arrive()
        b0.step(order)
        c0.step(order)
        lasts.step()
        input_grad = jnp.where(core == 0, lasts.result, bounds.result)
        ready = ([*a0.result, *b0.result, *c0.result], [*a1.result, *c1.result])
        outs = joined(core == 0, ready, D)
    return (layer_out[None], input_grad[None], *[t.reshape(1, -1) for t in outs])


def joined(first, done, D):
    outs = []
    for zero, one in zip(*done):
        got_zero = lax.ppermute(zero, "section", [(1, 0)])
        got_one = lax.ppermute(one, "section", [(0, 1)])
        outs.append((jnp.where(first, zero, got_one), jnp.where(first, got_zero, one)))
    (gate, up), down, out, late = outs
    rows = D // 16
    gate, up = gate[:rows], up[:rows]
    down = jnp.concatenate(down, axis=0)
    out = jnp.concatenate([t[:rows, : D // 2] for t in out], axis=1)
    gain = late[0][rows, : 2 * D // 16]
    qkv = jnp.concatenate([t[:rows, : D // 2 + KVD] for t in late], axis=1)
    return [gain, qkv[:, :D], qkv[:, D : D + KVD], qkv[:, D + KVD :], out, gate, up, down]


def plain_sums(layers, R, D):
    gains = [
        jnp.concatenate([sum(t["gain1"][0] for t in its), sum(t["gain2"][0] for t in its)])
        for its in layers
    ]

    def inner(pairs):
        left = jnp.concatenate([a for a, _ in pairs], axis=0)
        right = jnp.concatenate([b for _, b in pairs], axis=0)
        return lax.dot_general(left, right, (((0,), (0,)), ((), ())), preferred_element_type=F32)

    flat = []
    wide = lambda t: t.transpose(1, 0, 2).reshape(R, GQ * SLAB)
    for layer in range(2):
        its = layers[layer]
        gq = inner([(t["normed"], wide(t["qg"])) for t in its])
        gq = gq.reshape(D, GQ, SLAB)[:, :, :KVD].reshape(D, GQ, KV, HD).transpose(0, 2, 1, 3)
        gkv = inner([(t["normed"], t["kvg"]) for t in its])
        go = inner([(wide(t["att"]), t["og"]) for t in its])
        go = go.reshape(GQ, SLAB, D)[:, VOFF:, :].reshape(GQ, KV, HD, D).transpose(1, 0, 2, 3)
        gg = inner([(t["n2"], t["gg"]) for t in its])
        gu = inner([(t["n2"], t["ug"]) for t in its])
        gd = inner([(t["act"], t["dg"]) for t in its])
        flat.append(
            [gains[layer]]
            + [t.reshape(-1).astype(BF16) for t in (gq, gkv[:, :KVD], gkv[:, KVD:], go, gg, gu, gd)]
        )
    outs = []
    for a, b in zip(*flat):
        both = lax.psum_scatter(jnp.stack([a, b]), "section", scatter_dimension=0, tiled=True)
        own = lax.psum_scatter(both.reshape(-1), ("seq", "dp"), scatter_dimension=0, tiled=True)
        outs.append(own.astype(F32))
    return outs


def solution(mesh):
    placed = (
        P("dp", "seq", None),
        P("dp", "seq", None),
        P("dp", None),
        P("dp"),
        P("section", None),
        P("section", None, None),
        P("section", None, None),
        P("section", None, None),
        P("section", None, None),
        P("section", None),
        P("section", None, None),
        P("section", None, None),
        P("section", None, None),
    )
    return jax.shard_map(
        per_device,
        mesh=mesh,
        in_specs=placed,
        out_specs=(
            P("section", "dp", "seq", None),
            P("section", "dp", "seq", None),
        )
        + (P("section", ("seq", "dp")),) * 8,
        check_vma=False,
    )
```

time: 875 us -> 715 us (0.82)
  local copies, waits for them, and re-layouts: 81 us -> 33.7 us
  waiting for transfers between devices: 118 us -> 78.7 us
  starting transfers between devices: 199 us -> 162 us
  other arithmetic: 64.4 us -> 36.3 us
    ppermute x117 -> x83, starting transfers between devices: 102 us -> 69.7 us  [the longest x12 17.6 us: step(): self.ins = [lax.ppermute(parts[1], ('seq', 'dp')[axis - 1], pairs)]]
    ppermute x25 -> x21, waiting for transfers between devices: 33.8 us -> 17.8 us  [along_x(): return lax.ppermute(t, 'dp', [(i, i ^ 1) for i in range(4)])]
    convert_element_type x31 -> x9, other arithmetic: 27.4 us -> 11.5 us  [the longest x8 11.4 us: scattered(): part = [(at(keep, m) + at(got, m)).astype(BF16) for m in range(4)]]
    ppermute x16, starting transfers between devices: 30.3 us -> 18.6 us  [diagonal(): return lax.ppermute(t, ('seq', 'dp'), pairs)]
    ppermute x16, waiting for transfers between devices: 19 us -> 7.69 us  [diagonal(): return lax.ppermute(t, ('seq', 'dp'), pairs)]
    ppermute x16, waiting for transfers between devices: 14.3 us -> 3.19 us  [along_z(): return lax.ppermute(t, 'seq', [(i, i ^ 1) for i in range(4)])]
    reshape x11 -> x5, local copies, waits for them, and re-layouts: 14.4 us -> 3.87 us  [per_device(): t.reshape(1, -1)]
    pallas_call x22 -> x45, Pallas kernels: 352 us -> 346 us  [call(): pl.pallas_call(body, out_shape=outs, in_specs=[spec[c]() for c in spaces]...]
  transfers between devices with their start and end apart: 182 -> 144, of which waited for: 42 -> 21; matrix products, arithmetic and copies ran while one was open for 15% -> 7% of each run, Pallas kernels for 45% -> 49%
where the time goes in v2:
time: 715 us; the launch traced here: 703 us
  Pallas kernels  376 us (53%)
  starting transfers between devices  162 us (23%)
  waiting for transfers between devices  78.7 us (11%)
  other arithmetic  36.3 us (5%)
  local copies, waits for them, and re-layouts  33.7 us (5%)
  between operations  16.4 us (2%)
    pallas_call x45, Pallas kernels, call(): pl.pallas_call(body, out_shape=outs, in_specs=[spec[c]() for c in spaces]...  346 us
    ppermute x21, starting transfers between devices, along_x(): return lax.ppermute(t, 'dp', [(i, i ^ 1) for i in range(4)])  30.6 us
    pallas_call x4, Pallas kernels, grid_call(): pl.pallas_call(body, out_shape=outs, grid=grid, in_specs=[SM()] + in_spec...  30.4 us
    ppermute x12, waiting for transfers between devices, step(): self.ins = [lax.ppermute(parts[1], ('seq', 'dp')[axis - 1], pairs)]  29.7 us
    ppermute x4, starting transfers between devices, mirrored(): return lax.ppermute(t, 'seq', [(i, 3 - i) for i in range(4)])  22 us
    ppermute x16, starting transfers between devices, along_z(): return lax.ppermute(t, 'seq', [(i, i ^ 1) for i in range(4)])  20.6 us
    ppermute x16, starting transfers between devices, diagonal(): return lax.ppermute(t, ('seq', 'dp'), pairs)  18.6 us
    unnamed x294, local copies, waits for them, and re-layouts  18.5 us
  transfers between devices with their start and end apart: 144, of which 21 were waited for; matrix products, arithmetic and copies ran while one was open for 7% of the time, Pallas kernels for 49%

profile of v2, /device:TPU:0, one launch (start us, length us, event | category | flops | bytes accessed | tf_op | source)
XLA Modules:
  0.0 703.4 jit_solution(2102972437354927144)
XLA Ops:
  52.6 9.1 %collective-permute-done.4.refs_2_ = bf16[576,128]{1,0:T(8,128)(2,1)S(1)} collective-permute-done((bf16[576,128]{1,0:T(8,128)(2,1)S(1)}, bf16[576,128]{1,0:T(8,128)(2,1)S(1)}, u32[]{:S(2)}, u32[]{:S(2)}) %collective-permute-start.4) | collective-permute-done | bytes 147488 | tf_op jit(solution)/shard_map/ppermute | solution.py:1196
  73.6 10.9 %forward.8 = (f32[256,576]{1,0:T(8,128)}, f32[256,576]{1,0:T(8,128)}, bf16[3,256,256]{2,1,0:T(8,128)(2,1)}, bf16[256,1536]{1,0:T(8,128)(2,1)}, bf16[256,1536]{1,...) custom-call(s32[3]{0:T(128)} %pad_add_fusion.1.scal.refs_0_, ...), custom_call_target="tpu_custom_call" | custom-call | flops 56623104 | bytes 1000 | tf_op jit(solution)/shard_map/forward/pallas_call | solution.py:674
  90.0 13.5 %forward.9 = (f32[256,576]{1,0:T(8,128)}, f32[256,576]{1,0:T(8,128)}, bf16[3,256,256]{2,1,0:T(8,128)(2,1)}, bf16[256,1536]{1,0:T(8,128)(2,1)}, bf16[256,1536]{1,...) custom-call(s32[3]{0:T(128)} %pad_add_fusion.1.scal.refs_0_, ...), custom_call_target="tpu_custom_call" | custom-call | flops 56623104 | bytes 1000 | tf_op jit(solution)/shard_map/forward/pallas_call | solution.py:674
  108.9 11.3 %forward.10 = (f32[256,576]{1,0:T(8,128)}, f32[256,576]{1,0:T(8,128)}, bf16[3,256,256]{2,1,0:T(8,128)(2,1)}, bf16[256,1536]{1,0:T(8,128)(2,1)}, bf16[256,1536]{1...) custom-call(s32[3]{0:T(128)} %pad_add_fusion.1.scal.refs_0_, ...), custom_call_target="tpu_custom_call" | custom-call | flops 56623104 | bytes 1000 | tf_op jit(solution)/shard_map/forward/pallas_call | solution.py:674
  125.7 13.6 %forward.11 = (f32[256,576]{1,0:T(8,128)}, f32[256,576]{1,0:T(8,128)}, bf16[3,256,256]{2,1,0:T(8,128)(2,1)}, bf16[256,1536]{1,0:T(8,128)(2,1)}, bf16[256,1536]{1...) custom-call(s32[3]{0:T(128)} %pad_add_fusion.1.scal.refs_0_, ...), custom_call_target="tpu_custom_call" | custom-call | flops 56623104 | bytes 1000 | tf_op jit(solution)/shard_map/forward/pallas_call | solution.py:674
  144.6 11.1 %forward.12 = (f32[256,576]{1,0:T(8,128)}, f32[256,576]{1,0:T(8,128)}, bf16[3,256,256]{2,1,0:T(8,128)(2,1)}, bf16[256,1536]{1,0:T(8,128)(2,1)}, bf16[256,1536]{1...) custom-call(s32[3]{0:T(128)} %pad_add_fusion.1.scal.refs_0_, ...), custom_call_target="tpu_custom_call" | custom-call | flops 56623104 | bytes 1000 | tf_op jit(solution)/shard_map/forward/pallas_call | solution.py:674
  163.6 13.7 %forward.13 = (f32[256,576]{1,0:T(8,128)}, f32[256,576]{1,0:T(8,128)}, bf16[3,256,256]{2,1,0:T(8,128)(2,1)}, bf16[256,1536]{1,0:T(8,128)(2,1)}, bf16[256,1536]{1...) custom-call(s32[3]{0:T(128)} %pad_add_fusion.1.scal.refs_0_, ...), custom_call_target="tpu_custom_call" | custom-call | flops 56623104 | bytes 1000 | tf_op jit(solution)/shard_map/forward/pallas_call | solution.py:674
  185.0 9.9 %forward.14 = (f32[256,576]{1,0:T(8,128)}, f32[256,576]{1,0:T(8,128)}, bf16[3,256,256]{2,1,0:T(8,128)(2,1)}, bf16[256,1536]{1,0:T(8,128)(2,1)}, bf16[256,1536]{1...) custom-call(s32[3]{0:T(128)} %pad_add_fusion.1.scal.refs_0_, s32[2,9]{1,0:T(2,128)} %copy-done.97, ...), custom_call_target="tpu_custom_call" | custom-call | flops 56623104 | bytes 1000 | tf_op jit(solution)/shard_map/forward/pallas_call | solution.py:674
  195.6 15.4 %backward.10 = (f32[256,576]{1,0:T(8,128)}, bf16[256,576]{1,0:T(8,128)(2,1)}, bf16[256,1536]{1,0:T(8,128)(2,1)}, bf16[256,1536]{1,0:T(8,128)(2,1)}, bf16[256,153...) custom-call(s32[3]{0:T(128)} %pad_add_fusion.1.scal.refs_0_, ...), custom_call_target="tpu_custom_call" | custom-call | flops 113246208 | bytes 1000 | tf_op jit(solution)/shard_map/backward/pallas_call | solution.py:674
  234.4 11.6 %collective-permute-start.2 = (bf16[576,128]{1,0:T(8,128)(2,1)S(1)}, bf16[576,128]{1,0:T(8,128)(2,1)S(1)}, u32[]{:S(2)}, u32[]{:S(2)}) collective-permute-start(bf16[576,128]{1,0:T(8,128)(2,1)S(1)} %get-tuple-element.808), channel_id=1, source_target_pairs={{0,12},{4,8},{8,4},{12,0},{1,13},{5,9},{9,5},{13,1},{2,14},{6,10},... | collective-permute-start | bytes 442376 | tf_op jit(solution)/shard_map/ppermute | solution.py:1196
  246.7 12.7 %forward.15 = (f32[256,576]{1,0:T(8,128)}, f32[256,576]{1,0:T(8,128)}, bf16[3,256,256]{2,1,0:T(8,128)(2,1)}, bf16[256,1536]{1,0:T(8,128)(2,1)}, bf16[256,1536]{1...) custom-call(s32[3]{0:T(128)} %pad_add_fusion.1.scal.refs_0_, s32[2,9]{1,0:T(2,128)} %copy-done.97, ...), custom_call_target="tpu_custom_call" | custom-call | flops 56623104 | bytes 1000 | tf_op jit(solution)/shard_map/forward/pallas_call | solution.py:674
  260.1 22.3 %backward.11 = (f32[256,576]{1,0:T(8,128)}, bf16[256,576]{1,0:T(8,128)(2,1)}, bf16[256,1536]{1,0:T(8,128)(2,1)}, bf16[256,1536]{1,0:T(8,128)(2,1)}, bf16[256,153...) custom-call(s32[3]{0:T(128)} %pad_add_fusion.1.scal.refs_0_, ...), custom_call_target="tpu_custom_call" | custom-call | flops 113246208 | bytes 1000 | tf_op jit(solution)/shard_map/backward/pallas_call | solution.py:674
  289.5 16.8 %backward.12 = (bf16[256,384]{1,0:T(8,128)(2,1)}, bf16[256,576]{1,0:T(8,128)(2,1)}, f32[8,576]{1,0:T(8,128)}, f32[256,576]{1,0:T(8,128)}, bf16[256,576]{1,0:T(8,...) custom-call(s32[3]{0:T(128)} %pad_add_fusion.1.scal.refs_0_, ...), custom_call_target="tpu_custom_call" | custom-call | flops 113246208 | bytes 1000 | tf_op jit(solution)/shard_map/backward/pallas_call | solution.py:674
  313.4 23.4 %backward.13 = (bf16[256,384]{1,0:T(8,128)(2,1)}, bf16[256,576]{1,0:T(8,128)(2,1)}, f32[8,576]{1,0:T(8,128)}, f32[256,576]{1,0:T(8,128)}, bf16[256,576]{1,0:T(8,...) custom-call(s32[3]{0:T(128)} %pad_add_fusion.1.scal.refs_0_, ...), custom_call_target="tpu_custom_call" | custom-call | flops 113246208 | bytes 1000 | tf_op jit(solution)/shard_map/backward/pallas_call | solution.py:674
  341.7 8.7 %gate_up_grads.2 = (bf16[16,40,1536]{2,1,0:T(8,128)(2,1)}, bf16[16,40,1536]{2,1,0:T(8,128)(2,1)}) custom-call(s32[3]{0:T(128)} %pad_add_fusion.1.scal.refs_0_, bf16[256,576]{1,0:T(8,128)(2,1)} %get-tuple-element.539.refs_1_, bf16[256,576]{1,0:T(8,128)(2,1)} %get-tuple-element.540.refs_2_, bf16[256,576]{1,0:T(8,128)(2,1)} %get-tuple-element.541.refs_3_, ...), custom_call_target="tpu_custom_call" | custom-call | flops 56623104 | bytes 1000 | tf_op jit(solution)/shard_map/gate_up_grads/pallas_call | solution.py:862
  350.6 6.4 down_grads.2
  370.4 16.7 %backward.14 = (bf16[256,384]{1,0:T(8,128)(2,1)}, bf16[256,576]{1,0:T(8,128)(2,1)}, f32[8,576]{1,0:T(8,128)}, bf16[576,256]{1,0:T(8,128)(2,1)}, f32[256,576]{1,0...) custom-call(s32[3]{0:T(128)} %pad_add_fusion.1.scal.refs_0_, ...), custom_call_target="tpu_custom_call" | custom-call | flops 113246208 | bytes 1000 | tf_op jit(solution)/shard_map/backward/pallas_call | solution.py:674
  402.6 24.0 %backward.15 = (bf16[256,384]{1,0:T(8,128)(2,1)}, bf16[256,576]{1,0:T(8,128)(2,1)}, f32[8,576]{1,0:T(8,128)}, bf16[576,256]{1,0:T(8,128)(2,1)}, f32[256,576]{1,0...) custom-call(s32[3]{0:T(128)} %pad_add_fusion.1.scal.refs_0_, ...), custom_call_target="tpu_custom_call" | custom-call | flops 113246208 | bytes 1000 | tf_op jit(solution)/shard_map/backward/pallas_call | solution.py:674
  441.2 16.8 %backward.16 = (bf16[256,384]{1,0:T(8,128)(2,1)}, bf16[256,576]{1,0:T(8,128)(2,1)}, f32[8,576]{1,0:T(8,128)}, f32[256,576]{1,0:T(8,128)}, bf16[256,576]{1,0:T(8,...) custom-call(s32[3]{0:T(128)} %pad_add_fusion.1.scal.refs_0_, ...), custom_call_target="tpu_custom_call" | custom-call | flops 113246208 | bytes 1000 | tf_op jit(solution)/shard_map/backward/pallas_call | solution.py:674
  469.7 23.3 %backward.17 = (bf16[256,384]{1,0:T(8,128)(2,1)}, bf16[256,576]{1,0:T(8,128)(2,1)}, f32[8,576]{1,0:T(8,128)}, f32[256,576]{1,0:T(8,128)}, bf16[256,576]{1,0:T(8,...) custom-call(s32[3]{0:T(128)} %pad_add_fusion.1.scal.refs_0_, ...), custom_call_target="tpu_custom_call" | custom-call | flops 113246208 | bytes 1000 | tf_op jit(solution)/shard_map/backward/pallas_call | solution.py:674
  493.2 8.8 %gate_up_grads.3 = (bf16[16,40,1536]{2,1,0:T(8,128)(2,1)}, bf16[16,40,1536]{2,1,0:T(8,128)(2,1)}) custom-call(s32[3]{0:T(128)} %pad_add_fusion.1.scal.refs_0_, bf16[256,576]{1,0:T(8,128)(2,1)} %get-tuple-element.648.refs_1_, bf16[256,576]{1,0:T(8,128)(2,1)} %get-tuple-element.649.refs_2_, bf16[256,576]{1,0:T(8,128)(2,1)} %get-tuple-element.650.refs_3_, ...), custom_call_target="tpu_custom_call" | custom-call | flops 56623104 | bytes 1000 | tf_op jit(solution)/shard_map/gate_up_grads/pallas_call | solution.py:862
  513.2 6.4 down_grads.3
  519.6 10.9 %collective-permute-start.116 = (bf16[16,48,576]{2,1,0:T(8,128)(2,1)}, bf16[16,48,576]{2,1,0:T(8,128)(2,1)}, u32[]{:S(2)}, u32[]{:S(2)}) collective-permute-start(bf16[16,48,576]{2,1,0:T(8,128)(2,1)} %get-tuple-element.700), channel_id=1, source_target_pairs={{0,16},{16,0},{1,17},{17,1},{2,18},{18,2},{3,19},{19,3},{4,20},{20... | collective-permute-start | bytes 2654216 | tf_op jit(solution)/shard_map/ppermute | solution.py:1013
  594.0 19.4 %collective-permute-done.121.refs_2_ = bf16[8,192,128]{2,1,0:T(8,128)(2,1)S(1)} collective-permute-done((bf16[8,192,128]{2,1,0:T(8,128)(2,1)S(1)}, bf16[8,192,128]{2,1,0:T(8,128)(2,1)S(1)}, u32[]{:S(2)}, u32[]{:S(2)}) %collective-permute-start.121) | collective-permute-done | bytes 393248 | tf_op jit(solution)/shard_map/ppermute | solution.py:1040
  (681 shorter events, 350.1 us)
Async XLA Ops:
  7.2 578.2 %reduce-scatter.11.cloned.1.call-start = ((), (), s32[]{:S(2)}) async-start(), calls=%async_computation.6 | async-start | bytes 4300800 | tf_op jit(solution)/shard_map/reduce_scatter | solution.py:997
  7.2 33.6 %collective-permute-start.7 = (bf16[576,1536]{1,0:T(8,128)(2,1)}, bf16[576,1536]{1,0:T(8,128)(2,1)S(1)}, u32[]{:S(2)}, u32[]{:S(2)}) collective-permute-start(bf16[576,1536]{1,0:T(8,128)(2,1)} %bitcast.80), channel_id=1, source_target_pairs={{0,16},{16,0},{1,17},{17,1},{2,18},{18,2},{3,19},{19,3},{4,20},{20... | collective-permute-start | bytes 5308424 | tf_op jit(solution)/shard_map/ppermute | solution.py:1335
  7.7 33.1 %collective-permute-start.8 = (bf16[576,1536]{1,0:T(8,128)(2,1)}, bf16[576,1536]{1,0:T(8,128)(2,1)S(1)}, u32[]{:S(2)}, u32[]{:S(2)}) collective-permute-start(bf16[576,1536]{1,0:T(8,128)(2,1)} %bitcast.97), channel_id=1, source_target_pairs={{0,16},{16,0},{1,17},{17,1},{2,18},{18,2},{3,19},{19,3},{4,20},{20... | collective-permute-start | bytes 5308424 | tf_op jit(solution)/shard_map/ppermute | solution.py:1335
  7.8 33.1 %collective-permute-start.9 = (bf16[576,1536]{1,0:T(8,128)(2,1)}, bf16[576,1536]{1,0:T(8,128)(2,1)}, u32[]{:S(2)}, u32[]{:S(2)}) collective-permute-start(bf16[576,1536]{1,0:T(8,128)(2,1)} %bitcast.114), channel_id=1, source_target_pairs={{0,16},{16,0},{1,17},{17,1},{2,18},{18,2},{3,19},{19,3},{4,20},{20... | collective-permute-start | bytes 5308424 | tf_op jit(solution)/shard_map/ppermute | solution.py:1335
  230.2 52.3 %collective-permute-start.72 = (bf16[256,384]{1,0:T(8,128)(2,1)}, bf16[256,384]{1,0:T(8,128)(2,1)S(1)}, u32[]{:S(2)}, u32[]{:S(2)}) collective-permute-start(bf16[256,384]{1,0:T(8,128)(2,1)} %get-tuple-element.792), channel_id=1, source_target_pairs={{0,1},{1,0},{2,3},{3,2},{4,5},{5,4},{6,7},{7,6},{8,9},{9,8},{10,11... | collective-permute-start | bytes 589832 | tf_op jit(solution)/shard_map/ppermute | solution.py:1186
  231.8 50.7 %collective-permute-start.73 = (bf16[256,384]{1,0:T(8,128)(2,1)}, bf16[256,384]{1,0:T(8,128)(2,1)S(1)}, u32[]{:S(2)}, u32[]{:S(2)}) collective-permute-start(bf16[256,384]{1,0:T(8,128)(2,1)} %get-tuple-element.791), channel_id=1, source_target_pairs={{0,4},{4,0},{8,12},{12,8},{1,5},{5,1},{9,13},{13,9},{2,6},{6,2},{1... | collective-permute-start | bytes 589832 | tf_op jit(solution)/shard_map/ppermute | solution.py:1189
  233.6 48.9 %collective-permute-start.74 = (bf16[256,384]{1,0:T(8,128)(2,1)S(1)}, bf16[256,384]{1,0:T(8,128)(2,1)S(1)}, u32[]{:S(2)}, u32[]{:S(2)}) collective-permute-start(bf16[256,384]{1,0:T(8,128)(2,1)S(1)} %get-tuple-element.790), channel_id=1, source_target_pairs={{0,5},{1,4},{2,7},{3,6},{4,1},{5,0},{6,3},{7,2},{8,13},{9,12},{10,... | collective-permute-start | bytes 589832 | tf_op jit(solution)/shard_map/ppermute | solution.py:1193
  307.6 29.2 %collective-permute-start.81 = (bf16[2,576,256]{2,1,0:T(8,128)(2,1)S(1)}, bf16[2,576,256]{2,1,0:T(8,128)(2,1)S(1)}, u32[]{:S(2)}, u32[]{:S(2)}) collective-permute-start(bf16[2,576,256]{2,1,0:T(8,128)(2,1)S(1)} %broadcast_select_fusion.25), channel_id=1, source_target_pairs={{0,12},{4,8},{8,4},{12,0},{1,13},{5,9},{9,5},{13,1},{2,14},{6,10},... | collective-permute-start | bytes 1769480 | tf_op jit(solution)/shard_map/ppermute | solution.py:1255
  350.4 36.8 %collective-permute-start.89 = (bf16[16,40,1536]{2,1,0:T(8,128)(2,1)}, bf16[16,40,1536]{2,1,0:T(8,128)(2,1)}, u32[]{:S(2)}, u32[]{:S(2)}) collective-permute-start(bf16[16,40,1536]{2,1,0:T(8,128)(2,1)} %get-tuple-element.556), channel_id=1, source_target_pairs={{0,16},{16,0},{1,17},{17,1},{2,18},{18,2},{3,19},{19,3},{4,20},{20... | collective-permute-start | bytes 5898248 | tf_op jit(solution)/shard_map/ppermute | solution.py:981
  357.1 30.1 %collective-permute-start.90 = (bf16[16,48,576]{2,1,0:T(8,128)(2,1)}, bf16[16,48,576]{2,1,0:T(8,128)(2,1)S(1)}, u32[]{:S(2)}, u32[]{:S(2)}) collective-permute-start(bf16[16,48,576]{2,1,0:T(8,128)(2,1)} %get-tuple-element.557), channel_id=1, source_target_pairs={{0,16},{16,0},{1,17},{17,1},{2,18},{18,2},{3,19},{19,3},{4,20},{20... | collective-permute-start | bytes 2654216 | tf_op jit(solution)/shard_map/ppermute | solution.py:981
  393.9 226.2 %reduce-scatter.7.cloned.1.call-start = ((), (), s32[]{:S(2)}) async-start(), calls=%async_computation.4 | async-start | bytes 983040 | tf_op jit(solution)/shard_map/reduce_scatter | solution.py:997
  394.7 31.8 %collective-permute-start.96 = (bf16[2,576,256]{2,1,0:T(8,128)(2,1)S(1)}, bf16[2,576,256]{2,1,0:T(8,128)(2,1)S(1)}, u32[]{:S(2)}, u32[]{:S(2)}) collective-permute-start(bf16[2,576,256]{2,1,0:T(8,128)(2,1)S(1)} %broadcast_select_fusion.12), channel_id=1, source_target_pairs={{0,1},{1,0},{2,3},{3,2},{4,5},{5,4},{6,7},{7,6},{8,9},{9,8},{10,11... | collective-permute-start | bytes 1769480 | tf_op jit(solution)/shard_map/ppermute | solution.py:1255
  397.9 28.7 %collective-permute-start.93 = (bf16[256,384]{1,0:T(8,128)(2,1)}, bf16[256,384]{1,0:T(8,128)(2,1)S(1)}, u32[]{:S(2)}, u32[]{:S(2)}) collective-permute-start(bf16[256,384]{1,0:T(8,128)(2,1)} %get-tuple-element.776), channel_id=1, source_target_pairs={{0,1},{1,0},{2,3},{3,2},{4,5},{5,4},{6,7},{7,6},{8,9},{9,8},{10,11... | collective-permute-start | bytes 589832 | tf_op jit(solution)/shard_map/ppermute | solution.py:1186
  399.0 27.6 %collective-permute-start.94 = (bf16[256,384]{1,0:T(8,128)(2,1)}, bf16[256,384]{1,0:T(8,128)(2,1)S(1)}, u32[]{:S(2)}, u32[]{:S(2)}) collective-permute-start(bf16[256,384]{1,0:T(8,128)(2,1)} %get-tuple-element.775), channel_id=1, source_target_pairs={{0,4},{4,0},{8,12},{12,8},{1,5},{5,1},{9,13},{13,9},{2,6},{6,2},{1... | collective-permute-start | bytes 589832 | tf_op jit(solution)/shard_map/ppermute | solution.py:1189
  458.8 34.3 %collective-permute-start.103 = (bf16[2,576,256]{2,1,0:T(8,128)(2,1)S(1)}, bf16[2,576,256]{2,1,0:T(8,128)(2,1)S(1)}, u32[]{:S(2)}, u32[]{:S(2)}) collective-permute-start(bf16[2,576,256]{2,1,0:T(8,128)(2,1)S(1)} %pad_maximum_fusion.4), channel_id=1, source_target_pairs={{0,16},{1,17},{2,18},{3,19},{4,20},{5,21},{6,22},{7,23},{8,24},{9,... | collective-permute-start | bytes 1769480 | tf_op jit(solution)/shard_map/ppermute | solution.py:1268
  462.1 31.0 %collective-permute-start.104 = (bf16[256,384]{1,0:T(8,128)(2,1)}, bf16[256,384]{1,0:T(8,128)(2,1)S(1)}, u32[]{:S(2)}, u32[]{:S(2)}) collective-permute-start(bf16[256,384]{1,0:T(8,128)(2,1)} %get-tuple-element.768), channel_id=1, source_target_pairs={{0,1},{1,0},{2,3},{3,2},{4,5},{5,4},{6,7},{7,6},{8,9},{9,8},{10,11... | collective-permute-start | bytes 589832 | tf_op jit(solution)/shard_map/ppermute | solution.py:1186
  464.3 28.8 %collective-permute-start.105 = (bf16[256,384]{1,0:T(8,128)(2,1)}, bf16[256,384]{1,0:T(8,128)(2,1)S(1)}, u32[]{:S(2)}, u32[]{:S(2)}) collective-permute-start(bf16[256,384]{1,0:T(8,128)(2,1)} %get-tuple-element.767), channel_id=1, source_target_pairs={{0,4},{4,0},{8,12},{12,8},{1,5},{5,1},{9,13},{13,9},{2,6},{6,2},{1... | collective-permute-start | bytes 589832 | tf_op jit(solution)/shard_map/ppermute | solution.py:1189
  502.0 41.3 %collective-permute-start.112 = (bf16[16,40,1536]{2,1,0:T(8,128)(2,1)}, bf16[16,40,1536]{2,1,0:T(8,128)(2,1)}, u32[]{:S(2)}, u32[]{:S(2)}) collective-permute-start(bf16[16,40,1536]{2,1,0:T(8,128)(2,1)} %get-tuple-element.671), channel_id=1, source_target_pairs={{0,16},{16,0},{1,17},{17,1},{2,18},{18,2},{3,19},{19,3},{4,20},{20... | collective-permute-start | bytes 5898248 | tf_op jit(solution)/shard_map/ppermute | solution.py:1013
  503.1 29.4 %collective-permute-start.108 = (bf16[2,576,256]{2,1,0:T(8,128)(2,1)S(1)}, bf16[2,576,256]{2,1,0:T(8,128)(2,1)S(1)}, u32[]{:S(2)}, u32[]{:S(2)}) collective-permute-start(bf16[2,576,256]{2,1,0:T(8,128)(2,1)S(1)} %broadcast_select_fusion.21), channel_id=1, source_target_pairs={{16,28},{20,24},{24,20},{28,16},{17,29},{21,25},{25,21},{29,17},{1... | collective-permute-start | bytes 1769480 | tf_op jit(solution)/shard_map/ppermute | solution.py:1255
  519.6 47.1 %collective-permute-start.116 = (bf16[16,48,576]{2,1,0:T(8,128)(2,1)}, bf16[16,48,576]{2,1,0:T(8,128)(2,1)}, u32[]{:S(2)}, u32[]{:S(2)}) collective-permute-start(bf16[16,48,576]{2,1,0:T(8,128)(2,1)} %get-tuple-element.700), channel_id=1, source_target_pairs={{0,16},{16,0},{1,17},{17,1},{2,18},{18,2},{3,19},{19,3},{4,20},{20... | collective-permute-start | bytes 2654216 | tf_op jit(solution)/shard_map/ppermute | solution.py:1013
  530.5 110.1 %reduce-scatter.13.cloned.1.call-start = ((), (), s32[]{:S(2)}) async-start(), calls=%async_computation.7 | async-start | bytes 1075200
  583.1 30.3 %collective-permute-start.122 = (bf16[8,360,128]{2,1,0:T(8,128)(2,1)}, bf16[8,360,128]{2,1,0:T(8,128)(2,1)}, u32[]{:S(2)}, u32[]{:S(2)}) collective-permute-start(bf16[8,360,128]{2,1,0:T(8,128)(2,1)} %get-tuple-element.714), channel_id=1, source_target_pairs={{0,1},{1,0},{2,3},{3,2},{4,5},{5,4},{6,7},{7,6},{8,9},{9,8},{10,11... | collective-permute-start | bytes 2211848 | tf_op jit(solution)/shard_map/ppermute | solution.py:1040
  585.4 59.8 %reduce-scatter.9.cloned.1.call-start = ((), (), s32[]{:S(2)}) async-start(), calls=%async_computation.5 | async-start | bytes 245760 | tf_op jit(solution)/shard_map/reduce_scatter | solution.py:997
  643.1 28.0 %collective-permute-start.136 = (f32[40,1536]{1,0:T(8,128)}, f32[40,1536]{1,0:T(8,128)}, u32[]{:S(2)}, u32[]{:S(2)}) collective-permute-start(f32[40,1536]{1,0:T(8,128)} %get-tuple-element.731.refs_2_), channel_id=1, source_target_pairs={{0,16},{1,17},{2,18},{3,19},{4,20},{5,21},{6,22},{7,23},{8,24},{9,... | collective-permute-start | bytes 737288 | tf_op jit(solution)/shard_map/ppermute | solution.py:1663
  (266 other events, 2391.2 us)
Sparse Core Ops, SparseCore 0:
  394.0 68.4 reduce-scatter.10
  530.6 30.0 reduce-scatter.6
  585.5 31.8 reduce-scatter.12
  620.2 23.4 reduce-scatter.8

commit v3 on v2

--- a/solution.py
+++ b/solution.py
@@ -677,7 +677,9 @@
         in_specs=[spec[c]() for c in spaces],
         out_specs=[(VM if in_vmem else HB)() for _ in outs],
         scratch_shapes=scratch,
-        compiler_params=pltpu.CompilerParams(vmem_limit_bytes=60 * 1024 * 1024),
+        compiler_params=pltpu.CompilerParams(
+            vmem_limit_bytes=(24 if name.startswith("sum") else 60) * 1024 * 1024
+        ),
         cost_estimate=pl.CostEstimate(flops=flops // 64, bytes_accessed=1000, transcendentals=0),
         name=name,
     )(*args)
@@ -689,6 +691,15 @@
 
 def sems(n):
     return [pltpu.SemaphoreType.DMA((n,))]
+
+
+def in_chunks(t, chunks, rows):
+    have = t.shape[0] // chunks
+    zero = jnp.zeros((rows - have, t.shape[1]), t.dtype)
+    parts = []
+    for c in range(chunks):
+        parts += [t[c * have : (c + 1) * have], zero]
+    return jnp.concatenate(parts, axis=0)
 
 
 def gate_up_kernel(scal, *refs):
@@ -699,7 +710,8 @@
     @pl.when(pl.program_id(0) == 0)
     def _():
         for i in range(4):
-            left[:, i * R : (i + 1) * R] = n2[i][...].T
+            turned = in_chunks(n2[i][...].T, *keep.shape[:2])
+            left[:, i * R : (i + 1) * R] = turned
 
     a = dot(left[...], jnp.concatenate([t[...] for t in gg], axis=0))
     b = dot(left[...], jnp.concatenate([t[...] for t in ug], axis=0))
@@ -724,14 +736,12 @@
     att, og = refs[0:4], refs[4:8]
     keep, give = refs[8:10]
     grads = jnp.concatenate([t[...] for t in og], axis=0)
-    outs = []
-    for j in range(GQ):
-        left = jnp.concatenate([t[j].T for t in att], axis=1)
-        outs.append(dot(left, grads))
-    o = jnp.concatenate(
-        [outs[j][VOFF + n * HD : VOFF + (n + 1) * HD] for n in range(KV) for j in range(GQ)],
+    slabs = [jnp.concatenate([t[j].T for t in att], axis=1) for j in range(GQ)]
+    left = jnp.concatenate(
+        [slabs[j][VOFF + n * HD : VOFF + (n + 1) * HD] for n in range(KV) for j in range(GQ)],
         axis=0,
     )
+    o = dot(in_chunks(left, *keep.shape[:2]), grads)
     half = o.shape[1] // 2
     share(scal, o[:, :half], o[:, half:], keep, give)
 
@@ -755,13 +765,14 @@
     normed, qg, kvg, gain1, gain2 = refs[0:4], refs[4:8], refs[8:12], refs[12:16], refs[16:20]
     keep, give = refs[20:22]
     left = jnp.concatenate([t[...].T for t in normed], axis=1)
+    left = in_chunks(left, *keep.shape[:2])
     slabs = [dot(left, jnp.concatenate([t[j] for t in qg], axis=0)) for j in range(GQ)]
     cols = [slabs[j][:, n * HD : (n + 1) * HD] for n in range(KV) for j in range(GQ)]
     cols.append(dot(left, jnp.concatenate([t[...] for t in kvg], axis=0)))
     w = jnp.concatenate(cols, axis=1)
     half = w.shape[1] // 2
     share(scal, w[:, :half], w[:, half:], keep, give)
-    chunks, rows = keep.shape[0], w.shape[0] // keep.shape[0]
+    chunks, rows = keep.shape[0], normed[0].shape[1] // keep.shape[0]
     zero = scal[0] == 0
     n = 2 * gain1[0].shape[1] // chunks
     for c in range(chunks):
@@ -898,7 +909,7 @@
             + [pl.BlockSpec((R, tile), lambda i: (0, i))] * 8,
             [S((chunks, rows, FF), BF16)] * 2,
             [out] * 2,
-            [pltpu.VMEM((D, 4 * R), BF16)],
+            [pltpu.VMEM((chunks * rows, 4 * R), BF16)],
             (FF // tile,),
             16 * R * D * FF,
             "gate_up_grads",
@@ -1602,24 +1613,22 @@
         backward_step(1, 1)
         outputs.step()
         layer_out = outputs.result
-        c1 = Offloaded([late_grads(pairs_of(1), scal, R, D, 16, order)], scal)
+        late1 = late_grads(pairs_of(1), scal, R, D, 16, order)
         send_on(1)
-        order.expect(c1.ins)
+        bounds = RowsOut(dev, [bound], 1)
+        bounds.step(order)
         backward_step(0, 0)
-        c1.step(order)
-        bounds = RowsOut(dev, [bound], 1)
         bounds.step(order)
         send_on(0)
         backward_step(0, 1)
-        bounds.step(order)
+        bounds.step()
         grads = Early(pairs_of(0), scal, R, D, FF, 16, order)
-        a0 = Halving([grads.gate_up()], scal, "x")
+        a0 = Halving([grads.gate_up(), late1], scal, "x")
         send_on(1)
         order.expect(a0.ins)
         backward_step(-1, 0)
         down = grads.down()
         order.arrive()
-        bounds.step(order)
         a0.step(order)
         backward_step(-1, 1)
         lasts = RowsOut(dev, [last], 0)
@@ -1634,7 +1643,6 @@
         for turn in range(3):
             if turn == 2:
                 a1.last(order)
-                c1.last(order)
             for t in (a0, c0, b0):
                 t.step(order)
                 order.expect(t.ins)
@@ -1651,7 +1659,7 @@
         c0.step(order)
         lasts.step()
         input_grad = jnp.where(core == 0, lasts.result, bounds.result)
-        ready = ([*a0.result, *b0.result, *c0.result], [*a1.result, *c1.result])
+        ready = ([a0.result[0], *b0.result, *c0.result], [*a1.result, a0.result[1]])
         outs = joined(core == 0, ready, D)
     return (layer_out[None], input_grad[None], *[t.reshape(1, -1) for t in outs])
 

time: 715 us -> 691 us (0.966)
  Pallas kernels: 376 us -> 357 us
  local copies, waits for them, and re-layouts: 33.7 us -> 41 us
    pallas_call x45 -> x43, Pallas kernels: 346 us -> 326 us  [call(): pl.pallas_call(body, out_shape=outs, in_specs=[spec[c]() for c in spaces]...]
    ppermute x16, starting transfers between devices: 18.6 us -> 36.9 us  [diagonal(): return lax.ppermute(t, ('seq', 'dp'), pairs)]
    ppermute x16, starting transfers between devices: 20.6 us -> 7.78 us  [along_z(): return lax.ppermute(t, 'seq', [(i, i ^ 1) for i in range(4)])]
    ppermute x4, starting transfers between devices: 22 us -> 9.86 us  [mirrored(): return lax.ppermute(t, 'seq', [(i, 3 - i) for i in range(4)])]
    ppermute x8, starting transfers between devices: 14.3 us -> 3.07 us  [__init__(): self.ins = [lax.ppermute(g, 'section', SWAP) for _, g in pairs]]
    unnamed x294 -> x334, local copies, waits for them, and re-layouts: 18.5 us -> 23.9 us
  transfers between devices with their start and end apart: 144 -> 142, of which waited for: 21 -> 21; matrix products, arithmetic and copies ran while one was open for 7% -> 7% of each run, Pallas kernels for 49% -> 48%
where the time goes in v3:
time: 691 us; the launch traced here: 680 us
  Pallas kernels  357 us (52%)
  starting transfers between devices  155 us (22%)
  waiting for transfers between devices  78 us (11%)
  local copies, waits for them, and re-layouts  41 us (6%)
  other arithmetic  32.4 us (5%)
  between operations  17.2 us (2%)
    pallas_call x43, Pallas kernels, call(): pl.pallas_call(body, out_shape=outs, in_specs=[spec[c]() for c in spaces]...  326 us
    ppermute x16, starting transfers between devices, diagonal(): return lax.ppermute(t, ('seq', 'dp'), pairs)  36.9 us
    pallas_call x4, Pallas kernels, grid_call(): pl.pallas_call(body, out_shape=outs, grid=grid, in_specs=[SM()] + in_spec...  31.1 us
    ppermute x12, waiting for transfers between devices, step(): self.ins = [lax.ppermute(parts[1], ('seq', 'dp')[axis - 1], pairs)]  30.8 us
    ppermute x21, starting transfers between devices, along_x(): return lax.ppermute(t, 'dp', [(i, i ^ 1) for i in range(4)])  27.8 us
    ppermute x12, starting transfers between devices, step(): self.ins = [lax.ppermute(parts[1], ('seq', 'dp')[axis - 1], pairs)]  24.2 us
    unnamed x334, local copies, waits for them, and re-layouts  23.9 us
    ppermute x6, starting transfers between devices, along(): self.arrivals = [lax.ppermute(t, axis, pairs)]  20.2 us
  transfers between devices with their start and end apart: 142, of which 21 were waited for; matrix products, arithmetic and copies ran while one was open for 7% of the time, Pallas kernels for 48%

profile of v3, /device:TPU:0, one launch (start us, length us, event | category | flops | bytes accessed | tf_op | source)
XLA Modules:
  0.0 680.3 jit_solution(12970787221361316441)
XLA Ops:
  52.5 9.1 %collective-permute-done.4.refs_2_ = bf16[576,128]{1,0:T(8,128)(2,1)S(1)} collective-permute-done((bf16[576,128]{1,0:T(8,128)(2,1)S(1)}, bf16[576,128]{1,0:T(8,128)(2,1)S(1)}, u32[]{:S(2)}, u32[]{:S(2)}) %collective-permute-start.4) | collective-permute-done | bytes 147488 | tf_op jit(solution)/shard_map/ppermute | solution.py:1207
  73.6 13.8 %forward.8 = (f32[256,576]{1,0:T(8,128)}, f32[256,576]{1,0:T(8,128)}, bf16[3,256,256]{2,1,0:T(8,128)(2,1)}, bf16[256,1536]{1,0:T(8,128)(2,1)}, bf16[256,1536]{1,...) custom-call(s32[3]{0:T(128)} %pad_add_fusion.1.scal.refs_0_, ...), custom_call_target="tpu_custom_call" | custom-call | flops 56623104 | bytes 1000 | tf_op jit(solution)/shard_map/forward/pallas_call | solution.py:674
  92.8 11.0 %forward.9 = (f32[256,576]{1,0:T(8,128)}, f32[256,576]{1,0:T(8,128)}, bf16[3,256,256]{2,1,0:T(8,128)(2,1)}, bf16[256,1536]{1,0:T(8,128)(2,1)}, bf16[256,1536]{1,...) custom-call(s32[3]{0:T(128)} %pad_add_fusion.1.scal.refs_0_, ...), custom_call_target="tpu_custom_call" | custom-call | flops 56623104 | bytes 1000 | tf_op jit(solution)/shard_map/forward/pallas_call | solution.py:674
  109.1 13.6 %forward.10 = (f32[256,576]{1,0:T(8,128)}, f32[256,576]{1,0:T(8,128)}, bf16[3,256,256]{2,1,0:T(8,128)(2,1)}, bf16[256,1536]{1,0:T(8,128)(2,1)}, bf16[256,1536]{1...) custom-call(s32[3]{0:T(128)} %pad_add_fusion.1.scal.refs_0_, ...), custom_call_target="tpu_custom_call" | custom-call | flops 56623104 | bytes 1000 | tf_op jit(solution)/shard_map/forward/pallas_call | solution.py:674
  128.1 11.1 %forward.11 = (f32[256,576]{1,0:T(8,128)}, f32[256,576]{1,0:T(8,128)}, bf16[3,256,256]{2,1,0:T(8,128)(2,1)}, bf16[256,1536]{1,0:T(8,128)(2,1)}, bf16[256,1536]{1...) custom-call(s32[3]{0:T(128)} %pad_add_fusion.1.scal.refs_0_, ...), custom_call_target="tpu_custom_call" | custom-call | flops 56623104 | bytes 1000 | tf_op jit(solution)/shard_map/forward/pallas_call | solution.py:674
  144.6 13.9 %forward.12 = (f32[256,576]{1,0:T(8,128)}, f32[256,576]{1,0:T(8,128)}, bf16[3,256,256]{2,1,0:T(8,128)(2,1)}, bf16[256,1536]{1,0:T(8,128)(2,1)}, bf16[256,1536]{1...) custom-call(s32[3]{0:T(128)} %pad_add_fusion.1.scal.refs_0_, ...), custom_call_target="tpu_custom_call" | custom-call | flops 56623104 | bytes 1000 | tf_op jit(solution)/shard_map/forward/pallas_call | solution.py:674
  165.5 11.0 %forward.13 = (f32[256,576]{1,0:T(8,128)}, f32[256,576]{1,0:T(8,128)}, bf16[3,256,256]{2,1,0:T(8,128)(2,1)}, bf16[256,1536]{1,0:T(8,128)(2,1)}, bf16[256,1536]{1...) custom-call(s32[3]{0:T(128)} %pad_add_fusion.1.scal.refs_0_, ...), custom_call_target="tpu_custom_call" | custom-call | flops 56623104 | bytes 1000 | tf_op jit(solution)/shard_map/forward/pallas_call | solution.py:674
  183.6 12.5 %forward.14 = (f32[256,576]{1,0:T(8,128)}, f32[256,576]{1,0:T(8,128)}, bf16[3,256,256]{2,1,0:T(8,128)(2,1)}, bf16[256,1536]{1,0:T(8,128)(2,1)}, bf16[256,1536]{1...) custom-call(s32[3]{0:T(128)} %pad_add_fusion.1.scal.refs_0_, s32[2,9]{1,0:T(2,128)} %copy-done.137, ...), custom_call_target="tpu_custom_call" | custom-call | flops 56623104 | bytes 1000 | tf_op jit(solution)/shard_map/forward/pallas_call | solution.py:674
  196.7 22.4 %backward.10 = (f32[256,576]{1,0:T(8,128)}, bf16[256,576]{1,0:T(8,128)(2,1)}, bf16[256,1536]{1,0:T(8,128)(2,1)}, bf16[256,1536]{1,0:T(8,128)(2,1)}, bf16[256,153...) custom-call(s32[3]{0:T(128)} %pad_add_fusion.1.scal.refs_0_, ...), custom_call_target="tpu_custom_call" | custom-call | flops 113246208 | bytes 1000 | tf_op jit(solution)/shard_map/backward/pallas_call | solution.py:674
  243.3 9.9 %forward.15 = (f32[256,576]{1,0:T(8,128)}, f32[256,576]{1,0:T(8,128)}, bf16[3,256,256]{2,1,0:T(8,128)(2,1)}, bf16[256,1536]{1,0:T(8,128)(2,1)}, bf16[256,1536]{1...) custom-call(s32[3]{0:T(128)} %pad_add_fusion.1.scal.refs_0_, s32[2,9]{1,0:T(2,128)} %copy-done.137, ...), custom_call_target="tpu_custom_call" | custom-call | flops 56623104 | bytes 1000 | tf_op jit(solution)/shard_map/forward/pallas_call | solution.py:674
  253.9 15.7 %backward.11 = (f32[256,576]{1,0:T(8,128)}, bf16[256,576]{1,0:T(8,128)(2,1)}, bf16[256,1536]{1,0:T(8,128)(2,1)}, bf16[256,1536]{1,0:T(8,128)(2,1)}, bf16[256,153...) custom-call(s32[3]{0:T(128)} %pad_add_fusion.1.scal.refs_0_, ...), custom_call_target="tpu_custom_call" | custom-call | flops 113246208 | bytes 1000 | tf_op jit(solution)/shard_map/backward/pallas_call | solution.py:674
  280.5 23.3 %backward.12 = (bf16[256,384]{1,0:T(8,128)(2,1)}, bf16[256,576]{1,0:T(8,128)(2,1)}, f32[8,576]{1,0:T(8,128)}, f32[256,576]{1,0:T(8,128)}, bf16[256,576]{1,0:T(8,...) custom-call(s32[3]{0:T(128)} %pad_add_fusion.1.scal.refs_0_, ...), custom_call_target="tpu_custom_call" | custom-call | flops 113246208 | bytes 1000 | tf_op jit(solution)/shard_map/backward/pallas_call | solution.py:674
  316.1 16.7 %backward.13 = (bf16[256,384]{1,0:T(8,128)(2,1)}, bf16[256,576]{1,0:T(8,128)(2,1)}, f32[8,576]{1,0:T(8,128)}, f32[256,576]{1,0:T(8,128)}, bf16[256,576]{1,0:T(8,...) custom-call(s32[3]{0:T(128)} %pad_add_fusion.1.scal.refs_0_, ...), custom_call_target="tpu_custom_call" | custom-call | flops 113246208 | bytes 1000 | tf_op jit(solution)/shard_map/backward/pallas_call | solution.py:674
  338.0 8.9 %gate_up_grads.2 = (bf16[16,40,1536]{2,1,0:T(8,128)(2,1)}, bf16[16,40,1536]{2,1,0:T(8,128)(2,1)}) custom-call(s32[3]{0:T(128)} %pad_add_fusion.1.scal.refs_0_, bf16[256,576]{1,0:T(8,128)(2,1)} %get-tuple-element.540.refs_1_, bf16[256,576]{1,0:T(8,128)(2,1)} %get-tuple-element.541.refs_2_, bf16[256,576]{1,0:T(8,128)(2,1)} %get-tuple-element.542.refs_3_, ...), custom_call_target="tpu_custom_call" | custom-call | flops 56623104 | bytes 1000 | tf_op jit(solution)/shard_map/gate_up_grads/pallas_call | solution.py:873
  369.5 23.8 %backward.14 = (bf16[256,384]{1,0:T(8,128)(2,1)}, bf16[256,576]{1,0:T(8,128)(2,1)}, f32[8,576]{1,0:T(8,128)}, bf16[576,256]{1,0:T(8,128)(2,1)}, f32[256,576]{1,0...) custom-call(s32[3]{0:T(128)} %pad_add_fusion.1.scal.refs_0_, ...), custom_call_target="tpu_custom_call" | custom-call | flops 113246208 | bytes 1000 | tf_op jit(solution)/shard_map/backward/pallas_call | solution.py:674
  410.4 16.9 %backward.15 = (bf16[256,384]{1,0:T(8,128)(2,1)}, bf16[256,576]{1,0:T(8,128)(2,1)}, f32[8,576]{1,0:T(8,128)}, bf16[576,256]{1,0:T(8,128)(2,1)}, f32[256,576]{1,0...) custom-call(s32[3]{0:T(128)} %pad_add_fusion.1.scal.refs_0_, ...), custom_call_target="tpu_custom_call" | custom-call | flops 113246208 | bytes 1000 | tf_op jit(solution)/shard_map/backward/pallas_call | solution.py:674
  444.4 23.9 %backward.16 = (bf16[256,384]{1,0:T(8,128)(2,1)}, bf16[256,576]{1,0:T(8,128)(2,1)}, f32[8,576]{1,0:T(8,128)}, f32[256,576]{1,0:T(8,128)}, bf16[256,576]{1,0:T(8,...) custom-call(s32[3]{0:T(128)} %pad_add_fusion.1.scal.refs_0_, ...), custom_call_target="tpu_custom_call" | custom-call | flops 113246208 | bytes 1000 | tf_op jit(solution)/shard_map/backward/pallas_call | solution.py:674
  475.3 20.9 %backward.17 = (bf16[256,384]{1,0:T(8,128)(2,1)}, bf16[256,576]{1,0:T(8,128)(2,1)}, f32[8,576]{1,0:T(8,128)}, f32[256,576]{1,0:T(8,128)}, bf16[256,576]{1,0:T(8,...) custom-call(s32[3]{0:T(128)} %pad_add_fusion.1.scal.refs_0_, ...), custom_call_target="tpu_custom_call" | custom-call | flops 113246208 | bytes 1000 | tf_op jit(solution)/shard_map/backward/pallas_call | solution.py:674
  496.3 9.2 %gate_up_grads.3 = (bf16[16,40,1536]{2,1,0:T(8,128)(2,1)}, bf16[16,40,1536]{2,1,0:T(8,128)(2,1)}) custom-call(s32[3]{0:T(128)} %pad_add_fusion.1.scal.refs_0_, bf16[256,576]{1,0:T(8,128)(2,1)} %get-tuple-element.648.refs_1_, bf16[256,576]{1,0:T(8,128)(2,1)} %get-tuple-element.649.refs_2_, bf16[256,576]{1,0:T(8,128)(2,1)} %get-tuple-element.650.refs_3_, ...), custom_call_target="tpu_custom_call" | custom-call | flops 56623104 | bytes 1000 | tf_op jit(solution)/shard_map/gate_up_grads/pallas_call | solution.py:873
  521.4 6.6 down_grads.3
  556.2 9.1 %collective-permute-done.114.refs_2_ = bf16[8,672,128]{2,1,0:T(8,128)(2,1)S(1)} collective-permute-done((bf16[8,672,128]{2,1,0:T(8,128)(2,1)}, bf16[8,672,128]{2,1,0:T(8,128)(2,1)S(1)}, u32[]{:S(2)}, u32[]{:S(2)}) %collective-permute-start.114) | collective-permute-done | bytes 1376288 | tf_op jit(solution)/shard_map/ppermute | solution.py:1051
  577.5 9.7 %collective-permute-start.118 = (bf16[2,576,256]{2,1,0:T(8,128)(2,1)S(1)}, bf16[2,576,256]{2,1,0:T(8,128)(2,1)S(1)}, u32[]{:S(2)}, u32[]{:S(2)}) collective-permute-start(bf16[2,576,256]{2,1,0:T(8,128)(2,1)S(1)} %broadcast_select_fusion.20), channel_id=1, source_target_pairs={{0,12},{4,8},{8,4},{12,0},{1,13},{5,9},{9,5},{13,1},{2,14},{6,10},... | collective-permute-start | bytes 1769480 | tf_op jit(solution)/shard_map/ppermute | solution.py:1266
  590.2 11.0 %collective-permute-done.120.refs_2_ = bf16[8,192,128]{2,1,0:T(8,128)(2,1)S(1)} collective-permute-done((bf16[8,192,128]{2,1,0:T(8,128)(2,1)S(1)}, bf16[8,192,128]{2,1,0:T(8,128)(2,1)S(1)}, u32[]{:S(2)}, u32[]{:S(2)}) %collective-permute-start.120) | collective-permute-done | bytes 393248 | tf_op jit(solution)/shard_map/ppermute | solution.py:1051
  611.1 8.5 %collective-permute-start.123 = (bf16[2,672,128]{2,1,0:T(8,128)(2,1)S(1)}, bf16[2,672,128]{2,1,0:T(8,128)(2,1)S(1)}, u32[]{:S(2)}, u32[]{:S(2)}) collective-permute-start(bf16[2,672,128]{2,1,0:T(8,128)(2,1)S(1)} %get-tuple-element.723), channel_id=1, source_target_pairs={{0,4},{4,0},{8,12},{12,8},{1,5},{5,1},{9,13},{13,9},{2,6},{6,2},{1... | collective-permute-start | bytes 1032200 | tf_op jit(solution)/shard_map/ppermute | solution.py:1051
  (713 shorter events, 330.9 us)
Async XLA Ops:
  7.2 568.7 %reduce-scatter.5.cloned.1.call-start = ((), (), s32[]{:S(2)}) async-start(), calls=%async_computation.2 | async-start | bytes 4300800 | tf_op jit(solution)/shard_map/reduce_scatter | solution.py:1008
  7.2 33.6 %collective-permute-start.7 = (bf16[576,1536]{1,0:T(8,128)(2,1)}, bf16[576,1536]{1,0:T(8,128)(2,1)S(1)}, u32[]{:S(2)}, u32[]{:S(2)}) collective-permute-start(bf16[576,1536]{1,0:T(8,128)(2,1)} %bitcast.79), channel_id=1, source_target_pairs={{0,16},{16,0},{1,17},{17,1},{2,18},{18,2},{3,19},{19,3},{4,20},{20... | collective-permute-start | bytes 5308424 | tf_op jit(solution)/shard_map/ppermute | solution.py:1346
  7.7 33.1 %collective-permute-start.8 = (bf16[576,1536]{1,0:T(8,128)(2,1)}, bf16[576,1536]{1,0:T(8,128)(2,1)S(1)}, u32[]{:S(2)}, u32[]{:S(2)}) collective-permute-start(bf16[576,1536]{1,0:T(8,128)(2,1)} %bitcast.96), channel_id=1, source_target_pairs={{0,16},{16,0},{1,17},{17,1},{2,18},{18,2},{3,19},{19,3},{4,20},{20... | collective-permute-start | bytes 5308424 | tf_op jit(solution)/shard_map/ppermute | solution.py:1346
  7.8 33.0 %collective-permute-start.9 = (bf16[576,1536]{1,0:T(8,128)(2,1)}, bf16[576,1536]{1,0:T(8,128)(2,1)}, u32[]{:S(2)}, u32[]{:S(2)}) collective-permute-start(bf16[576,1536]{1,0:T(8,128)(2,1)} %bitcast.113), channel_id=1, source_target_pairs={{0,16},{16,0},{1,17},{17,1},{2,18},{18,2},{3,19},{19,3},{4,20},{20... | collective-permute-start | bytes 5308424 | tf_op jit(solution)/shard_map/ppermute | solution.py:1346
  238.3 31.3 %collective-permute-start.72 = (bf16[256,384]{1,0:T(8,128)(2,1)}, bf16[256,384]{1,0:T(8,128)(2,1)S(1)}, u32[]{:S(2)}, u32[]{:S(2)}) collective-permute-start(bf16[256,384]{1,0:T(8,128)(2,1)} %get-tuple-element.794), channel_id=1, source_target_pairs={{0,1},{1,0},{2,3},{3,2},{4,5},{5,4},{6,7},{7,6},{8,9},{9,8},{10,11... | collective-permute-start | bytes 589832 | tf_op jit(solution)/shard_map/ppermute | solution.py:1197
  239.4 30.2 %collective-permute-start.73 = (bf16[256,384]{1,0:T(8,128)(2,1)}, bf16[256,384]{1,0:T(8,128)(2,1)S(1)}, u32[]{:S(2)}, u32[]{:S(2)}) collective-permute-start(bf16[256,384]{1,0:T(8,128)(2,1)} %get-tuple-element.793), channel_id=1, source_target_pairs={{0,4},{4,0},{8,12},{12,8},{1,5},{5,1},{9,13},{13,9},{2,6},{6,2},{1... | collective-permute-start | bytes 589832 | tf_op jit(solution)/shard_map/ppermute | solution.py:1200
  239.7 29.9 %collective-permute-start.74 = (bf16[256,384]{1,0:T(8,128)(2,1)S(1)}, bf16[256,384]{1,0:T(8,128)(2,1)S(1)}, u32[]{:S(2)}, u32[]{:S(2)}) collective-permute-start(bf16[256,384]{1,0:T(8,128)(2,1)S(1)} %get-tuple-element.792), channel_id=1, source_target_pairs={{0,5},{1,4},{2,7},{3,6},{4,1},{5,0},{6,3},{7,2},{8,13},{9,12},{10,... | collective-permute-start | bytes 589832 | tf_op jit(solution)/shard_map/ppermute | solution.py:1204
  271.4 32.4 %collective-permute-start.79 = (bf16[2,576,256]{2,1,0:T(8,128)(2,1)}, bf16[2,576,256]{2,1,0:T(8,128)(2,1)S(1)}, u32[]{:S(2)}, u32[]{:S(2)}) collective-permute-start(bf16[2,576,256]{2,1,0:T(8,128)(2,1)} %broadcast_select_fusion.7), channel_id=1, source_target_pairs={{0,16},{16,0},{1,17},{17,1},{2,18},{18,2},{3,19},{19,3},{4,20},{20... | collective-permute-start | bytes 1769480 | tf_op jit(solution)/shard_map/ppermute | solution.py:1279
  273.2 30.6 %collective-permute-start.76 = (bf16[256,384]{1,0:T(8,128)(2,1)}, bf16[256,384]{1,0:T(8,128)(2,1)S(1)}, u32[]{:S(2)}, u32[]{:S(2)}) collective-permute-start(bf16[256,384]{1,0:T(8,128)(2,1)} %get-tuple-element.790), channel_id=1, source_target_pairs={{0,1},{1,0},{2,3},{3,2},{4,5},{5,4},{6,7},{7,6},{8,9},{9,8},{10,11... | collective-permute-start | bytes 589832 | tf_op jit(solution)/shard_map/ppermute | solution.py:1197
  346.8 46.6 %collective-permute-start.89 = (bf16[16,40,1536]{2,1,0:T(8,128)(2,1)}, bf16[16,40,1536]{2,1,0:T(8,128)(2,1)S(1)}, u32[]{:S(2)}, u32[]{:S(2)}) collective-permute-start(bf16[16,40,1536]{2,1,0:T(8,128)(2,1)} %get-tuple-element.557), channel_id=1, source_target_pairs={{0,16},{16,0},{1,17},{17,1},{2,18},{18,2},{3,19},{19,3},{4,20},{20... | collective-permute-start | bytes 5898248 | tf_op jit(solution)/shard_map/ppermute | solution.py:992
  353.4 39.9 %collective-permute-start.90 = (bf16[16,48,576]{2,1,0:T(8,128)(2,1)}, bf16[16,48,576]{2,1,0:T(8,128)(2,1)}, u32[]{:S(2)}, u32[]{:S(2)}) collective-permute-start(bf16[16,48,576]{2,1,0:T(8,128)(2,1)} %get-tuple-element.558), channel_id=1, source_target_pairs={{0,16},{16,0},{1,17},{17,1},{2,18},{18,2},{3,19},{19,3},{4,20},{20... | collective-permute-start | bytes 2654216 | tf_op jit(solution)/shard_map/ppermute | solution.py:992
  358.0 35.4 %collective-permute-start.91 = (bf16[16,40,384]{2,1,0:T(8,128)(2,1)}, bf16[16,40,384]{2,1,0:T(8,128)(2,1)S(1)}, u32[]{:S(2)}, u32[]{:S(2)}) collective-permute-start(bf16[16,40,384]{2,1,0:T(8,128)(2,1)} %get-tuple-element.559), channel_id=1, source_target_pairs={{0,16},{16,0},{1,17},{17,1},{2,18},{18,2},{3,19},{19,3},{4,20},{20... | collective-permute-start | bytes 1474568 | tf_op jit(solution)/shard_map/ppermute | solution.py:992
  359.9 33.4 %collective-permute-start.87 = (bf16[256,384]{1,0:T(8,128)(2,1)}, bf16[256,384]{1,0:T(8,128)(2,1)}, u32[]{:S(2)}, u32[]{:S(2)}) collective-permute-start(bf16[256,384]{1,0:T(8,128)(2,1)} %get-tuple-element.781), channel_id=1, source_target_pairs={{0,4},{4,0},{8,12},{12,8},{1,5},{5,1},{9,13},{13,9},{2,6},{6,2},{1... | collective-permute-start | bytes 589832 | tf_op jit(solution)/shard_map/ppermute | solution.py:1200
  397.4 30.0 %collective-permute-start.96 = (bf16[2,576,256]{2,1,0:T(8,128)(2,1)}, bf16[2,576,256]{2,1,0:T(8,128)(2,1)S(1)}, u32[]{:S(2)}, u32[]{:S(2)}) collective-permute-start(bf16[2,576,256]{2,1,0:T(8,128)(2,1)} %broadcast_select_fusion.12), channel_id=1, source_target_pairs={{0,1},{1,0},{2,3},{3,2},{4,5},{5,4},{6,7},{7,6},{8,9},{9,8},{10,11... | collective-permute-start | bytes 1769480 | tf_op jit(solution)/shard_map/ppermute | solution.py:1266
  403.7 225.9 %reduce-scatter.7.cloned.1.call-start = ((), (), s32[]{:S(2)}) async-start(), calls=%async_computation.3 | async-start | bytes 1075200
  431.3 37.0 %collective-permute-start.101 = (bf16[2,576,256]{2,1,0:T(8,128)(2,1)S(1)}, bf16[2,576,256]{2,1,0:T(8,128)(2,1)S(1)}, u32[]{:S(2)}, u32[]{:S(2)}) collective-permute-start(bf16[2,576,256]{2,1,0:T(8,128)(2,1)S(1)} %pad_maximum_fusion.4), channel_id=1, source_target_pairs={{0,16},{1,17},{2,18},{3,19},{4,20},{5,21},{6,22},{7,23},{8,24},{9,... | collective-permute-start | bytes 1769480 | tf_op jit(solution)/shard_map/ppermute | solution.py:1279
  435.0 33.4 %collective-permute-start.98 = (bf16[256,384]{1,0:T(8,128)(2,1)S(1)}, bf16[256,384]{1,0:T(8,128)(2,1)S(1)}, u32[]{:S(2)}, u32[]{:S(2)}) collective-permute-start(bf16[256,384]{1,0:T(8,128)(2,1)S(1)} %get-tuple-element.774), channel_id=1, source_target_pairs={{0,1},{1,0},{2,3},{3,2},{4,5},{5,4},{6,7},{7,6},{8,9},{9,8},{10,11... | collective-permute-start | bytes 589832 | tf_op jit(solution)/shard_map/ppermute | solution.py:1197
  436.6 31.8 %collective-permute-start.99 = (bf16[256,384]{1,0:T(8,128)(2,1)S(1)}, bf16[256,384]{1,0:T(8,128)(2,1)S(1)}, u32[]{:S(2)}, u32[]{:S(2)}) collective-permute-start(bf16[256,384]{1,0:T(8,128)(2,1)S(1)} %get-tuple-element.773), channel_id=1, source_target_pairs={{0,4},{4,0},{8,12},{12,8},{1,5},{5,1},{9,13},{13,9},{2,6},{6,2},{1... | collective-permute-start | bytes 589832 | tf_op jit(solution)/shard_map/ppermute | solution.py:1200
  436.6 31.8 %collective-permute-start.100 = (bf16[256,384]{1,0:T(8,128)(2,1)S(1)}, bf16[256,384]{1,0:T(8,128)(2,1)S(1)}, u32[]{:S(2)}, u32[]{:S(2)}) collective-permute-start(bf16[256,384]{1,0:T(8,128)(2,1)S(1)} %get-tuple-element.772), channel_id=1, source_target_pairs={{0,5},{1,4},{2,7},{3,6},{4,1},{5,0},{6,3},{7,2},{8,13},{9,12},{10,... | collective-permute-start | bytes 589832 | tf_op jit(solution)/shard_map/ppermute | solution.py:1204
  533.7 31.6 %collective-permute-start.114 = (bf16[8,672,128]{2,1,0:T(8,128)(2,1)}, bf16[8,672,128]{2,1,0:T(8,128)(2,1)S(1)}, u32[]{:S(2)}, u32[]{:S(2)}) collective-permute-start(bf16[8,672,128]{2,1,0:T(8,128)(2,1)} %get-tuple-element.699), channel_id=1, source_target_pairs={{0,1},{1,0},{2,3},{3,2},{4,5},{5,4},{6,7},{7,6},{8,9},{9,8},{10,11... | collective-permute-start | bytes 4128776 | tf_op jit(solution)/shard_map/ppermute | solution.py:1051
  572.6 34.2 %collective-permute-start.121 = (bf16[8,360,128]{2,1,0:T(8,128)(2,1)}, bf16[8,360,128]{2,1,0:T(8,128)(2,1)S(1)}, u32[]{:S(2)}, u32[]{:S(2)}) collective-permute-start(bf16[8,360,128]{2,1,0:T(8,128)(2,1)} %get-tuple-element.714), channel_id=1, source_target_pairs={{0,1},{1,0},{2,3},{3,2},{4,5},{5,4},{6,7},{7,6},{8,9},{9,8},{10,11... | collective-permute-start | bytes 2211848 | tf_op jit(solution)/shard_map/ppermute | solution.py:1051
  577.3 29.5 %collective-permute-start.119 = (bf16[4,672,128]{2,1,0:T(8,128)(2,1)S(1)}, bf16[4,672,128]{2,1,0:T(8,128)(2,1)S(1)}, u32[]{:S(2)}, u32[]{:S(2)}) collective-permute-start(bf16[4,672,128]{2,1,0:T(8,128)(2,1)S(1)} %copy-done.22), channel_id=1, source_target_pairs={{0,2},{1,3},{2,0},{3,1},{4,6},{5,7},{6,4},{7,5},{8,10},{9,11},{10,... | collective-permute-start | bytes 2064392 | tf_op jit(solution)/shard_map/ppermute | solution.py:1051
  577.5 29.3 %collective-permute-start.118 = (bf16[2,576,256]{2,1,0:T(8,128)(2,1)S(1)}, bf16[2,576,256]{2,1,0:T(8,128)(2,1)S(1)}, u32[]{:S(2)}, u32[]{:S(2)}) collective-permute-start(bf16[2,576,256]{2,1,0:T(8,128)(2,1)S(1)} %broadcast_select_fusion.20), channel_id=1, source_target_pairs={{0,12},{4,8},{8,4},{12,0},{1,13},{5,9},{9,5},{13,1},{2,14},{6,10},... | collective-permute-start | bytes 1769480 | tf_op jit(solution)/shard_map/ppermute | solution.py:1266
  589.5 35.9 %collective-permute-start.126 = (bf16[2,576,256]{2,1,0:T(8,128)(2,1)S(1)}, bf16[2,576,256]{2,1,0:T(8,128)(2,1)S(1)}, u32[]{:S(2)}, u32[]{:S(2)}) collective-permute-start(bf16[2,576,256]{2,1,0:T(8,128)(2,1)S(1)} %broadcast_select_fusion.8), channel_id=1, source_target_pairs={{16,17},{17,16},{18,19},{19,18},{20,21},{21,20},{22,23},{23,22},{2... | collective-permute-start | bytes 1769480 | tf_op jit(solution)/shard_map/ppermute | solution.py:1266
  (284 other events, 2418.9 us)
Sparse Core Ops, SparseCore 0:
  403.9 58.0 reduce-scatter.4
  576.0 36.5 reduce-scatter.6

commit v4 on v3

--- a/solution.py
+++ b/solution.py
@@ -229,10 +229,11 @@
     wqkv[...] = jnp.concatenate(cols, axis=1)
     for j in range(GQ):
         wout[j * SLAB : j * SLAB + VOFF, :] = jnp.zeros((VOFF, wout.shape[1]), BF16)
+        side = jnp.zeros((HD, wout.shape[1] - wo.shape[1]), BF16)
         for n in range(KV):
             h = n * GQ + j
             at = j * SLAB + VOFF + n * HD
-            wout[at : at + HD, :] = wo[h * HD : (h + 1) * HD, :]
+            wout[at : at + HD, :] = jnp.concatenate([wo[h * HD : (h + 1) * HD, :], side], axis=1)
     gains[...] = jnp.concatenate(
         [ga[...].astype(F32), gf[...].astype(F32), jnp.zeros((6, ga.shape[1]), F32)], axis=0
     )
@@ -384,7 +385,7 @@
     wout = wout()
     h = h + dot(
         jnp.concatenate([att_v[j] for j in range(GQ)], axis=1),
-        wout[...],
+        wout[:, : h.shape[1]],
     )
     h_v[...] = h
     io.store(h_v, h_out)
@@ -574,7 +575,7 @@
         wout_r, att_r = wout(), att()
         lane = lax.broadcasted_iota(jnp.int32, (1, 128), 1)
         for j in range(GQ):
-            do = dot_t(og, wout_r[j * SLAB : (j + 1) * SLAB, :]).astype(BF16)
+            do = dot_t(og, wout_r[j * SLAB : (j + 1) * SLAB, : og.shape[1]]).astype(BF16)
             prod = do.astype(F32) * att_r[j].astype(F32)
             code = jnp.zeros((R, 128), F32)
             for n in range(KV):
@@ -1337,7 +1338,7 @@
         functools.partial(pack_kernel, fast),
         [w_query[0], turn(w_key[0]), turn(w_value[0]), w_out[0], attn_gain, ffn_gain],
         "v" * 6,
-        [S((D, GQ * SLAB + 2 * KVD), BF16), S((GQ * SLAB, D), BF16), S((8, D), F32)],
+        [S((D, GQ * SLAB + 2 * KVD), BF16), S((GQ * SLAB, padded(D, 128)), BF16), S((8, D), F32)],
         [],
         1_000_000,
         "pack_weights",

time: 691 us -> 684 us (0.990)
  waiting for transfers between devices: 78 us -> 88 us
  Pallas kernels: 357 us -> 350 us
    pallas_call x43, Pallas kernels: 326 us -> 319 us  [call(): pl.pallas_call(body, out_shape=outs, in_specs=[spec[c]() for c in spaces]...]
    ppermute x12, waiting for transfers between devices: 30.8 us -> 37.9 us  [step(): self.ins = [lax.ppermute(parts[1], ('seq', 'dp')[axis - 1], pairs)]]
  transfers between devices with their start and end apart: 142 -> 142, of which waited for: 21 -> 22; matrix products, arithmetic and copies ran while one was open for 7% -> 6% of each run, Pallas kernels for 48% -> 47%
where the time goes in v4:
time: 684 us; the launch traced here: 677 us
  Pallas kernels  350 us (51%)
  starting transfers between devices  154 us (23%)
  waiting for transfers between devices  88 us (13%)
  local copies, waits for them, and re-layouts  36 us (5%)
  other arithmetic  32.3 us (5%)
  between operations  17.1 us (3%)
    pallas_call x43, Pallas kernels, call(): pl.pallas_call(body, out_shape=outs, in_specs=[spec[c]() for c in spaces]...  319 us
    ppermute x12, waiting for transfers between devices, step(): self.ins = [lax.ppermute(parts[1], ('seq', 'dp')[axis - 1], pairs)]  37.9 us
    ppermute x16, starting transfers between devices, diagonal(): return lax.ppermute(t, ('seq', 'dp'), pairs)  35.6 us
    pallas_call x4, Pallas kernels, grid_call(): pl.pallas_call(body, out_shape=outs, grid=grid, in_specs=[SM()] + in_spec...  31.1 us
    ppermute x12, starting transfers between devices, step(): self.ins = [lax.ppermute(parts[1], ('seq', 'dp')[axis - 1], pairs)]  27.6 us
    ppermute x21, starting transfers between devices, along_x(): return lax.ppermute(t, 'dp', [(i, i ^ 1) for i in range(4)])  26.8 us
    unnamed x334, local copies, waits for them, and re-layouts  23.9 us
    ppermute x21, waiting for transfers between devices, along_x(): return lax.ppermute(t, 'dp', [(i, i ^ 1) for i in range(4)])  15.8 us
  transfers between devices with their start and end apart: 142, of which 22 were waited for; matrix products, arithmetic and copies ran while one was open for 6% of the time, Pallas kernels for 47%

profile of v4, /device:TPU:0, one launch (start us, length us, event | category | flops | bytes accessed | tf_op | source)
XLA Modules:
  0.0 677.4 jit_solution(12739567977014206308)
XLA Ops:
  52.8 8.9 %collective-permute-done.4.refs_2_ = bf16[576,128]{1,0:T(8,128)(2,1)S(1)} collective-permute-done((bf16[576,128]{1,0:T(8,128)(2,1)S(1)}, bf16[576,128]{1,0:T(8,128)(2,1)S(1)}, u32[]{:S(2)}, u32[]{:S(2)}) %collective-permute-start.4) | collective-permute-done | bytes 147488 | tf_op jit(solution)/shard_map/ppermute | solution.py:1208
  71.5 13.8 %forward.8 = (f32[256,576]{1,0:T(8,128)}, f32[256,576]{1,0:T(8,128)}, bf16[3,256,256]{2,1,0:T(8,128)(2,1)}, bf16[256,1536]{1,0:T(8,128)(2,1)}, bf16[256,1536]{1,...) custom-call(s32[3]{0:T(128)} %pad_add_fusion.1.scal.refs_0_, ...), custom_call_target="tpu_custom_call" | custom-call | flops 56623104 | bytes 1000 | tf_op jit(solution)/shard_map/forward/pallas_call | solution.py:675
  90.6 10.4 %forward.9 = (f32[256,576]{1,0:T(8,128)}, f32[256,576]{1,0:T(8,128)}, bf16[3,256,256]{2,1,0:T(8,128)(2,1)}, bf16[256,1536]{1,0:T(8,128)(2,1)}, bf16[256,1536]{1,...) custom-call(s32[3]{0:T(128)} %pad_add_fusion.1.scal.refs_0_, ...), custom_call_target="tpu_custom_call" | custom-call | flops 56623104 | bytes 1000 | tf_op jit(solution)/shard_map/forward/pallas_call | solution.py:675
  106.9 13.6 %forward.10 = (f32[256,576]{1,0:T(8,128)}, f32[256,576]{1,0:T(8,128)}, bf16[3,256,256]{2,1,0:T(8,128)(2,1)}, bf16[256,1536]{1,0:T(8,128)(2,1)}, bf16[256,1536]{1...) custom-call(s32[3]{0:T(128)} %pad_add_fusion.1.scal.refs_0_, ...), custom_call_target="tpu_custom_call" | custom-call | flops 56623104 | bytes 1000 | tf_op jit(solution)/shard_map/forward/pallas_call | solution.py:675
  125.9 10.6 %forward.11 = (f32[256,576]{1,0:T(8,128)}, f32[256,576]{1,0:T(8,128)}, bf16[3,256,256]{2,1,0:T(8,128)(2,1)}, bf16[256,1536]{1,0:T(8,128)(2,1)}, bf16[256,1536]{1...) custom-call(s32[3]{0:T(128)} %pad_add_fusion.1.scal.refs_0_, ...), custom_call_target="tpu_custom_call" | custom-call | flops 56623104 | bytes 1000 | tf_op jit(solution)/shard_map/forward/pallas_call | solution.py:675
  142.4 13.9 %forward.12 = (f32[256,576]{1,0:T(8,128)}, f32[256,576]{1,0:T(8,128)}, bf16[3,256,256]{2,1,0:T(8,128)(2,1)}, bf16[256,1536]{1,0:T(8,128)(2,1)}, bf16[256,1536]{1...) custom-call(s32[3]{0:T(128)} %pad_add_fusion.1.scal.refs_0_, ...), custom_call_target="tpu_custom_call" | custom-call | flops 56623104 | bytes 1000 | tf_op jit(solution)/shard_map/forward/pallas_call | solution.py:675
  163.5 10.4 %forward.13 = (f32[256,576]{1,0:T(8,128)}, f32[256,576]{1,0:T(8,128)}, bf16[3,256,256]{2,1,0:T(8,128)(2,1)}, bf16[256,1536]{1,0:T(8,128)(2,1)}, bf16[256,1536]{1...) custom-call(s32[3]{0:T(128)} %pad_add_fusion.1.scal.refs_0_, ...), custom_call_target="tpu_custom_call" | custom-call | flops 56623104 | bytes 1000 | tf_op jit(solution)/shard_map/forward/pallas_call | solution.py:675
  179.2 12.5 %forward.14 = (f32[256,576]{1,0:T(8,128)}, f32[256,576]{1,0:T(8,128)}, bf16[3,256,256]{2,1,0:T(8,128)(2,1)}, bf16[256,1536]{1,0:T(8,128)(2,1)}, bf16[256,1536]{1...) custom-call(s32[3]{0:T(128)} %pad_add_fusion.1.scal.refs_0_, s32[2,9]{1,0:T(2,128)} %copy-done.136, ...), custom_call_target="tpu_custom_call" | custom-call | flops 56623104 | bytes 1000 | tf_op jit(solution)/shard_map/forward/pallas_call | solution.py:675
  192.3 22.4 %backward.10 = (f32[256,576]{1,0:T(8,128)}, bf16[256,576]{1,0:T(8,128)(2,1)}, bf16[256,1536]{1,0:T(8,128)(2,1)}, bf16[256,1536]{1,0:T(8,128)(2,1)}, bf16[256,153...) custom-call(s32[3]{0:T(128)} %pad_add_fusion.1.scal.refs_0_, ...), custom_call_target="tpu_custom_call" | custom-call | flops 113246208 | bytes 1000 | tf_op jit(solution)/shard_map/backward/pallas_call | solution.py:675
  240.7 9.4 %forward.15 = (f32[256,576]{1,0:T(8,128)}, f32[256,576]{1,0:T(8,128)}, bf16[3,256,256]{2,1,0:T(8,128)(2,1)}, bf16[256,1536]{1,0:T(8,128)(2,1)}, bf16[256,1536]{1...) custom-call(s32[3]{0:T(128)} %pad_add_fusion.1.scal.refs_0_, s32[2,9]{1,0:T(2,128)} %copy-done.136, ...), custom_call_target="tpu_custom_call" | custom-call | flops 56623104 | bytes 1000 | tf_op jit(solution)/shard_map/forward/pallas_call | solution.py:675
  250.8 14.2 %backward.11 = (f32[256,576]{1,0:T(8,128)}, bf16[256,576]{1,0:T(8,128)(2,1)}, bf16[256,1536]{1,0:T(8,128)(2,1)}, bf16[256,1536]{1,0:T(8,128)(2,1)}, bf16[256,153...) custom-call(s32[3]{0:T(128)} %pad_add_fusion.1.scal.refs_0_, ...), custom_call_target="tpu_custom_call" | custom-call | flops 113246208 | bytes 1000 | tf_op jit(solution)/shard_map/backward/pallas_call | solution.py:675
  273.8 23.2 %backward.12 = (bf16[256,384]{1,0:T(8,128)(2,1)}, bf16[256,576]{1,0:T(8,128)(2,1)}, f32[8,576]{1,0:T(8,128)}, f32[256,576]{1,0:T(8,128)}, bf16[256,576]{1,0:T(8,...) custom-call(s32[3]{0:T(128)} %pad_add_fusion.1.scal.refs_0_, ...), custom_call_target="tpu_custom_call" | custom-call | flops 113246208 | bytes 1000 | tf_op jit(solution)/shard_map/backward/pallas_call | solution.py:675
  306.8 15.1 %backward.13 = (bf16[256,384]{1,0:T(8,128)(2,1)}, bf16[256,576]{1,0:T(8,128)(2,1)}, f32[8,576]{1,0:T(8,128)}, f32[256,576]{1,0:T(8,128)}, bf16[256,576]{1,0:T(8,...) custom-call(s32[3]{0:T(128)} %pad_add_fusion.1.scal.refs_0_, ...), custom_call_target="tpu_custom_call" | custom-call | flops 113246208 | bytes 1000 | tf_op jit(solution)/shard_map/backward/pallas_call | solution.py:675
  330.8 8.9 %gate_up_grads.2 = (bf16[16,40,1536]{2,1,0:T(8,128)(2,1)}, bf16[16,40,1536]{2,1,0:T(8,128)(2,1)}) custom-call(s32[3]{0:T(128)} %pad_add_fusion.1.scal.refs_0_, bf16[256,576]{1,0:T(8,128)(2,1)} %get-tuple-element.540.refs_1_, bf16[256,576]{1,0:T(8,128)(2,1)} %get-tuple-element.541.refs_2_, bf16[256,576]{1,0:T(8,128)(2,1)} %get-tuple-element.542.refs_3_, ...), custom_call_target="tpu_custom_call" | custom-call | flops 56623104 | bytes 1000 | tf_op jit(solution)/shard_map/gate_up_grads/pallas_call | solution.py:874
  360.3 23.8 %backward.14 = (bf16[256,384]{1,0:T(8,128)(2,1)}, bf16[256,576]{1,0:T(8,128)(2,1)}, f32[8,576]{1,0:T(8,128)}, bf16[576,256]{1,0:T(8,128)(2,1)}, f32[256,576]{1,0...) custom-call(s32[3]{0:T(128)} %pad_add_fusion.1.scal.refs_0_, ...), custom_call_target="tpu_custom_call" | custom-call | flops 113246208 | bytes 1000 | tf_op jit(solution)/shard_map/backward/pallas_call | solution.py:675
  401.8 15.2 %backward.15 = (bf16[256,384]{1,0:T(8,128)(2,1)}, bf16[256,576]{1,0:T(8,128)(2,1)}, f32[8,576]{1,0:T(8,128)}, bf16[576,256]{1,0:T(8,128)(2,1)}, f32[256,576]{1,0...) custom-call(s32[3]{0:T(128)} %pad_add_fusion.1.scal.refs_0_, ...), custom_call_target="tpu_custom_call" | custom-call | flops 113246208 | bytes 1000 | tf_op jit(solution)/shard_map/backward/pallas_call | solution.py:675
  432.4 23.5 %backward.16 = (bf16[256,384]{1,0:T(8,128)(2,1)}, bf16[256,576]{1,0:T(8,128)(2,1)}, f32[8,576]{1,0:T(8,128)}, f32[256,576]{1,0:T(8,128)}, bf16[256,576]{1,0:T(8,...) custom-call(s32[3]{0:T(128)} %pad_add_fusion.1.scal.refs_0_, ...), custom_call_target="tpu_custom_call" | custom-call | flops 113246208 | bytes 1000 | tf_op jit(solution)/shard_map/backward/pallas_call | solution.py:675
  463.0 21.1 %backward.17 = (bf16[256,384]{1,0:T(8,128)(2,1)}, bf16[256,576]{1,0:T(8,128)(2,1)}, f32[8,576]{1,0:T(8,128)}, f32[256,576]{1,0:T(8,128)}, bf16[256,576]{1,0:T(8,...) custom-call(s32[3]{0:T(128)} %pad_add_fusion.1.scal.refs_0_, ...), custom_call_target="tpu_custom_call" | custom-call | flops 113246208 | bytes 1000 | tf_op jit(solution)/shard_map/backward/pallas_call | solution.py:675
  484.2 9.2 %gate_up_grads.3 = (bf16[16,40,1536]{2,1,0:T(8,128)(2,1)}, bf16[16,40,1536]{2,1,0:T(8,128)(2,1)}) custom-call(s32[3]{0:T(128)} %pad_add_fusion.1.scal.refs_0_, bf16[256,576]{1,0:T(8,128)(2,1)} %get-tuple-element.648.refs_1_, bf16[256,576]{1,0:T(8,128)(2,1)} %get-tuple-element.649.refs_2_, bf16[256,576]{1,0:T(8,128)(2,1)} %get-tuple-element.650.refs_3_, ...), custom_call_target="tpu_custom_call" | custom-call | flops 56623104 | bytes 1000 | tf_op jit(solution)/shard_map/gate_up_grads/pallas_call | solution.py:874
  512.5 6.6 down_grads.3
  546.3 10.1 %collective-permute-done.114.refs_2_ = bf16[8,672,128]{2,1,0:T(8,128)(2,1)S(1)} collective-permute-done((bf16[8,672,128]{2,1,0:T(8,128)(2,1)}, bf16[8,672,128]{2,1,0:T(8,128)(2,1)S(1)}, u32[]{:S(2)}, u32[]{:S(2)}) %collective-permute-start.114) | collective-permute-done | bytes 1376288 | tf_op jit(solution)/shard_map/ppermute | solution.py:1052
  567.4 11.9 %collective-permute-start.119 = (bf16[4,672,128]{2,1,0:T(8,128)(2,1)S(1)}, bf16[4,672,128]{2,1,0:T(8,128)(2,1)S(1)}, u32[]{:S(2)}, u32[]{:S(2)}) collective-permute-start(bf16[4,672,128]{2,1,0:T(8,128)(2,1)S(1)} %copy-done.22), channel_id=1, source_target_pairs={{0,2},{1,3},{2,0},{3,1},{4,6},{5,7},{6,4},{7,5},{8,10},{9,11},{10,... | collective-permute-start | bytes 2064392 | tf_op jit(solution)/shard_map/ppermute | solution.py:1052
  585.8 15.5 %collective-permute-done.120.refs_2_ = bf16[8,192,128]{2,1,0:T(8,128)(2,1)S(1)} collective-permute-done((bf16[8,192,128]{2,1,0:T(8,128)(2,1)S(1)}, bf16[8,192,128]{2,1,0:T(8,128)(2,1)S(1)}, u32[]{:S(2)}, u32[]{:S(2)}) %collective-permute-start.120) | collective-permute-done | bytes 393248 | tf_op jit(solution)/shard_map/ppermute | solution.py:1052
  649.8 6.5 collective-permute-done.131.refs_2_
  (711 shorter events, 329.6 us)
Async XLA Ops:
  7.2 558.8 %reduce-scatter.5.cloned.1.call-start = ((), (), s32[]{:S(2)}) async-start(), calls=%async_computation.2 | async-start | bytes 4300800 | tf_op jit(solution)/shard_map/reduce_scatter | solution.py:1009
  7.2 33.9 %collective-permute-start.7 = (bf16[576,1536]{1,0:T(8,128)(2,1)}, bf16[576,1536]{1,0:T(8,128)(2,1)S(1)}, u32[]{:S(2)}, u32[]{:S(2)}) collective-permute-start(bf16[576,1536]{1,0:T(8,128)(2,1)} %bitcast.79), channel_id=1, source_target_pairs={{0,16},{16,0},{1,17},{17,1},{2,18},{18,2},{3,19},{19,3},{4,20},{20... | collective-permute-start | bytes 5308424 | tf_op jit(solution)/shard_map/ppermute | solution.py:1347
  7.7 33.4 %collective-permute-start.8 = (bf16[576,1536]{1,0:T(8,128)(2,1)}, bf16[576,1536]{1,0:T(8,128)(2,1)S(1)}, u32[]{:S(2)}, u32[]{:S(2)}) collective-permute-start(bf16[576,1536]{1,0:T(8,128)(2,1)} %bitcast.96), channel_id=1, source_target_pairs={{0,16},{16,0},{1,17},{17,1},{2,18},{18,2},{3,19},{19,3},{4,20},{20... | collective-permute-start | bytes 5308424 | tf_op jit(solution)/shard_map/ppermute | solution.py:1347
  7.8 33.4 %collective-permute-start.9 = (bf16[576,1536]{1,0:T(8,128)(2,1)}, bf16[576,1536]{1,0:T(8,128)(2,1)}, u32[]{:S(2)}, u32[]{:S(2)}) collective-permute-start(bf16[576,1536]{1,0:T(8,128)(2,1)} %bitcast.113), channel_id=1, source_target_pairs={{0,16},{16,0},{1,17},{17,1},{2,18},{18,2},{3,19},{19,3},{4,20},{20... | collective-permute-start | bytes 5308424 | tf_op jit(solution)/shard_map/ppermute | solution.py:1347
  233.9 31.1 %collective-permute-start.72 = (bf16[256,384]{1,0:T(8,128)(2,1)}, bf16[256,384]{1,0:T(8,128)(2,1)S(1)}, u32[]{:S(2)}, u32[]{:S(2)}) collective-permute-start(bf16[256,384]{1,0:T(8,128)(2,1)} %get-tuple-element.794), channel_id=1, source_target_pairs={{0,1},{1,0},{2,3},{3,2},{4,5},{5,4},{6,7},{7,6},{8,9},{9,8},{10,11... | collective-permute-start | bytes 589832 | tf_op jit(solution)/shard_map/ppermute | solution.py:1198
  234.5 30.5 %collective-permute-start.73 = (bf16[256,384]{1,0:T(8,128)(2,1)}, bf16[256,384]{1,0:T(8,128)(2,1)S(1)}, u32[]{:S(2)}, u32[]{:S(2)}) collective-permute-start(bf16[256,384]{1,0:T(8,128)(2,1)} %get-tuple-element.793), channel_id=1, source_target_pairs={{0,4},{4,0},{8,12},{12,8},{1,5},{5,1},{9,13},{13,9},{2,6},{6,2},{1... | collective-permute-start | bytes 589832 | tf_op jit(solution)/shard_map/ppermute | solution.py:1201
  234.8 30.2 %collective-permute-start.74 = (bf16[256,384]{1,0:T(8,128)(2,1)S(1)}, bf16[256,384]{1,0:T(8,128)(2,1)S(1)}, u32[]{:S(2)}, u32[]{:S(2)}) collective-permute-start(bf16[256,384]{1,0:T(8,128)(2,1)S(1)} %get-tuple-element.792), channel_id=1, source_target_pairs={{0,5},{1,4},{2,7},{3,6},{4,1},{5,0},{6,3},{7,2},{8,13},{9,12},{10,... | collective-permute-start | bytes 589832 | tf_op jit(solution)/shard_map/ppermute | solution.py:1205
  266.8 30.3 %collective-permute-start.79 = (bf16[2,576,256]{2,1,0:T(8,128)(2,1)}, bf16[2,576,256]{2,1,0:T(8,128)(2,1)S(1)}, u32[]{:S(2)}, u32[]{:S(2)}) collective-permute-start(bf16[2,576,256]{2,1,0:T(8,128)(2,1)} %broadcast_select_fusion.7), channel_id=1, source_target_pairs={{0,16},{16,0},{1,17},{17,1},{2,18},{18,2},{3,19},{19,3},{4,20},{20... | collective-permute-start | bytes 1769480 | tf_op jit(solution)/shard_map/ppermute | solution.py:1280
  268.9 28.2 %collective-permute-start.76 = (bf16[256,384]{1,0:T(8,128)(2,1)}, bf16[256,384]{1,0:T(8,128)(2,1)S(1)}, u32[]{:S(2)}, u32[]{:S(2)}) collective-permute-start(bf16[256,384]{1,0:T(8,128)(2,1)} %get-tuple-element.790), channel_id=1, source_target_pairs={{0,1},{1,0},{2,3},{3,2},{4,5},{5,4},{6,7},{7,6},{8,9},{9,8},{10,11... | collective-permute-start | bytes 589832 | tf_op jit(solution)/shard_map/ppermute | solution.py:1198
  339.6 44.6 %collective-permute-start.89 = (bf16[16,40,1536]{2,1,0:T(8,128)(2,1)}, bf16[16,40,1536]{2,1,0:T(8,128)(2,1)S(1)}, u32[]{:S(2)}, u32[]{:S(2)}) collective-permute-start(bf16[16,40,1536]{2,1,0:T(8,128)(2,1)} %get-tuple-element.557), channel_id=1, source_target_pairs={{0,16},{16,0},{1,17},{17,1},{2,18},{18,2},{3,19},{19,3},{4,20},{20... | collective-permute-start | bytes 5898248 | tf_op jit(solution)/shard_map/ppermute | solution.py:993
  346.3 37.9 %collective-permute-start.90 = (bf16[16,48,576]{2,1,0:T(8,128)(2,1)}, bf16[16,48,576]{2,1,0:T(8,128)(2,1)}, u32[]{:S(2)}, u32[]{:S(2)}) collective-permute-start(bf16[16,48,576]{2,1,0:T(8,128)(2,1)} %get-tuple-element.558), channel_id=1, source_target_pairs={{0,16},{16,0},{1,17},{17,1},{2,18},{18,2},{3,19},{19,3},{4,20},{20... | collective-permute-start | bytes 2654216 | tf_op jit(solution)/shard_map/ppermute | solution.py:993
  350.8 33.4 %collective-permute-start.91 = (bf16[16,40,384]{2,1,0:T(8,128)(2,1)}, bf16[16,40,384]{2,1,0:T(8,128)(2,1)S(1)}, u32[]{:S(2)}, u32[]{:S(2)}) collective-permute-start(bf16[16,40,384]{2,1,0:T(8,128)(2,1)} %get-tuple-element.559), channel_id=1, source_target_pairs={{0,16},{16,0},{1,17},{17,1},{2,18},{18,2},{3,19},{19,3},{4,20},{20... | collective-permute-start | bytes 1474568 | tf_op jit(solution)/shard_map/ppermute | solution.py:993
  350.9 33.2 %collective-permute-start.87 = (bf16[256,384]{1,0:T(8,128)(2,1)}, bf16[256,384]{1,0:T(8,128)(2,1)}, u32[]{:S(2)}, u32[]{:S(2)}) collective-permute-start(bf16[256,384]{1,0:T(8,128)(2,1)} %get-tuple-element.781), channel_id=1, source_target_pairs={{0,4},{4,0},{8,12},{12,8},{1,5},{5,1},{9,13},{13,9},{2,6},{6,2},{1... | collective-permute-start | bytes 589832 | tf_op jit(solution)/shard_map/ppermute | solution.py:1201
  388.2 28.8 %collective-permute-start.96 = (bf16[2,576,256]{2,1,0:T(8,128)(2,1)}, bf16[2,576,256]{2,1,0:T(8,128)(2,1)S(1)}, u32[]{:S(2)}, u32[]{:S(2)}) collective-permute-start(bf16[2,576,256]{2,1,0:T(8,128)(2,1)} %broadcast_select_fusion.12), channel_id=1, source_target_pairs={{0,1},{1,0},{2,3},{3,2},{4,5},{5,4},{6,7},{7,6},{8,9},{9,8},{10,11... | collective-permute-start | bytes 1769480 | tf_op jit(solution)/shard_map/ppermute | solution.py:1267
  395.1 231.8 %reduce-scatter.7.cloned.1.call-start = ((), (), s32[]{:S(2)}) async-start(), calls=%async_computation.3 | async-start | bytes 1075200
  418.9 36.9 %collective-permute-start.101 = (bf16[2,576,256]{2,1,0:T(8,128)(2,1)S(1)}, bf16[2,576,256]{2,1,0:T(8,128)(2,1)S(1)}, u32[]{:S(2)}, u32[]{:S(2)}) collective-permute-start(bf16[2,576,256]{2,1,0:T(8,128)(2,1)S(1)} %pad_maximum_fusion.4), channel_id=1, source_target_pairs={{0,16},{1,17},{2,18},{3,19},{4,20},{5,21},{6,22},{7,23},{8,24},{9,... | collective-permute-start | bytes 1769480 | tf_op jit(solution)/shard_map/ppermute | solution.py:1280
  422.9 33.0 %collective-permute-start.98 = (bf16[256,384]{1,0:T(8,128)(2,1)S(1)}, bf16[256,384]{1,0:T(8,128)(2,1)S(1)}, u32[]{:S(2)}, u32[]{:S(2)}) collective-permute-start(bf16[256,384]{1,0:T(8,128)(2,1)S(1)} %get-tuple-element.774), channel_id=1, source_target_pairs={{0,1},{1,0},{2,3},{3,2},{4,5},{5,4},{6,7},{7,6},{8,9},{9,8},{10,11... | collective-permute-start | bytes 589832 | tf_op jit(solution)/shard_map/ppermute | solution.py:1198
  425.0 30.9 %collective-permute-start.99 = (bf16[256,384]{1,0:T(8,128)(2,1)S(1)}, bf16[256,384]{1,0:T(8,128)(2,1)S(1)}, u32[]{:S(2)}, u32[]{:S(2)}) collective-permute-start(bf16[256,384]{1,0:T(8,128)(2,1)S(1)} %get-tuple-element.773), channel_id=1, source_target_pairs={{0,4},{4,0},{8,12},{12,8},{1,5},{5,1},{9,13},{13,9},{2,6},{6,2},{1... | collective-permute-start | bytes 589832 | tf_op jit(solution)/shard_map/ppermute | solution.py:1201
  425.0 31.0 %collective-permute-start.100 = (bf16[256,384]{1,0:T(8,128)(2,1)S(1)}, bf16[256,384]{1,0:T(8,128)(2,1)S(1)}, u32[]{:S(2)}, u32[]{:S(2)}) collective-permute-start(bf16[256,384]{1,0:T(8,128)(2,1)S(1)} %get-tuple-element.772), channel_id=1, source_target_pairs={{0,5},{1,4},{2,7},{3,6},{4,1},{5,0},{6,3},{7,2},{8,13},{9,12},{10,... | collective-permute-start | bytes 589832 | tf_op jit(solution)/shard_map/ppermute | solution.py:1205
  457.7 26.5 %collective-permute-start.103 = (bf16[2,576,256]{2,1,0:T(8,128)(2,1)S(1)}, bf16[2,576,256]{2,1,0:T(8,128)(2,1)S(1)}, u32[]{:S(2)}, u32[]{:S(2)}) collective-permute-start(bf16[2,576,256]{2,1,0:T(8,128)(2,1)S(1)} %broadcast_select_fusion.21), channel_id=1, source_target_pairs={{16,28},{20,24},{24,20},{28,16},{17,29},{21,25},{25,21},{29,17},{1... | collective-permute-start | bytes 1769480 | tf_op jit(solution)/shard_map/ppermute | solution.py:1267
  524.8 31.6 %collective-permute-start.114 = (bf16[8,672,128]{2,1,0:T(8,128)(2,1)}, bf16[8,672,128]{2,1,0:T(8,128)(2,1)S(1)}, u32[]{:S(2)}, u32[]{:S(2)}) collective-permute-start(bf16[8,672,128]{2,1,0:T(8,128)(2,1)} %get-tuple-element.699), channel_id=1, source_target_pairs={{0,1},{1,0},{2,3},{3,2},{4,5},{5,4},{6,7},{7,6},{8,9},{9,8},{10,11... | collective-permute-start | bytes 4128776 | tf_op jit(solution)/shard_map/ppermute | solution.py:1052
  563.7 41.7 %collective-permute-start.121 = (bf16[8,360,128]{2,1,0:T(8,128)(2,1)}, bf16[8,360,128]{2,1,0:T(8,128)(2,1)S(1)}, u32[]{:S(2)}, u32[]{:S(2)}) collective-permute-start(bf16[8,360,128]{2,1,0:T(8,128)(2,1)} %get-tuple-element.714), channel_id=1, source_target_pairs={{0,1},{1,0},{2,3},{3,2},{4,5},{5,4},{6,7},{7,6},{8,9},{9,8},{10,11... | collective-permute-start | bytes 2211848 | tf_op jit(solution)/shard_map/ppermute | solution.py:1052
  567.4 38.1 %collective-permute-start.119 = (bf16[4,672,128]{2,1,0:T(8,128)(2,1)S(1)}, bf16[4,672,128]{2,1,0:T(8,128)(2,1)S(1)}, u32[]{:S(2)}, u32[]{:S(2)}) collective-permute-start(bf16[4,672,128]{2,1,0:T(8,128)(2,1)S(1)} %copy-done.22), channel_id=1, source_target_pairs={{0,2},{1,3},{2,0},{3,1},{4,6},{5,7},{6,4},{7,5},{8,10},{9,11},{10,... | collective-permute-start | bytes 2064392 | tf_op jit(solution)/shard_map/ppermute | solution.py:1052
  585.1 35.9 %collective-permute-start.126 = (bf16[2,576,256]{2,1,0:T(8,128)(2,1)S(1)}, bf16[2,576,256]{2,1,0:T(8,128)(2,1)S(1)}, u32[]{:S(2)}, u32[]{:S(2)}) collective-permute-start(bf16[2,576,256]{2,1,0:T(8,128)(2,1)S(1)} %broadcast_select_fusion.8), channel_id=1, source_target_pairs={{16,17},{17,16},{18,19},{19,18},{20,21},{21,20},{22,23},{23,22},{2... | collective-permute-start | bytes 1769480 | tf_op jit(solution)/shard_map/ppermute | solution.py:1267
  (284 other events, 2453.7 us)
Sparse Core Ops, SparseCore 0:
  395.2 73.2 reduce-scatter.4
  566.1 42.3 reduce-scatter.6
